TPU v7x, 32 devices: a whole 2x2x4 slice. The times are simulated.
32 devices in a mesh: dp: 8 (over y, x, core), tensor: 4 (over z).
Axes of the slice: x: 2, y: 2, z: 4, core: 2. Of those that a mesh axis runs over, the one named last changes fastest.
Arguments:
- tokens: bfloat16 [16384, 768], P('dp'), may hold values from -6 to 6
- timesteps: int32 [256], P('dp'), may hold values from 0 to 1999, as said below
- time_table: bfloat16 [2000, 768], P(None, 'tensor'), may hold values from -3 to 3
- w_qkv: bfloat16 [768, 3, 768], P(None, None, 'tensor'), may hold values from -0.21875 to 0.21875
- b_qv: float32 [2, 768], P(None, 'tensor'), may hold values from -2 to 2
- w_out: bfloat16 [768, 768], P('tensor'), may hold values from -0.625 to 0.625
- b_out: float32 [768], replicated, may hold values from -2 to 2
- w_in: bfloat16 [768, 3072], P(None, 'tensor'), may hold values from -0.21875 to 0.21875
- b_in: float32 [3072], P('tensor'), may hold values from -3 to 3
- w_back: bfloat16 [3072, 768], P('tensor'), may hold values from -0.109375 to 0.109375
- b_back: float32 [768], replicated, may hold values from -2 to 2
- gain_one: float32 [768], replicated, may hold values from 0.25 to 1.75
- shift_one: float32 [768], replicated, may hold values from -2 to 2
- gain_two: float32 [768], replicated, may hold values from 0.25 to 1.75
- shift_two: float32 [768], replicated, may hold values from -2 to 2
- cotangent: bfloat16 [16384, 768], P('dp'), may hold values from -6 to 6
Outputs:
- output: bfloat16 [16384, 768], P('dp')
- grad_tokens: bfloat16 [16384, 768], P('dp')
- grad_table: float32 [2000, 768], P(None, 'tensor')
- grad_wqkv: float32 [768, 3, 768], P('dp', None, 'tensor')
- grad_bqv: float32 [2, 768], P(None, 'tensor')
- grad_wout: float32 [768, 768], P('tensor', 'dp')
- grad_bout: float32 [768], replicated
- grad_win: float32 [768, 3072], P('dp', 'tensor')
- grad_bin: float32 [3072], P('tensor')
- grad_wback: float32 [3072, 768], P('tensor', 'dp')
- grad_bback: float32 [768], replicated
- grad_gain_one: float32 [768], replicated
- grad_shift_one: float32 [768], replicated
- grad_gain_two: float32 [768], replicated
- grad_shift_two: float32 [768], replicated
Inputs may be any that keep to these rules, and one draw needn't show every extreme that they name: `timesteps`: diffusion step of each sentence, a row of time_table.
All inputs are finite; a program needn't handle non-finite values.
Results may differ from a plain program's by a relative error of at most 0.017.
Values may be sent and summed in bfloat16 or wider, within the bound.
No kernel may reach another device: no remote copies, remote signals or barrier semaphores. Data moves between devices by JAX's collectives and lax.ppermute only.
A program may use at most 192 MiB of HBM per device.

v0:
```python
import jax
import jax.numpy as jnp
from jax import lax
from jax.sharding import PartitionSpec as P

HEAD = 64
LEN = 64


EPS = 1e-05
HIGHEST_PREC = lax.Precision.HIGHEST


def norm_rows(rows, gain, shift):
    mean = jnp.mean(rows, axis=-1, keepdims=True)
    centred = rows - mean
    spread = jnp.mean(centred * centred, axis=-1, keepdims=True)
    return centred * lax.rsqrt(spread + EPS) * gain + shift


def gelu_exact(pre_act):
    return jax.nn.gelu(pre_act, approximate=False)


def dot_rows(left, right):
    return lax.dot_general(
        left, right, (((0,), (0,)), ((), ())), preferred_element_type=jnp.float32
    )


def dot_cols(left, right):
    return lax.dot_general(
        left, right, (((1,), (1,)), ((), ())), preferred_element_type=jnp.float32
    )


def body(
    tokens,
    timesteps,
    time_table,
    w_qkv,
    b_qv,
    w_out,
    b_out,
    w_in,
    b_in,
    w_back,
    b_back,
    gain_one,
    shift_one,
    gain_two,
    shift_two,
    cotangent,
):
    sentences = timesteps.shape[0]
    row_count = tokens.shape[0]
    model_width = tokens.shape[1]
    head_cols = w_out.shape[0]
    table_cols = time_table.shape[1]
    score_scale = HEAD ** (-0.5)
    steps_iota = lax.broadcasted_iota(jnp.int32, (sentences, time_table.shape[0]), 1)
    picked = timesteps[:, None] == steps_iota
    own_rows = jnp.dot(
        picked.astype(jnp.bfloat16), time_table, preferred_element_type=jnp.float32
    ).astype(jnp.bfloat16)
    time_rows = lax.all_gather(own_rows, "tensor", axis=1, tiled=True)
    entry_rows = (
        tokens.astype(jnp.float32).reshape(sentences, LEN, model_width)
        + time_rows.astype(jnp.float32)[:, None, :]
    )
    entry_rows = entry_rows.reshape(row_count, model_width)
    normed_one, pull_one = jax.vjp(norm_rows, entry_rows, gain_one, shift_one)
    n_one = normed_one.astype(jnp.bfloat16)
    flat_qkv = w_qkv.reshape(model_width, 3 * head_cols)
    bias_row = jnp.concatenate([b_qv[0], jnp.zeros((head_cols,), jnp.float32), b_qv[1]])
    projected = (jnp.dot(n_one, flat_qkv, preferred_element_type=jnp.float32) + bias_row).astype(
        jnp.bfloat16
    )
    queries = projected[:, :head_cols].reshape(sentences, LEN, -1, HEAD)
    key_heads = projected[:, head_cols : 2 * head_cols].reshape(sentences, LEN, -1, HEAD)
    values = projected[:, 2 * head_cols :].reshape(sentences, LEN, -1, HEAD)
    scores = (
        jnp.einsum("nqhe,nkhe->nhqk", queries, key_heads, preferred_element_type=jnp.float32)
        * score_scale
    )
    score_max = jnp.max(scores, axis=-1, keepdims=True)
    weights_exp = jnp.exp(scores - score_max)
    weight_total = jnp.sum(weights_exp, axis=-1, keepdims=True)
    log_total = score_max + jnp.log(weight_total)
    prob_low = (weights_exp / weight_total).astype(jnp.bfloat16)
    mixed_heads = jnp.einsum(
        "nhqk,nkhe->nqhe", prob_low, values, preferred_element_type=jnp.float32
    )
    mixed_heads = mixed_heads.reshape(row_count, head_cols).astype(jnp.bfloat16)
    attn_term = jnp.dot(mixed_heads, w_out, preferred_element_type=jnp.float32)
    attended = lax.psum(attn_term.astype(jnp.bfloat16), "tensor").astype(jnp.float32)
    middle = entry_rows + attended + b_out
    normed_two, pull_two = jax.vjp(norm_rows, middle, gain_two, shift_two)
    n_two = normed_two.astype(jnp.bfloat16)
    pre_act = jnp.dot(n_two, w_in, preferred_element_type=jnp.float32) + b_in
    activated, pull_gelu = jax.vjp(gelu_exact, pre_act)
    act_low = activated.astype(jnp.bfloat16)
    mlp_term = jnp.dot(act_low, w_back, preferred_element_type=jnp.float32)
    summed = lax.psum(mlp_term.astype(jnp.bfloat16), "tensor").astype(jnp.float32)
    output = (middle + summed + b_back).astype(jnp.bfloat16)
    upstream = cotangent.astype(jnp.float32)
    grad_bback = jnp.sum(upstream, axis=0)
    grad_wback = dot_rows(act_low, cotangent)
    grad_act = dot_cols(cotangent, w_back)
    grad_pre = pull_gelu(grad_act)[0].astype(jnp.bfloat16)
    grad_bin = jnp.sum(grad_pre.astype(jnp.float32), axis=0)
    grad_win = dot_rows(n_two, grad_pre)
    back_two = dot_cols(grad_pre, w_in)
    norm_two_grad = lax.psum(back_two.astype(jnp.bfloat16), "tensor").astype(jnp.float32)
    middle_part, grad_gain_two, grad_shift_two = pull_two(norm_two_grad)
    grad_middle = upstream + middle_part
    grad_bout = jnp.sum(grad_middle, axis=0)
    middle_low = grad_middle.astype(jnp.bfloat16)
    grad_wout = dot_rows(mixed_heads, middle_low)
    grad_mixed = dot_cols(middle_low, w_out).astype(jnp.bfloat16).reshape(sentences, LEN, -1, HEAD)
    rescored = (
        jnp.einsum("nqhe,nkhe->nhqk", queries, key_heads, preferred_element_type=jnp.float32)
        * score_scale
    )
    prob_full = jnp.exp(rescored - log_total)
    prob_again = prob_full.astype(jnp.bfloat16)
    grad_values = jnp.einsum(
        "nhqk,nqhe->nkhe", prob_again, grad_mixed, preferred_element_type=jnp.float32
    )
    grad_probs = jnp.einsum(
        "nqhe,nkhe->nhqk", grad_mixed, values, preferred_element_type=jnp.float32
    )
    row_dot = jnp.sum(prob_full * grad_probs, axis=-1, keepdims=True)
    grad_scores = (prob_full * (grad_probs - row_dot)).astype(jnp.bfloat16)
    grad_queries = (
        jnp.einsum("nhqk,nkhe->nqhe", grad_scores, key_heads, preferred_element_type=jnp.float32)
        * score_scale
    )
    grad_keys = (
        jnp.einsum("nhqk,nqhe->nkhe", grad_scores, queries, preferred_element_type=jnp.float32)
        * score_scale
    )
    grad_proj = jnp.concatenate(
        [
            grad_queries.reshape(row_count, head_cols),
            grad_keys.reshape(row_count, head_cols),
            grad_values.reshape(row_count, head_cols),
        ],
        axis=1,
    ).astype(jnp.bfloat16)
    grad_bqv = jnp.stack(
        [
            jnp.sum(grad_proj[:, :head_cols].astype(jnp.float32), axis=0),
            jnp.sum(grad_proj[:, 2 * head_cols :].astype(jnp.float32), axis=0),
        ]
    )
    grad_wqkv = dot_rows(n_one, grad_proj).reshape(model_width, 3, head_cols)
    back_one = dot_cols(grad_proj, flat_qkv)
    norm_one_grad = lax.psum(back_one.astype(jnp.bfloat16), "tensor").astype(jnp.float32)
    entry_part, grad_gain_one, grad_shift_one = pull_one(norm_one_grad)
    grad_entry = grad_middle + entry_part
    grad_tokens = grad_entry.astype(jnp.bfloat16)
    per_sentence = jnp.sum(grad_entry.reshape(sentences, LEN, model_width), axis=1)
    own_cols = lax.dynamic_slice_in_dim(
        per_sentence, lax.axis_index("tensor") * table_cols, table_cols, 1
    )
    grad_table = lax.dot_general(
        picked.astype(jnp.float32),
        own_cols,
        (((0,), (0,)), ((), ())),
        precision=HIGHEST_PREC,
        preferred_element_type=jnp.float32,
    )
    sums_small = lax.psum(
        (
            grad_bqv,
            grad_bout,
            grad_bin,
            grad_bback,
            grad_gain_one,
            grad_shift_one,
            grad_gain_two,
            grad_shift_two,
            grad_table,
        ),
        "dp",
    )
    sent_wqkv, sent_wout, sent_win, sent_wback = (
        lax.psum_scatter(grad_wqkv, "dp", scatter_dimension=0, tiled=True),
        lax.psum_scatter(grad_wout, "dp", scatter_dimension=1, tiled=True),
        lax.psum_scatter(grad_win, "dp", scatter_dimension=0, tiled=True),
        lax.psum_scatter(grad_wback, "dp", scatter_dimension=1, tiled=True),
    )
    return (
        output,
        grad_tokens,
        sums_small[8],
        sent_wqkv,
        sums_small[0],
        sent_wout,
        sums_small[1],
        sent_win,
        sums_small[2],
        sent_wback,
        sums_small[3],
        sums_small[4],
        sums_small[5],
        sums_small[6],
        sums_small[7],
    )


def solution(mesh):
    return jax.shard_map(
        body,
        mesh=mesh,
        in_specs=(
            P("dp", None),
            P("dp"),
            P(None, "tensor"),
            P(None, None, "tensor"),
            P(None, "tensor"),
            P("tensor", None),
            P(),
            P(None, "tensor"),
            P("tensor"),
            P("tensor", None),
            P(),
            P(),
            P(),
            P(),
            P(),
            P("dp", None),
        ),
        out_specs=(
            P("dp", None),
            P("dp", None),
            P(None, "tensor"),
            P("dp", None, "tensor"),
            P(None, "tensor"),
            P("tensor", "dp"),
            P(),
            P("dp", "tensor"),
            P("tensor"),
            P("tensor", "dp"),
            P(),
            P(),
            P(),
            P(),
            P(),
        ),
        check_vma=False,
    )
```

profile of v0, /device:TPU:0, one launch (start us, length us, event | category | flops | bytes accessed | tf_op | source)
XLA Modules:
  0.0 864.8 jit_solution(9921110277392228974)
XLA Ops:
  8.0 1.5 fusion.45
  9.6 14.9 %all-gather = bf16[4,192,32]{1,2,0:T(8,128)(2,1)S(1)} all-gather(bf16[1,192,32]{1,2,0:T(8,128)(2,1)S(1)} %fusion.45), channel_id=1, replica_groups=mesh['dp'=8,'tensor'=4] {'tensor'}, dimensions={0}, use_global_device_ids=true | all-gather | bytes 61440 | tf_op jit(solution)/shard_map/all_gather | solution.py:66
  24.7 2.7 fusion.15
  27.4 3.1 multiply_reduce_fusion.1
  30.6 1.6 add_convert_fusion.3
  32.3 2.0 add_convert_fusion.4
  34.3 1.4 fusion.59
  35.8 2.7 reshape.151
  38.5 3.7 reshape.150
  42.2 3.4 reshape.149
  45.6 3.4 copy.73
  49.0 3.3 multiply_reduce_fusion.3
  54.3 2.2 copy.71
  56.4 3.2 convert_element_type.101
  59.7 2.7 convolution_convert_fusion.3
  62.5 122.3 %all-reduce.7.cloned.1.call-done = bf16[2048,768]{1,0:T(8,128)(2,1)} async-done(((bf16[2048,768]{1,0:T(8,128)(2,1)}), bf16[2048,768]{1,0:T(8,128)(2,1)}) %all-reduce.7.cloned.1.call-update) | async-done | bytes 3145744 | tf_op jit(solution)/shard_map/psum | solution.py:96
  184.8 4.3 fusion.55
  189.5 2.0 multiply_reduce_fusion
  191.5 2.0 add_convert_fusion.2
  193.6 2.8 fusion.61
  196.6 18.5 %convert_reduce_fusion.3 = (f32[768]{0:T(1024)S(1)}, bf16[2048,768]{1,0:T(8,128)(2,1)S(1)}, f32[2048,768]{1,0:T(8,128)}) fusion(f32[2048,768]{1,0:T(8,128)S(1)} %fusion.61, f32[768]{0:T(1024)S(1)} %copy-done.35, bf16[2048,768]{1,0:T(8,128)(2,1)S(1)} %copy-done.12, bf16[768,768]{1,0:T(8,128)(2,1)S(1)} %copy-done), kind=kOutput, calls=%fused_computation.22 | convolution fusion | flops 2533883136 | bytes 20060160 | tf_op jit(solution)/shard_map/dot_general | solution.py:32
  215.1 1.7 copy-done.40
  216.8 4.0 convolution_convert_fusion
  220.9 5.6 multiply_convert_fusion
  226.6 1.7 copy-done.26
  228.3 4.0 convolution_convert_fusion.1
  232.2 108.9 %all-reduce.9.cloned.1.call-done = bf16[2048,768]{1,0:T(8,128)(2,1)} async-done(((bf16[2048,768]{1,0:T(8,128)(2,1)}), bf16[2048,768]{1,0:T(8,128)(2,1)}) %all-reduce.9.cloned.1.call-update) | async-done | bytes 3145744 | tf_op jit(solution)/shard_map/psum | solution.py:114
  341.1 7.2 fusion.7
  348.4 3.7 fusion.58
  352.1 2.6 copy-done.8
  354.7 1.3 convolution_convert_fusion.4
  356.0 1.8 reshape.152
  357.8 3.3 fusion.28
  361.2 1.9 multiply_reduce_fusion.2
  363.1 1.1 multiply_convert_fusion.3
  364.5 2.2 fusion.32
  366.7 2.4 fusion.31
  369.1 2.2 copy.84
  371.3 2.8 reshape.155
  374.1 3.2 copy.77
  377.3 2.8 reshape.153
  380.1 3.2 copy.81
  383.2 2.8 reshape.154
  386.2 1.4 copy-done.29
  387.6 5.4 convolution_convert_fusion.2
  393.1 1.1 copy-done.20
  394.2 6.7 fusion.42
  401.0 7.0 fusion.62
  408.1 6.9 fusion.63
  415.1 6.7 fusion.18
  422.0 193.5 %all-reduce.13.cloned.1.call-done = (bf16[2048,768]{1,0:T(8,128)(2,1)}, bf16[2048,768]{1,0:T(8,128)(2,1)}) async-done(((bf16[2048,768]{1,0:T(8,128)(2,1)}, bf16[2048,768]{1,0:T(8,128)(2,1)}), (bf16[2048,768]{1,0:T(8,128)(2,1)}, bf16[2048,768]{1,0:T(8,128)(2,1)})) %all-reduce.13.cloned.1.call-update) | async-done | bytes 6291472 | tf_op jit(solution)/shard_map/psum | solution.py:104
  615.5 4.6 convert_reduce_fusion
  620.2 9.1 %fusion.8 = (f32[768]{0:T(1024)S(1)}, f32[2048]{0:T(1024)S(1)}, bf16[2048,768]{1,0:T(8,128)(2,1)}) fusion(bf16[2048,768]{1,0:T(8,128)(2,1)S(1)} %copy-done.11, bf16[2048,768]{1,0:T(8,128)(2,1)} %param.16, f32[2048]{0:T(1024)S(1)} %fusion.50, f32[2048]{0:T(1024)S(1)} %broadcast_multiply_fusion.1, f32[32,768]{1,0:T(8,128)S(1)} %bitcast.132, ...), kind=kLoop, calls=%fused_computation.19 | loop fusion | flops 31454464 | bytes 15872000 | tf_op jit(solution)/shard_map/transpose(jvp())/reduce_sum | solution.py:18
  629.4 4.9 bitcast_reduce_fusion
  634.3 2.0 fusion.46
  636.6 4.6 convert_reduce_fusion.2
  641.2 11.2 %reduce-scatter.13.cloned.1.call-done = f32[96,192]{1,0:T(8,128)} async-done(((f32[768,192]{1,0:T(8,128)}), f32[96,192]{1,0:T(8,128)}) %reduce-scatter.13.cloned.1.call-update) | async-done | bytes 73744
  652.4 1.6 copy.95
  654.1 23.3 %all-reduce = (f32[2,192]{1,0:T(2,128)}, f32[768]{0:T(1024)}, f32[768]{0:T(1024)}, f32[768]{0:T(1024)}, f32[768]{0:T(1024)}, /*index=5*/f32[768]{0:T(1024)}, f32[768]{0:T(1024)}, f32[768]{0:T(1024)}) all-reduce(f32[2,192]{1,0:T(2,128)S(1)} %pad_maximum_fusion.1, ...), channel_id=1, replica_groups=mesh['dp'=8,'tensor'=4] {'dp'}, use_global_device_ids=true, to_apply=%region_20.0 | all-reduce | flops 5760 | bytes 46080 | tf_op jit(solution)/shard_map/psum | solution.py:174
  677.4 21.3 %reduce-scatter.9.cloned.1.call-done = f32[96,768]{1,0:T(8,128)} async-done(((f32[768,768]{1,0:T(8,128)}), f32[96,768]{1,0:T(8,128)}) %reduce-scatter.9.cloned.1.call-update) | async-done | bytes 294928 | tf_op jit(solution)/shard_map/reduce_scatter | solution.py:191
  698.8 46.7 %reduce-scatter.11.cloned.1.call-done = f32[768,96]{0,1:T(8,128)} async-done(((f32[768,768]{0,1:T(8,128)}), f32[768,96]{0,1:T(8,128)}) %reduce-scatter.11.cloned.1.call-update) | async-done | bytes 294928 | tf_op jit(solution)/shard_map/reduce_scatter | solution.py:192
  745.4 46.4 %reduce-scatter.7.cloned.1.call-done = f32[96,3,192]{2,0,1:T(8,128)} async-done(((f32[768,3,192]{2,0,1:T(8,128)}), f32[96,3,192]{2,0,1:T(8,128)}) %reduce-scatter.7.cloned.1.call-update) | async-done | bytes 221200 | tf_op jit(solution)/shard_map/reduce_scatter | solution.py:189
  791.9 63.1 %all-reduce.11.cloned.1.call-done = f32[2000,192]{0,1:T(8,128)} async-done(((f32[2000,192]{0,1:T(8,128)}), f32[2000,192]{0,1:T(8,128)}) %all-reduce.11.cloned.1.call-update) | async-done | bytes 1536016 | tf_op jit(solution)/shard_map/psum | solution.py:174
  855.0 2.7 copy.121
  (120 shorter events, 5.2 us)
Async XLA Ops:
  7.2 189.2 %copy-start = (bf16[768,768]{1,0:T(8,128)(2,1)S(1)}, bf16[768,768]{1,0:T(8,128)(2,1)}, u32[]{:S(2)}) copy-start(bf16[768,768]{1,0:T(8,128)(2,1)} %param.25) | copy-start | bytes 3538948
  7.2 23.4 %copy-start.31 = (f32[768]{0:T(1024)S(1)}, f32[768]{0:T(1024)}, u32[]{:S(2)}) copy-start(f32[768]{0:T(1024)} %param.27) | copy-start | bytes 9220
  7.2 23.4 %copy-start.34 = (f32[768]{0:T(1024)S(1)}, f32[768]{0:T(1024)}, u32[]{:S(2)}) copy-start(f32[768]{0:T(1024)} %param.28) | copy-start | bytes 9220
  7.2 177.5 %all-reduce.7.cloned.1.call-start = ((), (), s32[]{:S(2)}) async-start(), calls=%async_computation.4 | async-start | bytes 6291456 | tf_op jit(solution)/shard_map/psum | solution.py:96
  24.7 6.0 copy-start.2
  24.7 7.6 copy-start.39
  32.3 2.1 copy-start.25
  38.5 13.8 %copy-start.15 = (bf16[32,64,3,64]{1,0,3,2:T(8,128)(2,1)}, bf16[32,64,3,64]{1,0,3,2:T(8,128)(2,1)S(1)}, u32[]{:S(2)}) copy-start(bf16[32,64,3,64]{1,0,3,2:T(8,128)(2,1)S(1)} %reshape.151) | copy-start | bytes 2359300
  49.0 4.3 copy-start.22
  52.3 2.0 copy-start.9
  53.2 6.4 copy-start.28
  56.4 128.3 %copy-start.30 = (f32[768]{0:T(1024)S(1)}, f32[768]{0:T(1024)}, u32[]{:S(2)}) copy-start(f32[768]{0:T(1024)} %param.22) | copy-start | bytes 9220
  59.7 129.4 %copy-start.19 = (bf16[2048,192]{0,1:T(8,128)(2,1)}, bf16[2048,192]{0,1:T(8,128)(2,1)S(1)}, u32[]{:S(2)}) copy-start(bf16[2048,192]{0,1:T(8,128)(2,1)S(1)} %convert_element_type.101) | copy-start | bytes 2359300
  62.4 129.1 %copy-start.32 = (f32[768]{0:T(1024)S(1)}, f32[768]{0:T(1024)}, u32[]{:S(2)}) copy-start(f32[768]{0:T(1024)} %param.29) | copy-start | bytes 9220
  62.4 129.1 %copy-start.33 = (f32[768]{0:T(1024)S(1)}, f32[768]{0:T(1024)}, u32[]{:S(2)}) copy-start(f32[768]{0:T(1024)} %param.30) | copy-start | bytes 9220
  62.4 278.7 %all-reduce.9.cloned.1.call-start = ((), (), s32[]{:S(2)}) async-start(), calls=%async_computation.5 | async-start | bytes 6291456 | tf_op jit(solution)/shard_map/psum | solution.py:114
  184.8 4.3 copy-start.3
  184.8 4.7 copy-start.6
  191.4 2.1 copy-start.38
  193.6 2.8 copy-start.24
  193.6 3.0 copy-start.12
  193.6 3.0 copy-start.35
  196.6 18.5 %copy-start.21 = (f32[2048,768]{1,0:T(8,128)}, f32[2048,768]{1,0:T(8,128)S(1)}, u32[]{:S(2)}) copy-start(f32[2048,768]{1,0:T(8,128)S(1)} %fusion.61) | copy-start | bytes 18874372
  215.1 1.7 copy-start.40
  220.9 394.6 %all-reduce.13.cloned.1.call-start = ((), (), s32[]{:S(2)}) async-start(), calls=%async_computation.11 | async-start | bytes 12582912 | tf_op jit(solution)/shard_map/psum | solution.py:104
  226.6 1.7 copy-start.26
  341.1 7.2 copy-start.4
  341.1 7.2 copy-start.7
  341.1 7.2 copy-start.18
  348.4 6.3 copy-start.13
  352.0 2.7 copy-start.8
  357.8 3.3 copy-start.10
  357.8 3.3 copy-start.23
  363.1 1.4 copy-start.17
  363.1 3.6 copy-start.16
  386.2 1.4 copy-start.29
  393.1 1.1 copy-start.20
  393.1 259.4 %reduce-scatter.13.cloned.1.call-start = ((), (), s32[]{:S(2)}) async-start(), calls=%async_computation.10 | async-start | bytes 884736
  400.9 297.8 %reduce-scatter.9.cloned.1.call-start = ((), (), s32[]{:S(2)}) async-start(), calls=%async_computation.8 | async-start | bytes 2654208 | tf_op jit(solution)/shard_map/reduce_scatter | solution.py:191
  408.0 337.4 %reduce-scatter.11.cloned.1.call-start = ((), (), s32[]{:S(2)}) async-start(), calls=%async_computation.9 | async-start | bytes 2654208 | tf_op jit(solution)/shard_map/reduce_scatter | solution.py:192
  415.0 376.9 %reduce-scatter.7.cloned.1.call-start = ((), (), s32[]{:S(2)}) async-start(), calls=%async_computation.7 | async-start | bytes 2654208 | tf_op jit(solution)/shard_map/reduce_scatter | solution.py:189
  421.7 198.4 %copy-start.36 = (f32[768]{0:T(1024)S(1)}, f32[768]{0:T(1024)}, u32[]{:S(2)}) copy-start(f32[768]{0:T(1024)} %param.26) | copy-start | bytes 9220
  421.8 433.2 %all-reduce.11.cloned.1.call-start = ((), (), s32[]{:S(2)}) async-start(), calls=%async_computation.6 | async-start | bytes 3145728 | tf_op jit(solution)/shard_map/psum | solution.py:174
  615.5 4.7 copy-start.11
  615.5 4.7 copy-start.27
  615.5 13.9 %slice-start = ((s8[6291456]{0:T(1024)(128)(4,1)}), s8[4194304]{0:T(1024)(128)(4,1)S(1)}, s32[]{:S(2)}) async-start(s8[6291456]{0:T(1024)(128)(4,1)} %bitcast.121), calls=%async_computation.12 | async-start | bytes 8388608
  620.2 9.2 %copy-start.5 = (bf16[2048,768]{1,0:T(8,128)(2,1)S(1)}, bf16[2048,768]{1,0:T(8,128)(2,1)}, u32[]{:S(2)}) copy-start(bf16[2048,768]{1,0:T(8,128)(2,1)} %param.16) | copy-start | bytes 9437188
  620.2 9.2 %slice-start.1 = ((s8[6291456]{0:T(1024)(128)(4,1)}), s8[2097152]{0:T(1024)(128)(4,1)S(1)}, s32[]{:S(2)}) async-start(s8[6291456]{0:T(1024)(128)(4,1)} %bitcast.121), calls=%async_computation.13 | async-start | bytes 4194304
  620.2 9.2 %copy-start.14 = (bf16[2048,768]{1,0:T(8,128)(2,1)S(1)}, bf16[2048,768]{1,0:T(8,128)(2,1)}, u32[]{:S(2)}) copy-start(bf16[2048,768]{1,0:T(8,128)(2,1)} %param.31) | copy-start | bytes 9437188
  629.4 5.0 copy-start.37
  636.6 221.1 %copy-start.1 = (bf16[768,768]{1,0:T(8,128)(2,1)S(1)}, bf16[768,768]{1,0:T(8,128)(2,1)}, u32[]{:S(2)}) copy-start(bf16[768,768]{1,0:T(8,128)(2,1)} %param.25) | copy-start | bytes 3538948
Sparse Core Ops, SparseCore 0:
  62.5 122.1 all-reduce.6
  221.0 120.0 all-reduce.8
  393.2 222.2 all-reduce.12
  618.5 33.9 reduce-scatter.12
  656.2 42.5 reduce-scatter.8
  702.9 42.4 reduce-scatter.10
  749.4 42.4 reduce-scatter.6
  796.0 58.9 all-reduce.10
where the time goes:
time: 868 us; the launch traced here: 865 us
  waiting for transfers between devices  614 us (71%)
  matrix products  85.8 us (10%)
  other arithmetic  58.1 us (7%)
  local copies, waits for them, and re-layouts  53.7 us (6%)
  blocking collectives  38.2 us (4%)
  between operations  15.1 us (2%)
    psum x1, waiting for transfers between devices, body(): lax.psum(mlp_term.astype(jnp.bfloat16), 'tensor').astype(jnp.float32)  193 us
    psum x1, waiting for transfers between devices, body(): lax.psum(attn_term.astype(jnp.bfloat16), 'tensor').astype(jnp.float32)  122 us
    psum x1, waiting for transfers between devices, body(): lax.psum(back_two.astype(jnp.bfloat16), 'tensor').astype(jnp.float32)  109 us
    psum x1, waiting for transfers between devices, body(): lax.psum((grad_bqv, grad_bout, grad_bin, grad_bback, grad_gain_one, grad_...  63.1 us
    reduce_scatter x1, waiting for transfers between devices, body(): lax.psum_scatter(grad_wback, 'dp', scatter_dimension=1, tiled=True)  46.7 us
    reduce_scatter x1, waiting for transfers between devices, body(): lax.psum_scatter(grad_wqkv, 'dp', scatter_dimension=0, tiled=True)  46.4 us
    dot_general x4, matrix products, dot_cols(): lax.dot_general(left, right, (((1,), (1,)), ((), ())), preferred_element_...  29.3 us
    psum x1, blocking collectives, body(): lax.psum((grad_bqv, grad_bout, grad_bin, grad_bback, grad_gain_one, grad_...  23.3 us
  transfers between devices with their start and end apart: 8, of which 8 were waited for; matrix products, arithmetic and copies ran while one was open for 7% of the time, Pallas kernels for 0%

commit v1 on v0

v1 whole, which is shorter than its diff:
```python
import functools

import jax
import jax.numpy as jnp
from jax import lax
from jax.experimental import pallas as pl
from jax.experimental.pallas import tpu as pltpu
from jax.sharding import PartitionSpec as P

HEAD = 64
LEN = 64
EPS = 1e-05
BR = 256
VMEM_BYTES = 56 * 1024 * 1024
HIGHEST_PREC = lax.Precision.HIGHEST
F32 = jnp.float32
BF16 = jnp.bfloat16


def dot_nn(a, b):
    return lax.dot_general(a, b, (((1,), (0,)), ((), ())), preferred_element_type=F32)


def dot_nt(a, b):
    return lax.dot_general(a, b, (((1,), (1,)), ((), ())), preferred_element_type=F32)


def dot_tn(a, b):
    return lax.dot_general(a, b, (((0,), (0,)), ((), ())), preferred_element_type=F32)


def params():
    return pltpu.CompilerParams(
        dimension_semantics=("arbitrary",), vmem_limit_bytes=VMEM_BYTES
    )


def rows_spec(width, rows=BR):
    return pl.BlockSpec((rows, width), lambda i, *_: (i, 0))


def whole_spec(shape):
    return pl.BlockSpec(shape, lambda i, *_: (0,) * len(shape))


def slot_spec(shape, k):
    return pl.BlockSpec((1,) + shape, lambda i, s: (s[k],) + (0,) * len(shape))


def normed(x):
    mean = jnp.mean(x, axis=-1, keepdims=True)
    centred = x - mean
    spread = jnp.mean(centred * centred, axis=-1, keepdims=True)
    inv = lax.rsqrt(spread + EPS)
    return centred * inv, inv


def norm_back(d_out, gain, xhat, inv):
    gy = d_out * gain
    m1 = jnp.mean(gy, axis=-1, keepdims=True)
    m2 = jnp.mean(gy * xhat, axis=-1, keepdims=True)
    return inv * (gy - m1 - xhat * m2)


def fold8(x):
    return jnp.sum(x.reshape(x.shape[0] // 8, 8, x.shape[1]), axis=0)


def entry_of(tok_ref, time_ref):
    tok = tok_ref[...].astype(F32)
    n = tok.shape[0] // LEN
    return (tok.reshape(n, LEN, tok.shape[1]) + time_ref[0][:, None, :]).reshape(tok.shape)


def half_masks():
    lane = lax.broadcasted_iota(jnp.int32, (LEN, 2 * HEAD), 1)
    low = (lane < HEAD).astype(F32)
    return low.astype(BF16), (1.0 - low).astype(BF16), lane < HEAD


def block_diag(x, mlo, mhi):
    return jnp.concatenate([x * mlo, x * mhi], axis=0)


def load_pair(wa_ref, wb_ref, wqkv, wo):
    hc = HEAD * 3
    for t in range(3):
        wqkv[2 * t * hc : (2 * t + 1) * hc, :] = wa_ref[0, t * hc : (t + 1) * hc, :]
        wqkv[(2 * t + 1) * hc : (2 * t + 2) * hc, :] = wb_ref[0, t * hc : (t + 1) * hc, :]
    wo[:hc, :] = wa_ref[0, 3 * hc :, :]
    wo[hc:, :] = wb_ref[0, 3 * hc :, :]


def attend(n_one, wqkv, wo, bias, qkv_ref, p_ref, mix_ref):
    width = wo.shape[0]
    qkv_ref[...] = (dot_nt(n_one, wqkv[...]) + bias).astype(BF16)
    mlo, mhi, low = half_masks()
    for s in range(n_one.shape[0] // LEN):
        rows = slice(s * LEN, (s + 1) * LEN)
        for j in range(width // 128):
            cols = slice(j * 128, (j + 1) * 128)
            q = qkv_ref[rows, j * 128 : (j + 1) * 128]
            k = qkv_ref[rows, width + j * 128 : width + (j + 1) * 128]
            v = qkv_ref[rows, 2 * width + j * 128 : 2 * width + (j + 1) * 128]
            scores = dot_nt(k, block_diag(q, mlo, mhi))
            top = jnp.max(scores, axis=0, keepdims=True)
            e = jnp.exp((scores - top) * (HEAD**-0.5))
            p = (e * (1.0 / jnp.sum(e, axis=0, keepdims=True))).astype(BF16)
            p_ref[rows, cols] = p
            r = dot_tn(p, v)
            mix_ref[rows, cols] = jnp.where(low, r[:LEN], r[LEN:]).astype(BF16)
    return dot_nn(mix_ref[...], wo[...])


def attend_first(
    slots, tok, time, g1, s1, wa, wb, bias, n_one_ref, qkv_ref, p_ref, mix_ref, part_ref, wqkv, wo
):
    @pl.when(pl.program_id(0) == 0)
    def _():
        load_pair(wa, wb, wqkv, wo)

    xhat, _ = normed(entry_of(tok, time))
    n_one = (xhat * g1[...] + s1[...]).astype(BF16)
    n_one_ref[...] = n_one
    part_ref[...] = attend(n_one, wqkv, wo, bias[...], qkv_ref, p_ref, mix_ref)


def attend_last(
    slots, tok, time, n_one, part, bout, g2, s2, wa, wb, bias,
    qkv_ref, p_ref, middle_ref, n_two_ref, wqkv, wo, mix_ref,
):
    @pl.when(pl.program_id(0) == 0)
    def _():
        load_pair(wa, wb, wqkv, wo)

    more = attend(n_one[...], wqkv, wo, bias[...], qkv_ref, p_ref, mix_ref)
    middle = entry_of(tok, time) + part[...] + more + bout[...]
    middle_ref[...] = middle
    xhat, _ = normed(middle)
    n_two_ref[...] = (xhat * g2[...] + s2[...]).astype(BF16)


ERF_P = 0.3275911
ERF_A = (0.254829592, -0.284496736, 1.421413741, -1.453152027, 1.061405429)


def gelu_both(x):
    bell = jnp.exp(x * x * (-0.5))
    t = 1.0 / (1.0 + jnp.abs(x) * (ERF_P * 0.5**0.5))
    poly = t * (
        0.5 * ERF_A[0]
        + t * (0.5 * ERF_A[1] + t * (0.5 * ERF_A[2] + t * (0.5 * ERF_A[3] + t * (0.5 * ERF_A[4]))))
    )
    tail = poly * bell
    cdf = jnp.where(x >= 0, 1.0 - tail, tail)
    return x * cdf, cdf + x * bell * 0.3989422804014327


def mlp_slot(n_two, c, wi, wb, b):
    pre = dot_nt(n_two, wi) + b
    d_act = dot_nt(c, wb)
    act, slope = gelu_both(pre)
    act = act.astype(BF16)
    d_pre = (d_act * slope).astype(BF16)
    return act, d_pre


def mlp_first(n_two, c, wi, wb, b, out_ref, dn2_ref, act_ref, dpre_ref, gbin_ref):
    act, d_pre = mlp_slot(n_two[...], c[...], wi[...], wb[...], b[...])
    act_ref[...] = act
    dpre_ref[...] = d_pre

    @pl.when(pl.program_id(0) == 0)
    def _():
        gbin_ref[...] = jnp.zeros_like(gbin_ref)

    gbin_ref[...] += fold8(d_pre.astype(F32))
    out_ref[...] = dot_nn(act, wb[...])
    dn2_ref[...] = dot_nn(d_pre, wi[...])


def mlp_rest(
    slots, n_two, c, middle, out_in, dn2_in, g2, bback, w1, w2, w3, b,
    out_ref, dmid_ref, dml_ref, sums_ref,
):
    hid = b.shape[-1] // 3
    out = out_in[...]
    dn2 = dn2_in[...]
    for k, w in enumerate((w1, w2, w3)):
        wi = w[0, :hid, :]
        wb = w[0, hid:, :]
        act, d_pre = mlp_slot(n_two[...], c[...], wi, wb, b[:, k * hid : (k + 1) * hid])
        out = out + dot_nn(act, wb)
        dn2 = dn2 + dot_nn(d_pre, wi)
    mid = middle[...]
    cot = c[...].astype(F32)
    out_ref[...] = (mid + out + bback[...]).astype(BF16)
    xhat, inv = normed(mid)
    d_mid = cot + norm_back(dn2, g2[...], xhat, inv)
    dmid_ref[...] = d_mid
    dml_ref[...] = d_mid.astype(BF16)

    @pl.when(pl.program_id(0) == 0)
    def _():
        sums_ref[...] = jnp.zeros_like(sums_ref)

    sums_ref[0:8, :] += fold8(dn2 * xhat)
    sums_ref[8:16, :] += fold8(dn2)
    sums_ref[16:24, :] += fold8(d_mid)
    sums_ref[24:32, :] += fold8(cot)


def attend_back(dml, qkv, p, wqkv, wo, dqkv, dmix):
    width = wo.shape[0]
    scale = HEAD**-0.5
    dmix[...] = dot_nt(dml, wo[...]).astype(BF16)
    mlo, mhi, low = half_masks()
    for s in range(dml.shape[0] // LEN):
        rows = slice(s * LEN, (s + 1) * LEN)
        for j in range(width // 128):
            cols = slice(j * 128, (j + 1) * 128)
            kcols = slice(width + j * 128, width + (j + 1) * 128)
            vcols = slice(2 * width + j * 128, 2 * width + (j + 1) * 128)
            q, k, v = qkv[rows, cols], qkv[rows, kcols], qkv[rows, vcols]
            prob = p[rows, cols]
            d_out = block_diag(dmix[rows, cols], mlo, mhi)
            dqkv[rows, vcols] = dot_nn(prob, d_out).astype(BF16)
            d_p = dot_nt(v, d_out)
            pf = prob.astype(F32)
            dot = jnp.sum(pf * d_p, axis=0, keepdims=True)
            d_s = (pf * (d_p - dot)).astype(BF16)
            dqkv[rows, kcols] = (dot_nn(d_s, block_diag(q, mlo, mhi)) * scale).astype(BF16)
            r = dot_tn(d_s, k)
            dqkv[rows, cols] = (jnp.where(low, r[:LEN], r[LEN:]) * scale).astype(BF16)
    return dot_nn(dqkv[...], wqkv[...])


def back_first(slots, dml, qkv, p, wa, wb, dn1_ref, dq_ref, dk_ref, dv_ref, sums_ref, wqkv, wo, dqkv, dmix):
    @pl.when(pl.program_id(0) == 0)
    def _():
        load_pair(wa, wb, wqkv, wo)
        sums_ref[...] = jnp.zeros_like(sums_ref)

    dn1_ref[...] = attend_back(dml[...], qkv, p, wqkv, wo, dqkv, dmix)
    hc = HEAD * 3
    width = 2 * hc
    for t, ref in enumerate((dq_ref, dk_ref, dv_ref)):
        ref[...] = dqkv[:, t * width : t * width + hc]
    sums_ref[...] += fold8(dqkv[...].astype(F32))


def back_last(
    slots, tok, time, dml, dmid, dn1, g1, qkv, p, wa, wb,
    gtok_ref, sent_ref, sums_ref, wqkv, wo, dqkv, dmix,
):
    @pl.when(pl.program_id(0) == 0)
    def _():
        load_pair(wa, wb, wqkv, wo)
        sums_ref[...] = jnp.zeros_like(sums_ref)

    d_n = dn1[...] + attend_back(dml[...], qkv, p, wqkv, wo, dqkv, dmix)
    xhat, inv = normed(entry_of(tok, time))
    d_entry = dmid[...] + norm_back(d_n, g1[...], xhat, inv)
    gtok_ref[...] = d_entry.astype(BF16)
    sent_ref[0] = jnp.sum(d_entry.reshape(d_entry.shape[0] // LEN, LEN, -1), axis=1)
    sums_ref[0:8, :] += fold8(d_n * xhat)
    sums_ref[8:16, :] += fold8(d_n)


def call(kernel, grid, in_specs, out_specs, out_shape, scratch, slots, args):
    if slots is None:
        return pl.pallas_call(
            kernel, grid=grid, in_specs=in_specs, out_specs=out_specs, out_shape=out_shape,
            scratch_shapes=scratch, compiler_params=params(),
        )(*args)
    return pl.pallas_call(
        kernel,
        grid_spec=pltpu.PrefetchScalarGridSpec(
            num_scalar_prefetch=1, grid=grid, in_specs=in_specs, out_specs=out_specs,
            scratch_shapes=scratch,
        ),
        out_shape=out_shape,
        compiler_params=params(),
    )(slots, *args)


def body(
    tokens, timesteps, time_table, w_qkv, b_qv, w_out, b_out, w_in, b_in, w_back, b_back,
    gain_one, shift_one, gain_two, shift_two, cotangent,
):
    sentences = timesteps.shape[0]
    rows, dim = tokens.shape
    hc = w_out.shape[0]
    hid = w_back.shape[0]
    table_cols = time_table.shape[1]
    n_tensor = dim // hc
    me = lax.axis_index("tensor")
    part = lax.axis_index("dp")
    dp = lax.axis_size("dp")
    slots = (me ^ jnp.arange(n_tensor, dtype=jnp.int32)).astype(jnp.int32)

    steps_iota = lax.broadcasted_iota(jnp.int32, (sentences, time_table.shape[0]), 1)
    picked = timesteps[:, None] == steps_iota
    own_rows = jnp.dot(picked.astype(BF16), time_table, preferred_element_type=F32).astype(BF16)
    time_rows = lax.all_gather(own_rows, "tensor", axis=1, tiled=True).astype(F32)
    time_blocks = time_rows.reshape(rows // BR, BR // LEN, dim)

    att_own = jnp.concatenate(
        [jnp.transpose(w_qkv, (1, 2, 0)).reshape(3 * hc, dim), w_out], axis=0
    )
    wi_own = w_in.T
    mlp_own = jnp.concatenate([wi_own, w_back], axis=0)

    def everywhere(shard):
        n = shard.shape[0] // dp
        piece = lax.dynamic_slice_in_dim(shard, part * n, n, 0)
        return lax.all_gather(piece, ("tensor", "dp"), axis=0, tiled=True).reshape(
            n_tensor, shard.shape[0], dim
        )

    att_all = everywhere(att_own)
    mlp_all = everywhere(mlp_own)
    biases = lax.all_gather(jnp.concatenate([b_qv.reshape(-1), b_in]), "tensor", axis=0)
    biases = jnp.take(biases, slots, axis=0)
    bq, bv, bi = biases[:, :hc], biases[:, hc : 2 * hc], biases[:, 2 * hc :]
    no_bias = jnp.zeros((2 * hc,), F32)

    def pair_bias(k):
        return jnp.concatenate(
            [bq[k : k + 2].reshape(-1), no_bias, bv[k : k + 2].reshape(-1)]
        ).reshape(1, 6 * hc)

    row = lambda v: v.reshape(1, -1)
    nb = rows // BR
    grid = (nb,)
    time_spec = pl.BlockSpec((1, BR // LEN, dim), lambda i, *_: (i, 0, 0))
    vec = whole_spec((1, dim))
    att_spec = lambda k: slot_spec((4 * hc, dim), k)
    pair_scr = [pltpu.VMEM((6 * hc, dim), BF16), pltpu.VMEM((2 * hc, dim), BF16)]
    sds = jax.ShapeDtypeStruct

    n_one, qkv_a, p_a, mix_a, attn_part = call(
        attend_first, grid,
        [rows_spec(dim), time_spec, vec, vec, att_spec(0), att_spec(1), whole_spec((1, 6 * hc))],
        [rows_spec(dim), rows_spec(6 * hc), rows_spec(2 * hc), rows_spec(2 * hc), rows_spec(dim)],
        [sds((rows, dim), BF16), sds((rows, 6 * hc), BF16), sds((rows, 2 * hc), BF16),
         sds((rows, 2 * hc), BF16), sds((rows, dim), F32)],
        pair_scr, slots,
        (tokens, time_blocks, row(gain_one), row(shift_one), att_all, att_all, pair_bias(0)),
    )
    qkv_b, p_b, middle, n_two = call(
        attend_last, grid,
        [rows_spec(dim), time_spec, rows_spec(dim), rows_spec(dim), vec, vec, vec,
         att_spec(2), att_spec(3), whole_spec((1, 6 * hc))],
        [rows_spec(6 * hc), rows_spec(2 * hc), rows_spec(dim), rows_spec(dim)],
        [sds((rows, 6 * hc), BF16), sds((rows, 2 * hc), BF16), sds((rows, dim), F32),
         sds((rows, dim), BF16)],
        pair_scr + [pltpu.VMEM((BR, 2 * hc), BF16)], slots,
        (tokens, time_blocks, n_one, attn_part, row(b_out), row(gain_two), row(shift_two),
         att_all, att_all, pair_bias(2)),
    )
    out_acc, dn2_acc, act, d_pre, gbin = call(
        mlp_first, grid,
        [rows_spec(dim), rows_spec(dim), whole_spec((hid, dim)), whole_spec((hid, dim)),
         whole_spec((1, hid))],
        [rows_spec(dim), rows_spec(dim), rows_spec(hid), rows_spec(hid), whole_spec((8, hid))],
        [sds((rows, dim), F32), sds((rows, dim), F32), sds((rows, hid), BF16),
         sds((rows, hid), BF16), sds((8, hid), F32)],
        [], None,
        (n_two, cotangent, wi_own, w_back, row(b_in)),
    )
    mlp_spec = lambda k: slot_spec((2 * hid, dim), k)
    output, d_mid, d_mid_low, sums_two = call(
        mlp_rest, grid,
        [rows_spec(dim), rows_spec(dim), rows_spec(dim), rows_spec(dim), rows_spec(dim), vec, vec,
         mlp_spec(1), mlp_spec(2), mlp_spec(3), whole_spec((1, 3 * hid))],
        [rows_spec(dim), rows_spec(dim), rows_spec(dim), whole_spec((32, dim))],
        [sds((rows, dim), BF16), sds((rows, dim), F32), sds((rows, dim), BF16),
         sds((32, dim), F32)],
        [], slots,
        (n_two, cotangent, middle, out_acc, dn2_acc, row(gain_two), row(b_back),
         mlp_all, mlp_all, mlp_all, bi[1:].reshape(1, -1)),
    )
    back_scr = pair_scr + [pltpu.VMEM((BR, 6 * hc), BF16), pltpu.VMEM((BR, 2 * hc), BF16)]
    dn1_acc, d_q, d_k, d_v, sums_qkv = call(
        back_first, grid,
        [rows_spec(dim), rows_spec(6 * hc), rows_spec(2 * hc), att_spec(0), att_spec(1)],
        [rows_spec(dim), rows_spec(hc), rows_spec(hc), rows_spec(hc), whole_spec((8, 6 * hc))],
        [sds((rows, dim), F32)] + [sds((rows, hc), BF16)] * 3 + [sds((8, 6 * hc), F32)],
        back_scr, slots,
        (d_mid_low, qkv_a, p_a, att_all, att_all),
    )
    grad_tokens, per_sentence, sums_one = call(
        back_last, grid,
        [rows_spec(dim), time_spec, rows_spec(dim), rows_spec(dim), rows_spec(dim), vec,
         rows_spec(6 * hc), rows_spec(2 * hc), att_spec(2), att_spec(3)],
        [rows_spec(dim), time_spec, whole_spec((16, dim))],
        [sds((rows, dim), BF16), sds((nb, BR // LEN, dim), F32), sds((16, dim), F32)],
        back_scr, slots,
        (tokens, time_blocks, d_mid_low, d_mid, dn1_acc, row(gain_one), qkv_b, p_b,
         att_all, att_all),
    )

    def scattered(grad):
        return lax.psum_scatter(
            grad.astype(BF16), "dp", scatter_dimension=0, tiled=True
        ).astype(F32)

    grad_win = scattered(dot_tn(n_two, d_pre))
    grad_wback = scattered(dot_tn(cotangent, act)).T
    grad_wout = scattered(dot_tn(d_mid_low, mix_a[:, :hc])).T
    grad_wqkv = scattered(
        jnp.stack([dot_tn(n_one, d) for d in (d_q, d_k, d_v)], axis=1)
    )

    own_cols = lax.dynamic_slice_in_dim(
        per_sentence.reshape(sentences, dim), me * table_cols, table_cols, 1
    )
    all_cols = lax.all_gather(own_cols, "dp", axis=0, tiled=True)
    all_steps = lax.all_gather(timesteps, "dp", axis=0, tiled=True)
    all_picked = all_steps[:, None] == lax.broadcasted_iota(
        jnp.int32, (all_steps.shape[0], time_table.shape[0]), 1
    )
    grad_table = lax.dot_general(
        all_picked.astype(F32), all_cols, (((0,), (0,)), ((), ())),
        precision=HIGHEST_PREC, preferred_element_type=F32,
    )
    sums_two = jnp.sum(sums_two.reshape(4, 8, dim), axis=1)
    sums_one = jnp.sum(sums_one.reshape(2, 8, dim), axis=1)
    sums_qkv = jnp.sum(sums_qkv, axis=0)
    small = lax.psum(
        jnp.concatenate(
            [sums_two.reshape(-1), sums_one.reshape(-1), jnp.sum(gbin, axis=0),
             sums_qkv[:hc], sums_qkv[4 * hc : 5 * hc]]
        ),
        "dp",
    )
    cut = lambda k: small[k * dim : (k + 1) * dim]
    base = 6 * dim
    grad_bin = small[base : base + hid]
    grad_bqv = small[base + hid :].reshape(2, hc)
    return (
        output, grad_tokens, grad_table, grad_wqkv, grad_bqv, grad_wout, cut(2), grad_win,
        grad_bin, grad_wback, cut(3), cut(4), cut(5), cut(0), cut(1),
    )


def solution(mesh):
    return jax.shard_map(
        body,
        mesh=mesh,
        in_specs=(
            P("dp", None), P("dp"), P(None, "tensor"), P(None, None, "tensor"), P(None, "tensor"),
            P("tensor", None), P(), P(None, "tensor"), P("tensor"), P("tensor", None), P(), P(),
            P(), P(), P(), P("dp", None),
        ),
        out_specs=(
            P("dp", None), P("dp", None), P(None, "tensor"), P("dp", None, "tensor"),
            P(None, "tensor"), P("tensor", "dp"), P(), P("dp", "tensor"), P("tensor"),
            P("tensor", "dp"), P(), P(), P(), P(), P(),
        ),
        check_vma=False,
    )
```

time: 868 us -> 516 us (0.59)
  waiting for transfers between devices: 614 us -> 170 us
  Pallas kernels: 0 us -> 208 us
  matrix products: 85.8 us -> 22 us
  other arithmetic: 58.1 us -> 8.43 us
  local copies, waits for them, and re-layouts: 53.7 us -> 22.7 us
  blocking collectives: 38.2 us -> 68.2 us
    psum x4 -> x0, waiting for transfers between devices: 488 us -> none  [the longest x1 193 us: body(): lax.psum(mlp_term.astype(jnp.bfloat16), 'tensor').astype(jnp.float32)]
    pallas_call x0 -> x6, Pallas kernels: none -> 208 us  [the longest x5 190 us: call(): pl.pallas_call(kernel, grid_spec=pltpu.PrefetchScalarGridSpec(num_scalar_...]
    all_gather x0 -> x2, waiting for transfers between devices: none -> 113 us  [everywhere(): lax.all_gather(piece, ('tensor', 'dp'), axis=0, tiled=True)]
    reduce_scatter x3 -> x2, waiting for transfers between devices: 114 us -> 38.9 us  [scattered(): lax.psum_scatter(grad.astype(BF16), 'dp', scatter_dimension=0, tiled=True)]
    dot_general x19 -> x8, matrix products: 79.1 us -> 22 us  [the longest x6 18.7 us: dot_tn(): lax.dot_general(a, b, (((0,), (0,)), ((), ())), preferred_element_type=F32)]
    reduce_sum x13 -> x4, other arithmetic: 47.5 us -> 0.89 us  [the longest x1 0.82 us: body(): sums_one = jnp.sum(sums_one.reshape(2, 8, dim), axis=1)]
    all_gather x1 -> x3, blocking collectives: 14.9 us -> 37.4 us  [the longest x1 14.8 us: body(): lax.all_gather(jnp.concatenate([b_qv.reshape(-1), b_in]), 'tensor', axis=0)]
    reshape x8 -> x21, local copies, waits for them, and re-layouts: 23.3 us -> 9.5 us  [the longest x7 4.75 us: body(): row = lambda v: v.reshape(1, -1)]
  transfers between devices with their start and end apart: 8 -> 6, of which waited for: 8 -> 4; matrix products, arithmetic and copies ran while one was open for 7% -> 7% of each run, Pallas kernels for 0% -> 14%
where the time goes in v1:
time: 516 us; the launch traced here: 515 us
  Pallas kernels  208 us (40%)
  waiting for transfers between devices  170 us (33%)
  blocking collectives  68.2 us (13%)
  local copies, waits for them, and re-layouts  22.7 us (4%)
  matrix products  22 us (4%)
  between operations  15.1 us (3%)
  other arithmetic  8.43 us (2%)
    pallas_call x5, Pallas kernels, call(): pl.pallas_call(kernel, grid_spec=pltpu.PrefetchScalarGridSpec(num_scalar_...  190 us
    all_gather x2, waiting for transfers between devices, everywhere(): lax.all_gather(piece, ('tensor', 'dp'), axis=0, tiled=True)  113 us
    reduce_scatter x2, waiting for transfers between devices, scattered(): lax.psum_scatter(grad.astype(BF16), 'dp', scatter_dimension=0, tiled=True)  38.9 us
    psum x1, blocking collectives, body(): lax.psum(jnp.concatenate([sums_two.reshape(-1), sums_one.reshape(-1), jnp...  23.5 us
    pallas_call x1, Pallas kernels, call(): pl.pallas_call(kernel, grid=grid, in_specs=in_specs, out_specs=out_specs,...  18.9 us
    dot_general x6, matrix products, dot_tn(): lax.dot_general(a, b, (((0,), (0,)), ((), ())), preferred_element_type=F32)  18.7 us
    unnamed x8, waiting for transfers between devices  17.9 us
    all_gather x1, blocking collectives, body(): lax.all_gather(jnp.concatenate([b_qv.reshape(-1), b_in]), 'tensor', axis=0)  14.8 us
  transfers between devices with their start and end apart: 6, of which 4 were waited for; matrix products, arithmetic and copies ran while one was open for 7% of the time, Pallas kernels for 14%

profile of v1, /device:TPU:0, one launch (start us, length us, event | category | flops | bytes accessed | tf_op | source)
XLA Modules:
  0.0 515.1 jit_solution(14509951820721087760)
XLA Ops:
  7.3 1.8 fusion.9
  9.2 0.8 reshape.146
  9.9 1.3 reshape.156.b
  11.2 0.7 pad_maximum_fusion.3
  11.9 14.8 %all-gather.2 = f32[4,1,1152]{2,1,0:T(1,128)S(1)} all-gather(f32[1,1,1152]{2,1,0:T(1,128)S(1)} %reshape.182), channel_id=2, replica_groups=mesh['dp'=8,'tensor'=4] {'tensor'}, dimensions={0}, use_global_device_ids=true | all-gather | bytes 23040 | tf_op jit(solution)/shard_map/all_gather | solution.py:323
  26.7 0.6 gather_fusion
  27.5 0.1 reshape.147
  27.5 0.1 reshape.148
  27.8 0.6 reshape.149.bias
  28.4 1.0 fusion.5
  29.4 13.4 %all-gather.1 = bf16[4,192,32]{1,2,0:T(8,128)(2,1)S(1)} all-gather(bf16[1,192,32]{1,2,0:T(8,128)(2,1)S(1)} %fusion.5), channel_id=1, replica_groups=mesh['dp'=8,'tensor'=4] {'tensor'}, dimensions={0}, use_global_device_ids=true | all-gather | bytes 61440 | tf_op jit(solution)/shard_map/all_gather | solution.py:305
  42.9 0.1 reshape.189
  43.0 0.7 reshape.167.time
  43.7 0.6 reshape.142.g1
  44.3 0.6 reshape.143.s1
  44.8 0.6 reshape.155.bias
  45.4 0.6 reshape.151.g2
  46.0 0.6 reshape.150.bout
  46.6 0.6 reshape.152.s2
  47.2 1.4 copy.41
  48.6 0.5 iota_xor_fusion.slots
  49.1 28.9 %all-gather.6.cloned.1.call-done = bf16[3072,768]{1,0:T(8,128)(2,1)} async-done(((bf16[96,768]{1,0:T(8,128)(2,1)}), bf16[3072,768]{1,0:T(8,128)(2,1)}) %all-gather.6.cloned.1.call-update) | async-done | bytes 4718608 | tf_op jit(solution)/shard_map/all_gather | solution.py:317
  78.1 34.8 %shard_map.271 = (bf16[2048,768]{1,0:T(8,128)(2,1)}, bf16[2048,1152]{1,0:T(8,128)(2,1)}, bf16[2048,384]{1,0:T(8,128)(2,1)}, bf16[2048,384]{1,0:T(8,128)(2,1)}, f32[2048,768]{1,0:T(8,128)}) custom-call(s32[4]{0:T(128)} %iota_xor_fusion.slots, bf16[2048,768]{1,0:T(8,128)(2,1)} %tok.5, f32[8,4,768]{2,1,0:T(4,128)} %reshape.167.time, f32[1,768]{1,0:T(1,128)} %reshape.142.g1, ...), custom_call_target="tpu_custom_call" | custom-call | tf_op jit(solution)/shard_map/pallas_call | solution.py:276
  112.9 35.4 %shard_map.272 = (bf16[2048,1152]{1,0:T(8,128)(2,1)}, bf16[2048,384]{1,0:T(8,128)(2,1)}, f32[2048,768]{1,0:T(8,128)}, bf16[2048,768]{1,0:T(8,128)(2,1)}) custom-call(s32[4]{0:T(128)} %iota_xor_fusion.slots, bf16[2048,768]{1,0:T(8,128)(2,1)} %tok.5, f32[8,4,768]{2,1,0:T(4,128)} %reshape.167.time, bf16[2048,768]{1,0:T(8,128)(2,1)} %get-tuple-element.41.n_one, ...), custom_call_target="tpu_custom_call" | custom-call | tf_op jit(solution)/shard_map/pallas_call | solution.py:276
  148.3 18.9 %shard_map.273 = (f32[2048,768]{1,0:T(8,128)}, f32[2048,768]{1,0:T(8,128)}, bf16[2048,768]{1,0:T(8,128)(2,1)}, bf16[2048,768]{1,0:T(8,128)(2,1)}, f32[8,768]{1,0:T(8,128)}) custom-call(bf16[2048,768]{1,0:T(8,128)(2,1)} %get-tuple-element.43.n_two, bf16[2048,768]{1,0:T(8,128)(2,1)} %c.3, bf16[768,768]{1,0:T(8,128)(2,1)} %bitcast.67, bf16[768,768]{1,0:T(8,128)(2,1)} %wb.1, ...), custom_call_target="tpu_custom_call" | custom-call | tf_op jit(solution)/shard_map/pallas_call | solution.py:272
  167.2 5.7 %fusion.1 = bf16[768,768]{0,1:T(8,128)(2,1)} fusion(bf16[2048,768]{1,0:T(8,128)(2,1)} %get-tuple-element.66, bf16[2048,768]{1,0:T(8,128)(2,1)S(1)} %copy-done.2), kind=kOutput, calls=%fused_computation.7 | convolution fusion | flops 2416508928 | bytes 7471104 | tf_op jit(solution)/shard_map/dot_general | solution.py:29
  172.9 2.6 copy.47
  175.4 0.2 reduce-scatter.11.cloned.1.call-start
  175.7 5.6 %convolution_convert_fusion.1 = bf16[768,768]{1,0:T(8,128)(2,1)} fusion(bf16[2048,768]{1,0:T(8,128)(2,1)S(1)} %copy-done.3, bf16[2048,768]{1,0:T(8,128)(2,1)} %get-tuple-element.65), kind=kOutput, calls=%fused_computation.6 | convolution fusion | flops 2416508928 | bytes 7471104 | tf_op jit(solution)/shard_map/dot_general | solution.py:29
  181.4 1.9 fusion.8
  183.3 0.6 copy.52
  183.9 0.6 reshape.157.bback
  184.5 0.6 dynamic-slice
  185.8 0.2 dynamic-update-slice
  186.0 7.3 %all-reduce = s32[256]{0:T(256)S(1)} all-reduce(s32[256]{0:T(256)S(1)} %dynamic-update-slice), channel_id=1, replica_groups=mesh['dp'=8,'tensor'=4] {'dp'}, use_global_device_ids=true, to_apply=%add | all-reduce | flops 256 | bytes 2048
  193.4 17.8 %reduce-scatter.15.cloned.1.call-done = bf16[96,768]{1,0:T(8,128)(2,1)} async-done(((bf16[768,768]{1,0:T(8,128)(2,1)}), bf16[96,768]{1,0:T(8,128)(2,1)}) %reduce-scatter.15.cloned.1.call-update) | async-done | bytes 147472
  211.2 1.1 copy.48
  212.3 0.9 copy.44
  213.2 38.9 %reduce-scatter.11.cloned.1.call-done = bf16[96,768]{1,0:T(8,128)(2,1)} async-done(((bf16[768,768]{1,0:T(8,128)(2,1)}), bf16[96,768]{1,0:T(8,128)(2,1)}) %reduce-scatter.11.cloned.1.call-update) | async-done | bytes 147472 | tf_op jit(solution)/shard_map/reduce_scatter | solution.py:405
  252.1 1.6 convert_element_type.31
  253.8 83.7 %all-gather.8.cloned.1.call-done = bf16[6144,768]{1,0:T(8,128)(2,1)} async-done(((bf16[192,768]{1,0:T(8,128)(2,1)}), bf16[6144,768]{1,0:T(8,128)(2,1)}) %all-gather.8.cloned.1.call-update) | async-done | bytes 9437200 | tf_op jit(solution)/shard_map/all_gather | solution.py:317
  337.5 49.3 %shard_map.274 = (bf16[2048,768]{1,0:T(8,128)(2,1)}, f32[2048,768]{1,0:T(8,128)}, bf16[2048,768]{1,0:T(8,128)(2,1)}, f32[32,768]{1,0:T(8,128)}) custom-call(s32[4]{0:T(128)} %iota_xor_fusion.slots, bf16[2048,768]{1,0:T(8,128)(2,1)} %get-tuple-element.43.n_two, bf16[2048,768]{1,0:T(8,128)(2,1)} %c.3, f32[2048,768]{1,0:T(8,128)} %get-tuple-element.44.middle, ...), custom_call_target="tpu_custom_call" | custom-call | tf_op jit(solution)/shard_map/pallas_call | solution.py:276
  386.9 3.7 convolution_convert_fusion.2
  390.6 0.3 reduce-scatter.13.cloned.1.call-start
  390.9 33.7 %shard_map.275 = (f32[2048,768]{1,0:T(8,128)}, bf16[2048,192]{1,0:T(8,128)(2,1)}, bf16[2048,192]{1,0:T(8,128)(2,1)}, bf16[2048,192]{1,0:T(8,128)(2,1)}, f32[8,1152]{1,0:T(8,128)}) custom-call(s32[4]{0:T(128)} %iota_xor_fusion.slots, bf16[2048,768]{1,0:T(8,128)(2,1)} %get-tuple-element.48.dml, bf16[2048,1152]{1,0:T(8,128)(2,1)} %get-tuple-element.50.qkv, ...), custom_call_target="tpu_custom_call" | custom-call | tf_op jit(solution)/shard_map/pallas_call | solution.py:276
  424.6 2.1 fusion.2
  426.7 0.8 fusion.3
  427.6 0.4 copy-done.17
  427.9 0.8 fusion.4
  428.8 0.1 pad_maximum_fusion
  428.9 1.3 copy.49
  430.3 36.3 %shard_map.276 = (bf16[2048,768]{1,0:T(8,128)(2,1)}, f32[8,4,768]{2,1,0:T(4,128)}, f32[16,768]{1,0:T(8,128)}) custom-call(s32[4]{0:T(128)} %iota_xor_fusion.slots, bf16[2048,768]{1,0:T(8,128)(2,1)} %tok.5, f32[8,4,768]{2,1,0:T(4,128)} %reshape.167.time, bf16[2048,768]{1,0:T(8,128)(2,1)} %get-tuple-element.48.dml, f32[2048,768]{1,0:T(8,128)} %get-tuple-element.49.dmid, ...), custom_call_target="tpu_custom_call" | custom-call | tf_op jit(solution)/shard_map/pallas_call | solution.py:276
  466.5 0.8 bitcast_reduce_fusion.1
  467.5 23.5 %psum.7 = f32[5760]{0:T(1024)S(1)} all-reduce(f32[5760]{0:T(1024)S(1)} %concatenate.23), channel_id=1, replica_groups=mesh['dp'=8,'tensor'=4] {'dp'}, use_global_device_ids=true, to_apply=%region_5.6 | all-reduce | flops 5760 | bytes 46080 | tf_op jit(solution)/shard_map/psum | solution.py:431
  491.0 0.7 reshape.165
  491.7 0.9 reshape.160
  492.6 0.1 constant_dynamic-slice_fusion
  492.7 9.2 %all_gather.27 = f32[256,192]{1,0:T(8,128)S(1)} all-gather(f32[32,192]{1,0:T(8,128)S(1)} %constant_dynamic-slice_fusion), channel_id=1, replica_groups=mesh['dp'=8,'tensor'=4] {'dp'}, dimensions={0}, use_global_device_ids=true | all-gather | bytes 221184 | tf_op jit(solution)/shard_map/all_gather | solution.py:419
  501.9 0.6 fusion.14
  502.5 2.2 fusion
  504.8 0.8 convert_bitcast_fusion.1
  505.6 0.7 copy.43
  506.3 1.0 copy.50
  507.4 0.9 copy.42
  (74 shorter events, 1.0 us)
Async XLA Ops:
  7.2 21.2 %copy-start = (bf16[2000,192]{0,1:T(8,128)(2,1)S(1)}, bf16[2000,192]{0,1:T(8,128)(2,1)}, u32[]{:S(2)}) copy-start(bf16[2000,192]{0,1:T(8,128)(2,1)} %param.18) | copy-start | bytes 2304004
  7.2 36.5 %copy-start.9 = (f32[768]{0:T(1024)S(1)}, f32[768]{0:T(1024)}, u32[]{:S(2)}) copy-start(f32[768]{0:T(1024)} %param.27) | copy-start | bytes 9220
  7.2 37.1 %copy-start.10 = (f32[768]{0:T(1024)S(1)}, f32[768]{0:T(1024)}, u32[]{:S(2)}) copy-start(f32[768]{0:T(1024)} %param.28) | copy-start | bytes 9220
  7.2 38.2 %copy-start.11 = (f32[768]{0:T(1024)S(1)}, f32[768]{0:T(1024)}, u32[]{:S(2)}) copy-start(f32[768]{0:T(1024)} %param.29) | copy-start | bytes 9220
  7.2 38.8 %copy-start.12 = (f32[768]{0:T(1024)S(1)}, f32[768]{0:T(1024)}, u32[]{:S(2)}) copy-start(f32[768]{0:T(1024)} %param.22) | copy-start | bytes 9220
  7.2 39.4 %copy-start.13 = (f32[768]{0:T(1024)S(1)}, f32[768]{0:T(1024)}, u32[]{:S(2)}) copy-start(f32[768]{0:T(1024)} %param.30) | copy-start | bytes 9220
  7.2 39.9 %copy-start.5 = (bf16[768,768]{1,0:T(8,128)(2,1)S(1)}, bf16[768,768]{1,0:T(8,128)(2,1)}, u32[]{:S(2)}) copy-start(bf16[768,768]{1,0:T(8,128)(2,1)} %param.23) | copy-start | bytes 3538948
  7.3 70.8 %all-gather.6.cloned.1.call-start = ((), (), s32[]{:S(2)}) async-start(), calls=%async_computation.4 | async-start | bytes 4866048 | tf_op jit(solution)/shard_map/all_gather | solution.py:317
  9.1 202.1 %reduce-scatter.15.cloned.1.call-start = ((), (), s32[]{:S(2)}) async-start(), calls=%async_computation.9 | async-start | bytes 1327104
  148.3 18.9 %copy-start.2 = (bf16[2048,768]{1,0:T(8,128)(2,1)S(1)}, bf16[2048,768]{1,0:T(8,128)(2,1)}, u32[]{:S(2)}) copy-start(bf16[2048,768]{1,0:T(8,128)(2,1)} %c.3) | copy-start | bytes 9437188
  172.9 2.8 copy-start.3
  175.4 76.7 %reduce-scatter.11.cloned.1.call-start = ((), (), s32[]{:S(2)}) async-start(), calls=%async_computation.7 | async-start | bytes 1327104 | tf_op jit(solution)/shard_map/reduce_scatter | solution.py:405
  181.3 2.7 copy-start.14
  181.3 3.2 copy-start.19
  181.3 4.5 copy-start.15
  181.3 12.1 %copy-start.8 = (f32[8,768]{1,0:T(8,128)S(1)}, f32[8,768]{1,0:T(8,128)}, u32[]{:S(2)}) copy-start(f32[8,768]{1,0:T(8,128)} %get-tuple-element.62) | copy-start | bytes 73732
  181.3 156.2 %all-gather.8.cloned.1.call-start = ((), (), s32[]{:S(2)}) async-start(), calls=%async_computation.5 | async-start | bytes 9732096 | tf_op jit(solution)/shard_map/all_gather | solution.py:317
  183.3 321.5 %reduce-scatter.9.cloned.1.call-start = ((), (), s32[]{:S(2)}) async-start(), calls=%async_computation.6 | async-start | bytes 442368 | tf_op jit(solution)/shard_map/reduce_scatter | solution.py:405
  337.5 49.4 %copy-start.16 = (bf16[2048,384]{1,0:T(8,128)(2,1)S(1)}, bf16[2048,384]{1,0:T(8,128)(2,1)}, u32[]{:S(2)}) copy-start(bf16[2048,384]{1,0:T(8,128)(2,1)} %get-tuple-element.64) | copy-start | bytes 4718596
  390.6 115.8 %reduce-scatter.13.cloned.1.call-start = ((), (), s32[]{:S(2)}) async-start(), calls=%async_computation.8 | async-start | bytes 1105920
  390.9 33.7 %copy-start.4 = (bf16[2048,768]{1,0:T(8,128)(2,1)S(1)}, bf16[2048,768]{1,0:T(8,128)(2,1)}, u32[]{:S(2)}) copy-start(bf16[2048,768]{1,0:T(8,128)(2,1)} %get-tuple-element.41.n_one) | copy-start | bytes 9437188
  424.6 2.2 copy-start.18
  426.7 1.2 copy-start.17
  430.2 37.1 %copy-start.7 = (f32[8,1152]{1,0:T(8,128)S(1)}, f32[8,1152]{1,0:T(8,128)}, u32[]{:S(2)}) copy-start(f32[8,1152]{1,0:T(8,128)} %get-tuple-element.63) | copy-start | bytes 110596
  430.2 37.2 %copy-start.6 = (f32[32,768]{1,0:T(8,128)S(1)}, f32[32,768]{1,0:T(8,128)}, u32[]{:S(2)}) copy-start(f32[32,768]{1,0:T(8,128)} %get-tuple-element.60) | copy-start | bytes 294916
  430.2 78.0 %copy-start.1 = (bf16[2000,192]{0,1:T(8,128)(2,1)S(1)}, bf16[2000,192]{0,1:T(8,128)(2,1)}, u32[]{:S(2)}) copy-start(bf16[2000,192]{0,1:T(8,128)(2,1)} %param.18) | copy-start | bytes 2304004
Sparse Core Ops, SparseCore 0:
  11.6 66.4 all-gather.5
  175.6 35.5 reduce-scatter.14
  215.4 36.7 reduce-scatter.10
  255.5 82.0 all-gather.7
  390.7 32.5 reduce-scatter.8
  430.3 34.4 reduce-scatter.12

commit v2 on v1

v2 whole, which is shorter than its diff:
```python
import functools

import jax
import jax.numpy as jnp
from jax import lax
from jax.experimental import pallas as pl
from jax.experimental.pallas import tpu as pltpu
from jax.sharding import PartitionSpec as P

HEAD = 64
HEADS = 3
LEN = 64
EPS = 1e-05
BR = 512
VMEM_BYTES = 58 * 1024 * 1024
HIGHEST_PREC = lax.Precision.HIGHEST
F32 = jnp.float32
BF16 = jnp.bfloat16


def dot_nn(a, b):
    return lax.dot_general(a, b, (((1,), (0,)), ((), ())), preferred_element_type=F32)


def dot_nt(a, b):
    return lax.dot_general(a, b, (((1,), (1,)), ((), ())), preferred_element_type=F32)


def dot_tn(a, b):
    return lax.dot_general(a, b, (((0,), (0,)), ((), ())), preferred_element_type=F32)


def params():
    return pltpu.CompilerParams(
        dimension_semantics=("arbitrary",), vmem_limit_bytes=VMEM_BYTES
    )


def rows_spec(width, rows=BR):
    return pl.BlockSpec((rows, width), lambda i, *_: (i, 0))


def whole_spec(shape):
    return pl.BlockSpec(shape, lambda i, *_: (0,) * len(shape))


def slot_spec(shape, k):
    return pl.BlockSpec((1,) + shape, lambda i, s: (s[k],) + (0,) * len(shape))


def normed(x):
    mean = jnp.mean(x, axis=-1, keepdims=True)
    centred = x - mean
    spread = jnp.mean(centred * centred, axis=-1, keepdims=True)
    inv = lax.rsqrt(spread + EPS)
    return centred * inv, inv


def norm_back(d_out, gain, xhat, inv):
    gy = d_out * gain
    m1 = jnp.mean(gy, axis=-1, keepdims=True)
    m2 = jnp.mean(gy * xhat, axis=-1, keepdims=True)
    return inv * (gy - m1 - xhat * m2)


def fold8(x):
    return jnp.sum(x.reshape(x.shape[0] // 8, 8, x.shape[1]), axis=0)


def entry_of(tok_ref, time_ref):
    tok = tok_ref[...].astype(F32)
    n = tok.shape[0] // LEN
    return (tok.reshape(n, LEN, tok.shape[1]) + time_ref[...][:, None, :]).reshape(tok.shape)


def half_masks():
    lane = lax.broadcasted_iota(jnp.int32, (LEN, 2 * HEAD), 1)
    low = (lane < HEAD).astype(F32)
    return low.astype(BF16), (1.0 - low).astype(BF16), lane < HEAD


def block_diag(x, mlo, mhi):
    return jnp.concatenate([x * mlo, x * mhi], axis=0)


def load_own(att, wqkv, wo):
    hc = HEADS * HEAD
    width = wo.shape[0]
    wqkv[...] = jnp.zeros_like(wqkv)
    wo[...] = jnp.zeros_like(wo)
    for t in range(3):
        wqkv[t * width : t * width + hc, :] = att[t * hc : (t + 1) * hc, :]
    wo[:hc, :] = att[3 * hc :, :]


def load_rest(core, mine, other, wqkv, wo):
    hc = HEADS * HEAD
    n = hc // 2
    width = wo.shape[0]
    wqkv[...] = jnp.zeros_like(wqkv)
    wo[...] = jnp.zeros_like(wo)
    for s in range(3):
        for src, at in ((mine, core * n), (other, (1 - core) * n)):
            for t in range(3):
                wqkv[pl.ds(pl.multiple_of(t * width + s * hc + at, 16), n), :] = src[t, s]
            wo[pl.ds(pl.multiple_of(s * hc + at, 16), n), :] = src[3, s]


def tile_list(rows, width):
    return [(s, j) for s in range(rows // LEN) for j in range(width // 128)]


def tile(ref, st, part=0, width=0):
    s, j = st
    return ref[s * LEN : (s + 1) * LEN, part * width + j * 128 : part * width + (j + 1) * 128]


def put_tile(ref, st, value, part=0, width=0):
    s, j = st
    ref[s * LEN : (s + 1) * LEN, part * width + j * 128 : part * width + (j + 1) * 128] = (
        value.astype(BF16)
    )


def attend(n_one, wqkv, wo, bias, qkv_ref, p_ref, mix_ref):
    width = wo.shape[0]
    qkv_ref[...] = (dot_nt(n_one, wqkv[...]) + bias).astype(BF16)
    mlo, mhi, low = half_masks()
    tiles = tile_list(n_one.shape[0], width)
    scores = [
        dot_nt(tile(qkv_ref, t, 1, width), block_diag(tile(qkv_ref, t, 0, width), mlo, mhi))
        for t in tiles
    ]
    probs = []
    for t, sc in zip(tiles, scores):
        top = jnp.max(sc, axis=0, keepdims=True)
        e = jnp.exp((sc - top) * (HEAD**-0.5))
        p = (e * (1.0 / jnp.sum(e, axis=0, keepdims=True))).astype(BF16)
        probs.append(p)
        put_tile(p_ref, t, p)
    both = [dot_tn(p, tile(qkv_ref, t, 2, width)) for t, p in zip(tiles, probs)]
    for t, r in zip(tiles, both):
        put_tile(mix_ref, t, jnp.where(low, r[:LEN], r[LEN:]))
    return dot_nn(mix_ref[...], wo[...])


def attend_own(
    tok, time, vecs, own, n_one_ref, qkv_ref, p_ref, mix_ref, part_ref, wqkv, wo,
):
    @pl.when(pl.program_id(0) == 0)
    def _():
        load_own(own, wqkv, wo)

    xhat, _ = normed(entry_of(tok, time))
    n_one = (xhat * vecs[0:1, :] + vecs[1:2, :]).astype(BF16)
    n_one_ref[...] = n_one
    part_ref[...] = attend(n_one, wqkv, wo, vecs[7:8, :], qkv_ref, p_ref, mix_ref)


def attend_rest(
    core, tok, time, n_one, part, vecs, mine, other, bias,
    qkv_ref, p_ref, middle_ref, n_two_ref, wqkv, wo, mix_ref,
):
    @pl.when(pl.program_id(0) == 0)
    def _():
        load_rest(core[0], mine, other, wqkv, wo)

    more = attend(n_one[...], wqkv, wo, bias[...], qkv_ref, p_ref, mix_ref)
    middle = entry_of(tok, time) + part[...] + more + vecs[4:5, :]
    middle_ref[...] = middle
    xhat, _ = normed(middle)
    n_two_ref[...] = (xhat * vecs[2:3, :] + vecs[3:4, :]).astype(BF16)


ERF_P = 0.3275911
ERF_A = (0.254829592, -0.284496736, 1.421413741, -1.453152027, 1.061405429)


def gelu_both(x):
    bell = jnp.exp(x * x * (-0.5))
    t = 1.0 / (1.0 + jnp.abs(x) * (ERF_P * 0.5**0.5))
    poly = t * (
        0.5 * ERF_A[0]
        + t * (0.5 * ERF_A[1] + t * (0.5 * ERF_A[2] + t * (0.5 * ERF_A[3] + t * (0.5 * ERF_A[4]))))
    )
    tail = poly * bell
    cdf = jnp.where(x >= 0, 1.0 - tail, tail)
    return x * cdf, cdf + x * bell * 0.3989422804014327


def mlp_slot(n_two, c, wi, wb, b):
    pre = dot_nt(n_two, wi) + b
    d_act = dot_nt(c, wb)
    act, slope = gelu_both(pre)
    act = act.astype(BF16)
    d_pre = (d_act * slope).astype(BF16)
    return act, d_pre


def mlp_own(n_two, c, wi, wb, vecs, out_ref, dn2_ref, grad_ref, gbin_ref, acc, sums):
    hid = wi.shape[0]

    @pl.when(pl.program_id(0) == 0)
    def _():
        acc[...] = jnp.zeros_like(acc)
        sums[...] = jnp.zeros_like(sums)

    act, d_pre = mlp_slot(n_two[...], c[...], wi[...], wb[...], vecs[6:7, :])
    sums[...] += fold8(d_pre.astype(F32))
    out_ref[...] = dot_nn(act, wb[...])
    dn2_ref[...] = dot_nn(d_pre, wi[...])
    acc[:, :hid] += dot_tn(n_two[...], d_pre)
    acc[:, hid:] += dot_tn(c[...], act)

    @pl.when(pl.program_id(0) == pl.num_programs(0) - 1)
    def _():
        grad_ref[...] = acc[...].astype(BF16)
        gbin_ref[...] = jnp.sum(sums[...], axis=0, keepdims=True)


def mlp_rest(
    slots, n_two, c, middle, out_in, dn2_in, vecs, w1, w2, w3, b,
    out_ref, dmid_ref, dml_ref, sums_ref, sums,
):
    hid = b.shape[-1]
    out = out_in[...]
    dn2 = dn2_in[...]
    for k, w in enumerate((w1, w2, w3)):
        wi = w[0, :hid, :]
        wb = w[0, hid:, :]
        act, d_pre = mlp_slot(n_two[...], c[...], wi, wb, b[k : k + 1, :])
        out = out + dot_nn(act, wb)
        dn2 = dn2 + dot_nn(d_pre, wi)
    mid = middle[...]
    cot = c[...].astype(F32)
    out_ref[...] = (mid + out + vecs[5:6, :]).astype(BF16)
    xhat, inv = normed(mid)
    d_mid = cot + norm_back(dn2, vecs[2:3, :], xhat, inv)
    dmid_ref[...] = d_mid
    dml_ref[...] = d_mid.astype(BF16)
    add_sums(sums, sums_ref, (dn2 * xhat, dn2, d_mid, cot))


def add_sums(sums, sums_ref, terms):
    @pl.when(pl.program_id(0) == 0)
    def _():
        sums[...] = jnp.zeros_like(sums)

    for k, term in enumerate(terms):
        sums[8 * k : 8 * k + 8, :] += fold8(term)

    @pl.when(pl.program_id(0) == pl.num_programs(0) - 1)
    def _():
        for k in range(len(terms)):
            sums_ref[k : k + 1, :] = jnp.sum(sums[8 * k : 8 * k + 8, :], axis=0, keepdims=True)


def attend_back(dml, qkv, p, wqkv, wo, dqkv, dmix):
    width = wo.shape[0]
    scale = HEAD**-0.5
    dmix[...] = dot_nt(dml, wo[...]).astype(BF16)
    mlo, mhi, low = half_masks()
    tiles = tile_list(dml.shape[0], width)
    d_outs = [block_diag(tile(dmix, t), mlo, mhi) for t in tiles]
    d_ps = [dot_nt(tile(qkv, t, 2, width), d) for t, d in zip(tiles, d_outs)]
    for t, d in zip(tiles, d_outs):
        put_tile(dqkv, t, dot_nn(tile(p, t), d), 2, width)
    d_ss = []
    for t, d_p in zip(tiles, d_ps):
        pf = tile(p, t).astype(F32)
        g = pf * d_p
        d_ss.append((g - pf * jnp.sum(g, axis=0, keepdims=True)).astype(BF16))
    for t, d_s in zip(tiles, d_ss):
        put_tile(
            dqkv, t, dot_nn(d_s, block_diag(tile(qkv, t, 0, width), mlo, mhi)) * scale, 1, width
        )
    both = [dot_tn(d_s, tile(qkv, t, 1, width)) for t, d_s in zip(tiles, d_ss)]
    for t, r in zip(tiles, both):
        put_tile(dqkv, t, jnp.where(low, r[:LEN], r[LEN:]) * scale)
    return dot_nn(dqkv[...], wqkv[...])


def back_own(
    dml, n_one, mix, qkv, p, own, dn1_ref, grad_ref, sums_ref,
    wqkv, wo, dqkv, dmix, acc, acc_out, sums,
):
    @pl.when(pl.program_id(0) == 0)
    def _():
        load_own(own, wqkv, wo)
        acc[...] = jnp.zeros_like(acc)
        acc_out[...] = jnp.zeros_like(acc_out)

    dn1_ref[...] = attend_back(dml[...], qkv, p, wqkv, wo, dqkv, dmix)
    acc[...] += dot_tn(n_one[...], dqkv[...])
    acc_out[...] += dot_tn(dml[...], mix[...])
    add_sums(sums, sums_ref, (dqkv[...].astype(F32),))

    @pl.when(pl.program_id(0) == pl.num_programs(0) - 1)
    def _():
        hc = HEADS * HEAD
        width = wo.shape[0]
        for t in range(3):
            grad_ref[:, t * hc : (t + 1) * hc] = acc[:, t * width : t * width + hc].astype(BF16)
        grad_ref[:, 3 * hc :] = acc_out[:, :hc].astype(BF16)


def back_rest(
    core, tok, time, dml, dmid, dn1, vecs, qkv, p, mine, other,
    gtok_ref, sent_ref, sums_ref, wqkv, wo, dqkv, dmix, sums,
):
    @pl.when(pl.program_id(0) == 0)
    def _():
        load_rest(core[0], mine, other, wqkv, wo)

    d_n = dn1[...] + attend_back(dml[...], qkv, p, wqkv, wo, dqkv, dmix)
    xhat, inv = normed(entry_of(tok, time))
    d_entry = dmid[...] + norm_back(d_n, vecs[0:1, :], xhat, inv)
    gtok_ref[...] = d_entry.astype(BF16)
    sent_ref[...] = jnp.sum(d_entry.reshape(d_entry.shape[0] // LEN, LEN, -1), axis=1)
    add_sums(sums, sums_ref, (d_n * xhat, d_n))


def call(kernel, grid, in_specs, out_specs, out_shape, scratch, slots, args):
    if slots is None:
        return pl.pallas_call(
            kernel, grid=grid, in_specs=in_specs, out_specs=out_specs, out_shape=out_shape,
            scratch_shapes=scratch, compiler_params=params(),
        )(*args)
    return pl.pallas_call(
        kernel,
        grid_spec=pltpu.PrefetchScalarGridSpec(
            num_scalar_prefetch=1, grid=grid, in_specs=in_specs, out_specs=out_specs,
            scratch_shapes=scratch,
        ),
        out_shape=out_shape,
        compiler_params=params(),
    )(slots, *args)


def body(
    tokens, timesteps, time_table, w_qkv, b_qv, w_out, b_out, w_in, b_in, w_back, b_back,
    gain_one, shift_one, gain_two, shift_two, cotangent,
):
    sentences = timesteps.shape[0]
    rows, dim = tokens.shape
    hc = w_out.shape[0]
    hid = w_back.shape[0]
    table_cols = time_table.shape[1]
    n_tensor = dim // hc
    me = lax.axis_index("tensor")
    part = lax.axis_index("dp")
    dp = lax.axis_size("dp")
    order = (me ^ jnp.arange(n_tensor, dtype=jnp.int32)).astype(jnp.int32)
    fast = dp == 8 and n_tensor == 4
    sds = jax.ShapeDtypeStruct

    att_own = jnp.concatenate(
        [jnp.transpose(w_qkv, (1, 2, 0)).reshape(3 * hc, dim), w_out], axis=0
    )
    n_att = att_own.shape[0] // dp
    att_piece = lax.dynamic_slice_in_dim(att_own, part * n_att, n_att, 0)
    if fast:
        core = (part % 2).astype(jnp.int32).reshape(1)
        mine, other = spread(att_piece)
    else:
        core = jnp.zeros((1,), jnp.int32)
        mine, other = spread_any(att_piece, order, dp)
    wi_own = w_in.T
    mlp_shard = jnp.concatenate([wi_own, w_back], axis=0)
    n_mlp = mlp_shard.shape[0] // dp
    mlp_all = lax.all_gather(
        lax.dynamic_slice_in_dim(mlp_shard, part * n_mlp, n_mlp, 0),
        ("tensor", "dp"), axis=0, tiled=True,
    ).reshape(n_tensor, mlp_shard.shape[0], dim)

    steps_iota = lax.broadcasted_iota(jnp.int32, (sentences, time_table.shape[0]), 1)
    picked = timesteps[:, None] == steps_iota
    own_rows = jnp.dot(picked.astype(BF16), time_table, preferred_element_type=F32)
    bias_count = 2 + hid // hc
    shared = lax.all_gather(
        jnp.concatenate(
            [own_rows, b_qv, b_in.reshape(-1, hc), jnp.zeros((-bias_count % 8, hc), F32)]
        ),
        "tensor", axis=0,
    )
    time_rows = jnp.transpose(shared[:, :sentences], (1, 0, 2)).reshape(sentences, dim)
    biases = picked_rows(shared[:, sentences:], order[1:])
    wide = 128 * (-(-3 * hc // 128))
    pad = jnp.zeros((wide - 3 * hc,), F32)
    bias_rest = jnp.concatenate(
        [biases[:, 0].reshape(-1), pad, jnp.zeros((wide,), F32), biases[:, 1].reshape(-1), pad]
    ).reshape(1, 3 * wide)
    bi_rest = biases[:, 2:bias_count].reshape(3, hid)
    thin = 128 * (-(-hc // 128))
    gap = jnp.zeros((thin - hc,), F32)
    bias_own = jnp.concatenate([b_qv[0], gap, jnp.zeros((thin,), F32), b_qv[1], gap])
    vecs = jnp.stack(
        [gain_one, shift_one, gain_two, shift_two, b_out, b_back, b_in, bias_own]
    )

    nb = rows // BR
    grid = (nb,)
    time_spec = rows_spec(dim, BR // LEN)
    vec = whole_spec((8, dim))
    own_spec = whole_spec((4 * hc, dim))
    piece_spec = whole_spec(mine.shape)
    own_scr = [pltpu.VMEM((3 * thin, dim), BF16), pltpu.VMEM((thin, dim), BF16)]
    rest_scr = [pltpu.VMEM((3 * wide, dim), BF16), pltpu.VMEM((wide, dim), BF16)]

    n_one, qkv_a, p_a, mix_a, attn_part = call(
        attend_own, grid,
        [rows_spec(dim), time_spec, vec, own_spec],
        [rows_spec(dim), rows_spec(3 * thin), rows_spec(thin), rows_spec(thin), rows_spec(dim)],
        [sds((rows, dim), BF16), sds((rows, 3 * thin), BF16), sds((rows, thin), BF16),
         sds((rows, thin), BF16), sds((rows, dim), F32)],
        own_scr, None,
        (tokens, time_rows, vecs, att_own),
    )
    qkv_b, p_b, middle, n_two = call(
        attend_rest, grid,
        [rows_spec(dim), time_spec, rows_spec(dim), rows_spec(dim), vec, piece_spec, piece_spec,
         whole_spec((1, 3 * wide))],
        [rows_spec(3 * wide), rows_spec(wide), rows_spec(dim), rows_spec(dim)],
        [sds((rows, 3 * wide), BF16), sds((rows, wide), BF16), sds((rows, dim), F32),
         sds((rows, dim), BF16)],
        rest_scr + [pltpu.VMEM((BR, wide), BF16)], core,
        (tokens, time_rows, n_one, attn_part, vecs, mine, other, bias_rest),
    )
    out_acc, dn2_acc, mlp_grads, gbin = call(
        mlp_own, grid,
        [rows_spec(dim), rows_spec(dim), whole_spec((hid, dim)), whole_spec((hid, dim)), vec],
        [rows_spec(dim), rows_spec(dim), whole_spec((dim, 2 * hid)), whole_spec((1, hid))],
        [sds((rows, dim), F32), sds((rows, dim), F32), sds((dim, 2 * hid), BF16),
         sds((1, hid), F32)],
        [pltpu.VMEM((dim, 2 * hid), F32), pltpu.VMEM((8, hid), F32)], None,
        (n_two, cotangent, wi_own, w_back, vecs),
    )

    def scattered(grad):
        return lax.psum_scatter(grad, "dp", scatter_dimension=0, tiled=True).astype(F32)

    mlp_grads = scattered(mlp_grads)
    mlp_spec = lambda k: slot_spec((2 * hid, dim), k)
    output, d_mid, d_mid_low, sums_two = call(
        mlp_rest, grid,
        [rows_spec(dim), rows_spec(dim), rows_spec(dim), rows_spec(dim), rows_spec(dim), vec,
         mlp_spec(1), mlp_spec(2), mlp_spec(3), whole_spec((3, hid))],
        [rows_spec(dim), rows_spec(dim), rows_spec(dim), whole_spec((4, dim))],
        [sds((rows, dim), BF16), sds((rows, dim), F32), sds((rows, dim), BF16),
         sds((4, dim), F32)],
        [pltpu.VMEM((32, dim), F32)], order,
        (n_two, cotangent, middle, out_acc, dn2_acc, vecs, mlp_all, mlp_all, mlp_all, bi_rest),
    )
    back = lambda w: [pltpu.VMEM((BR, 3 * w), BF16), pltpu.VMEM((BR, w), BF16)]
    dn1_acc, att_grads, sums_qkv = call(
        back_own, grid,
        [rows_spec(dim), rows_spec(dim), rows_spec(thin), rows_spec(3 * thin), rows_spec(thin),
         own_spec],
        [rows_spec(dim), whole_spec((dim, 4 * hc)), whole_spec((1, 3 * thin))],
        [sds((rows, dim), F32), sds((dim, 4 * hc), BF16), sds((1, 3 * thin), F32)],
        own_scr + back(thin)
        + [pltpu.VMEM((dim, 3 * thin), F32), pltpu.VMEM((dim, thin), F32),
           pltpu.VMEM((8, 3 * thin), F32)],
        None,
        (d_mid_low, n_one, mix_a, qkv_a, p_a, att_own),
    )
    att_grads = scattered(att_grads)
    grad_tokens, per_sentence, sums_one = call(
        back_rest, grid,
        [rows_spec(dim), time_spec, rows_spec(dim), rows_spec(dim), rows_spec(dim), vec,
         rows_spec(3 * wide), rows_spec(wide), piece_spec, piece_spec],
        [rows_spec(dim), time_spec, whole_spec((2, dim))],
        [sds((rows, dim), BF16), sds((sentences, dim), F32), sds((2, dim), F32)],
        rest_scr + back(wide) + [pltpu.VMEM((16, dim), F32)], core,
        (tokens, time_rows, d_mid_low, d_mid, dn1_acc, vecs, qkv_b, p_b, mine, other),
    )
    grad_win = mlp_grads[:, :hid]
    grad_wback = mlp_grads[:, hid:].T
    grad_wqkv = att_grads[:, : 3 * hc].reshape(-1, 3, hc)
    grad_wout = att_grads[:, 3 * hc :].T

    bias_row = jnp.concatenate(
        [sums_qkv[:, :thin], timesteps.astype(F32).reshape(1, -1),
         sums_qkv[:, thin + sentences :]], axis=1
    )
    terms = jnp.concatenate([per_sentence, sums_two, sums_one, gbin, bias_row], axis=0)
    terms = lax.all_gather(terms, "dp", axis=0)
    all_cols = lax.dynamic_slice_in_dim(
        terms[:, :sentences], me * table_cols, table_cols, 2
    ).reshape(-1, table_cols)
    small = jnp.sum(terms[:, sentences:], axis=0)
    all_steps = terms[:, -1, thin : thin + sentences].astype(jnp.int32).reshape(-1)
    all_picked = all_steps[:, None] == lax.broadcasted_iota(
        jnp.int32, (all_steps.shape[0], time_table.shape[0]), 1
    )
    grad_table = lax.dot_general(
        all_picked.astype(F32), all_cols, (((0,), (0,)), ((), ())),
        precision=HIGHEST_PREC, preferred_element_type=F32,
    )
    grad_bqv = jnp.stack([small[7, :hc], small[7, 2 * thin : 2 * thin + hc]])
    return (
        output, grad_tokens, grad_table, grad_wqkv, grad_bqv, grad_wout, small[2], grad_win,
        small[6], grad_wback, small[3], small[4], small[5], small[0], small[1],
    )


def picked_rows(array, order):
    return jnp.concatenate(
        [lax.dynamic_slice_in_dim(array, order[k], 1, 0) for k in range(order.shape[0])]
    )


def flipped(n, bits):
    return [(i, i ^ bits) for i in range(n)]


def spread(piece):
    slots = jnp.stack([lax.ppermute(piece, "tensor", flipped(4, k)) for k in (1, 2, 3)])
    whole = jnp.broadcast_to(slots[None], (4,) + slots.shape)
    mine = lax.all_to_all(
        whole, "dp", 0, 0, tiled=True, axis_index_groups=[[0, 2, 4, 6], [1, 3, 5, 7]]
    )
    return mine, lax.ppermute(mine, "dp", flipped(8, 1))


def spread_any(piece, order, dp):
    shards = lax.all_gather(piece, ("tensor", "dp"), axis=0, tiled=True)
    n_tensor = order.shape[0]
    rows = piece.shape[0] * dp
    shards = picked_rows(shards.reshape(n_tensor, rows, -1), order[1:])
    shards = shards.reshape(n_tensor - 1, 4, 2, rows // 8, -1)
    return tuple(jnp.transpose(shards[:, :, c], (1, 0, 2, 3)) for c in (0, 1))


def solution(mesh):
    return jax.shard_map(
        body,
        mesh=mesh,
        in_specs=(
            P("dp", None), P("dp"), P(None, "tensor"), P(None, None, "tensor"), P(None, "tensor"),
            P("tensor", None), P(), P(None, "tensor"), P("tensor"), P("tensor", None), P(), P(),
            P(), P(), P(), P("dp", None),
        ),
        out_specs=(
            P("dp", None), P("dp", None), P(None, "tensor"), P("dp", None, "tensor"),
            P(None, "tensor"), P("tensor", "dp"), P(), P("dp", "tensor"), P("tensor"),
            P("tensor", "dp"), P(), P(), P(), P(), P(),
        ),
        check_vma=False,
    )
```

time: 516 us -> 278 us (0.54)
  waiting for transfers between devices: 170 us -> 13.8 us
  Pallas kernels: 208 us -> 153 us
  matrix products: 22 us -> 2.6 us
  local copies, waits for them, and re-layouts: 22.7 us -> 13.8 us
  blocking collectives: 68.2 us -> 60 us
  between operations: 15.1 us -> 21.8 us
  starting transfers between devices: 0.65 us -> 5.99 us
    all_gather x2 -> x1, waiting for transfers between devices: 113 us -> 0.01 us  [body(): lax.all_gather(lax.dynamic_slice_in_dim(mlp_shard, part * n_mlp, n_mlp, 0...]
    pallas_call x5 -> x3, Pallas kernels: 190 us -> 101 us  [call(): pl.pallas_call(kernel, grid_spec=pltpu.PrefetchScalarGridSpec(num_scalar_...]
    reduce_scatter x2, waiting for transfers between devices: 38.9 us -> 0.03 us  [scattered(): lax.psum_scatter(grad, 'dp', scatter_dimension=0, tiled=True).astype(F32)]
    pallas_call x1 -> x3, Pallas kernels: 18.9 us -> 52.2 us  [call(): pl.pallas_call(kernel, grid=grid, in_specs=in_specs, out_specs=out_specs,...]
    all_to_all x0 -> x1, blocking collectives: none -> 28.5 us  [spread(): lax.all_to_all(whole, 'dp', 0, 0, tiled=True, axis_index_groups=[[0, 2, 4...]
    psum x1 -> x0, blocking collectives: 23.5 us -> none  [body(): lax.psum(jnp.concatenate([sums_two.reshape(-1), sums_one.reshape(-1), jnp...]
    dot_general x6 -> x0, matrix products: 18.7 us -> none  [dot_tn(): lax.dot_general(a, b, (((0,), (0,)), ((), ())), preferred_element_type=F32)]
    unnamed x8 -> x3, waiting for transfers between devices: 17.9 us -> 0.05 us
  transfers between devices with their start and end apart: 6 -> 7, of which waited for: 4 -> 2; matrix products, arithmetic and copies ran while one was open for 7% -> 6% of each run, Pallas kernels for 14% -> 55%
where the time goes in v2:
time: 278 us
  Pallas kernels  153 us (55%)
  blocking collectives  60 us (22%)
  between operations  21.8 us (8%)
  local copies, waits for them, and re-layouts  13.8 us (5%)
  waiting for transfers between devices  13.8 us (5%)
  other arithmetic  6.93 us (2%)
  starting transfers between devices  5.99 us (2%)
    pallas_call x3, Pallas kernels, call(): pl.pallas_call(kernel, grid_spec=pltpu.PrefetchScalarGridSpec(num_scalar_...  101 us
    pallas_call x3, Pallas kernels, call(): pl.pallas_call(kernel, grid=grid, in_specs=in_specs, out_specs=out_specs,...  52.2 us
    all_to_all x1, blocking collectives, spread(): lax.all_to_all(whole, 'dp', 0, 0, tiled=True, axis_index_groups=[[0, 2, 4...  28.5 us
    all_gather x1, blocking collectives, body(): lax.all_gather(jnp.concatenate([own_rows, b_qv, b_in.reshape(-1, hc), jnp...  21.1 us
    ppermute x3, waiting for transfers between devices, spread(): lax.ppermute(piece, 'tensor', flipped(4, k))  13.7 us
    all_gather x1, blocking collectives, body(): terms = lax.all_gather(terms, 'dp', axis=0)  10.4 us
    ppermute x3, starting transfers between devices, spread(): lax.ppermute(piece, 'tensor', flipped(4, k))  5.68 us
  transfers between devices with their start and end apart: 7, of which 2 were waited for; matrix products, arithmetic and copies ran while one was open for 6% of the time, Pallas kernels for 55%

profile of v2, /device:TPU:0, one launch (start us, length us, event | category | flops | bytes accessed | tf_op | source)
XLA Modules:
  0.0 277.9 jit_solution(5736601846829011967)
XLA Ops:
  8.0 0.0 copy-start
  8.0 0.0 all-gather.4.cloned.1.call-start
  8.1 1.7 copy.36
  9.8 0.0 copy-start.3
  9.8 1.1 fusion.2
  10.9 0.0 all-gather.4.cloned.1.call-update
  11.0 0.0 reduce-scatter.5.cloned.1.call-start
  11.0 1.0 fusion.4
  12.0 3.1 %collective-permute-start = (bf16[96,768]{1,0:T(8,128)(2,1)S(1)}, bf16[96,768]{1,0:T(8,128)(2,1)S(1)}, u32[]{:S(2)}, u32[]{:S(2)}) collective-permute-start(bf16[96,768]{1,0:T(8,128)(2,1)S(1)} %fusion.4), channel_id=1, source_target_pairs={{0,1},{1,0},{2,3},{3,2},{4,5},{5,4},{6,7},{7,6},{8,9},{9,8},{10,11... | collective-permute-start | bytes 442376 | tf_op jit(solution)/shard_map/ppermute | solution.py:518
  15.1 2.6 collective-permute-start.1
  17.7 3.3 %collective-permute-done = bf16[96,768]{1,0:T(8,128)(2,1)S(1)} collective-permute-done((bf16[96,768]{1,0:T(8,128)(2,1)S(1)}, bf16[96,768]{1,0:T(8,128)(2,1)S(1)}, u32[]{:S(2)}, u32[]{:S(2)}) %collective-permute-start) | collective-permute-done | bytes 147488 | tf_op jit(solution)/shard_map/ppermute | solution.py:518
  21.0 10.4 %collective-permute-done.1 = bf16[96,768]{1,0:T(8,128)(2,1)S(1)} collective-permute-done((bf16[96,768]{1,0:T(8,128)(2,1)S(1)}, bf16[96,768]{1,0:T(8,128)(2,1)S(1)}, u32[]{:S(2)}, u32[]{:S(2)}) %collective-permute-start.1) | collective-permute-done | bytes 147488 | tf_op jit(solution)/shard_map/ppermute | solution.py:518
  31.4 0.1 pad_maximum_fusion.1
  31.5 0.0 copy-start.7
  31.5 0.2 broadcast_in_dim.18
  31.7 0.0 copy-start.11
  31.7 0.0 copy-start.12
  31.7 0.0 copy-start.15
  31.7 28.5 %all_to_all.5.mine = bf16[4,3,96,768]{3,2,1,0:T(8,128)(2,1)S(1)} all-to-all(bf16[4,3,96,768]{3,2,1,0:T(8,128)(2,1)S(1)} %broadcast_in_dim.18), channel_id=1, replica_groups={{0,8,16,24},{4,12,20,28},{1,9,17,25},{5,13,21,29},{2,10,18,26},{6,14,22..., dimensions={0} | all-to-all | bytes 3538944 | tf_op jit(solution)/shard_map/all_to_all | solution.py:520
  60.3 0.7 fusion.9
  64.9 0.1 reshape.69
  65.0 0.1 pad.18.clone
  65.1 0.4 fusion.3
  65.5 0.1 maximum_maximum_fusion
  65.5 21.1 %all-gather = f32[160,192]{1,0:T(8,128)S(1)} all-gather(f32[40,192]{1,0:T(8,128)S(1)} %maximum_maximum_fusion), channel_id=2, replica_groups=mesh['dp'=8,'tensor'=4] {'tensor'}, dimensions={0}, use_global_device_ids=true | all-gather | bytes 153600 | tf_op jit(solution)/shard_map/all_gather | solution.py:380
  88.7 0.1 reshape_squeeze.6
  88.8 0.1 reshape_squeeze.7
  88.8 0.1 concatenate.28
  88.9 0.6 reshape.72.bias
  89.5 0.1 concatenate.25
  89.7 0.1 copy.42
  89.8 0.8 reshape.70.time
  90.6 0.7 stack.50.vecs
  91.2 2.1 pad_maximum_fusion.own
  93.3 11.0 %shard_map.271 = (bf16[2048,768]{1,0:T(8,128)(2,1)}, bf16[2048,768]{1,0:T(8,128)(2,1)}, bf16[2048,256]{1,0:T(8,128)(2,1)}, bf16[2048,256]{1,0:T(8,128)(2,1)}, f32[2048,768]{1,0:T(8,128)}) custom-call(bf16[2048,768]{1,0:T(8,128)(2,1)} %tok.5, f32[32,768]{1,0:T(8,128)} %reshape.70.time, f32[8,768]{1,0:T(8,128)} %stack.50.vecs, ...), custom_call_target="tpu_custom_call" | custom-call | tf_op jit(solution)/shard_map/pallas_call | solution.py:325
  104.3 22.0 %shard_map.272 = (bf16[2048,1920]{1,0:T(8,128)(2,1)}, bf16[2048,640]{1,0:T(8,128)(2,1)}, f32[2048,768]{1,0:T(8,128)}, bf16[2048,768]{1,0:T(8,128)(2,1)}) custom-call(s32[1]{0:T(128)} %bitcast.core, bf16[2048,768]{1,0:T(8,128)(2,1)} %tok.5, f32[32,768]{1,0:T(8,128)} %reshape.70.time, bf16[2048,768]{1,0:T(8,128)(2,1)} %get-tuple-element.38.n_one, ...), custom_call_target="tpu_custom_call" | custom-call | tf_op jit(solution)/shard_map/pallas_call | solution.py:329
  126.3 23.4 %shard_map.273 = (f32[2048,768]{1,0:T(8,128)}, f32[2048,768]{1,0:T(8,128)}, bf16[768,1536]{1,0:T(8,128)(2,1)}, f32[1,768]{1,0:T(1,128)}) custom-call(bf16[2048,768]{1,0:T(8,128)(2,1)} %get-tuple-element.40.n_two, bf16[2048,768]{1,0:T(8,128)(2,1)} %c.3, bf16[768,768]{1,0:T(8,128)(2,1)} %bitcast.33, bf16[768,768]{1,0:T(8,128)(2,1)} %wb.1, f32[8,768]{1,0:T(8,128)} %stack.50.vecs), custom_call_target="tpu_custom_call" | custom-call | tf_op jit(solution)/shard_map/pallas_call | solution.py:325
  149.8 0.0 reduce-scatter.5.cloned.1.call-update
  149.8 0.2 reduce-scatter.3.cloned.1.call-start
  150.1 0.7 reshape.74.b
  150.8 48.8 %shard_map.274 = (bf16[2048,768]{1,0:T(8,128)(2,1)}, f32[2048,768]{1,0:T(8,128)}, bf16[2048,768]{1,0:T(8,128)(2,1)}, f32[4,768]{1,0:T(4,128)}) custom-call(s32[4]{0:T(128)} %copy-done.9, bf16[2048,768]{1,0:T(8,128)(2,1)} %get-tuple-element.40.n_two, bf16[2048,768]{1,0:T(8,128)(2,1)} %c.3, f32[2048,768]{1,0:T(8,128)} %get-tuple-element.41.middle, ...), custom_call_target="tpu_custom_call" | custom-call | tf_op jit(solution)/shard_map/pallas_call | solution.py:329
  199.5 17.8 %shard_map.275 = (f32[2048,768]{1,0:T(8,128)}, bf16[768,768]{1,0:T(8,128)(2,1)}, f32[1,768]{1,0:T(1,128)}) custom-call(bf16[2048,768]{1,0:T(8,128)(2,1)} %get-tuple-element.45.dml, bf16[2048,768]{1,0:T(8,128)(2,1)} %get-tuple-element.38.n_one, bf16[2048,256]{1,0:T(8,128)(2,1)} %get-tuple-element.47.mix, bf16[2048,768]{1,0:T(8,128)(2,1)} %get-tuple-element.48.qkv, ...), custom_call_target="tpu_custom_call" | custom-call | tf_op jit(solution)/shard_map/pallas_call | solution.py:325
  217.3 0.0 reduce-scatter.3.cloned.1.call-update
  217.3 0.0 reduce-scatter.5.cloned.1.call-done
  217.4 1.0 convert_element_type.25
  218.4 1.6 slice.126
  220.0 0.7 slice_bitcast_fusion
  220.8 0.1 slice.99
  220.8 30.0 %shard_map.276 = (bf16[2048,768]{1,0:T(8,128)(2,1)}, f32[32,768]{1,0:T(8,128)}, f32[2,768]{1,0:T(2,128)}) custom-call(s32[1]{0:T(128)} %bitcast.core, bf16[2048,768]{1,0:T(8,128)(2,1)} %tok.5, f32[32,768]{1,0:T(8,128)} %reshape.70.time, bf16[2048,768]{1,0:T(8,128)(2,1)} %get-tuple-element.45.dml, f32[2048,768]{1,0:T(8,128)} %get-tuple-element.46.dmid, ...), custom_call_target="tpu_custom_call" | custom-call | tf_op jit(solution)/shard_map/pallas_call | solution.py:329
  250.8 0.1 pad_maximum_fusion.4
  250.9 1.6 concatenate.31
  252.5 10.4 %all-gather.1 = f32[320,768]{1,0:T(8,128)S(1)} all-gather(f32[40,768]{1,0:T(8,128)S(1)} %concatenate.31), channel_id=3, replica_groups=mesh['dp'=8,'tensor'=4] {'dp'}, dimensions={0}, use_global_device_ids=true | all-gather | bytes 1105920 | tf_op jit(solution)/shard_map/all_gather | solution.py:487
  262.9 0.1 slice.119
  263.0 0.1 convert_element_type.23
  263.1 0.6 pad_maximum_fusion.5
  263.7 0.7 slice_reduce_fusion.1
  264.3 0.1 constant_dynamic-slice_fusion
  264.5 2.2 fusion
  266.7 0.9 slice.120
  267.6 0.1 copy.37
  267.8 0.9 copy.38
  268.7 0.9 convert_element_type.24
  269.6 0.1 slice_bitcast_fusion.1
  269.7 0.7 copy.39
  (64 shorter events, 0.3 us)
Async XLA Ops:
  8.0 57.1 %copy-start = (bf16[2000,192]{0,1:T(8,128)(2,1)S(1)}, bf16[2000,192]{0,1:T(8,128)(2,1)}, u32[]{:S(2)}) copy-start(bf16[2000,192]{0,1:T(8,128)(2,1)} %param.18) | copy-start | bytes 2304004
  8.0 1.8 copy-start.4
  8.0 142.7 %all-gather.4.cloned.1.call-start = ((), (), s32[]{:S(2)}) async-start(), calls=%async_computation.3 | async-start | bytes 9732096 | tf_op jit(solution)/shard_map/all_gather | solution.py:371
  8.1 2.9 %copy-start.6 = (bf16[192,768]{1,0:T(8,128)(2,1)S(1)}, bf16[192,768]{1,0:T(8,128)(2,1)}, u32[]{:S(2)}) copy-start(bf16[192,768]{1,0:T(8,128)(2,1)} %param.21) | copy-start | bytes 884740
  9.8 21.6 %copy-start.3 = (bf16[768,768]{0,1:T(8,128)(2,1)}, bf16[768,768]{0,1:T(8,128)(2,1)S(1)}, u32[]{:S(2)}) copy-start(bf16[768,768]{0,1:T(8,128)(2,1)S(1)} %copy.36) | copy-start | bytes 3538948
  11.0 206.4 %reduce-scatter.5.cloned.1.call-start = ((), (), s32[]{:S(2)}) async-start(), calls=%async_computation.5 | async-start | bytes 2654208 | tf_op jit(solution)/shard_map/reduce_scatter | solution.py:440
  12.0 8.9 %collective-permute-start = (bf16[96,768]{1,0:T(8,128)(2,1)S(1)}, bf16[96,768]{1,0:T(8,128)(2,1)S(1)}, u32[]{:S(2)}, u32[]{:S(2)}) collective-permute-start(bf16[96,768]{1,0:T(8,128)(2,1)S(1)} %fusion.4), channel_id=1, source_target_pairs={{0,1},{1,0},{2,3},{3,2},{4,5},{5,4},{6,7},{7,6},{8,9},{9,8},{10,11... | collective-permute-start | bytes 442376 | tf_op jit(solution)/shard_map/ppermute | solution.py:518
  15.1 16.3 %collective-permute-start.1 = (bf16[96,768]{1,0:T(8,128)(2,1)S(1)}, bf16[96,768]{1,0:T(8,128)(2,1)S(1)}, u32[]{:S(2)}, u32[]{:S(2)}) collective-permute-start(bf16[96,768]{1,0:T(8,128)(2,1)S(1)} %fusion.4), channel_id=1, source_target_pairs={{0,2},{1,3},{2,0},{3,1},{4,6},{5,7},{6,4},{7,5},{8,10},{9,11},{10,... | collective-permute-start | bytes 442376 | tf_op jit(solution)/shard_map/ppermute | solution.py:518
  17.7 13.7 %collective-permute-start.2 = (bf16[96,768]{1,0:T(8,128)(2,1)S(1)}, bf16[96,768]{1,0:T(8,128)(2,1)S(1)}, u32[]{:S(2)}, u32[]{:S(2)}) collective-permute-start(bf16[96,768]{1,0:T(8,128)(2,1)S(1)} %fusion.4), channel_id=1, source_target_pairs={{0,3},{1,2},{2,1},{3,0},{4,7},{5,6},{6,5},{7,4},{8,11},{9,10},{10,... | collective-permute-start | bytes 442376 | tf_op jit(solution)/shard_map/ppermute | solution.py:518
  31.5 33.4 %copy-start.7 = (f32[768]{0:T(1024)S(1)}, f32[768]{0:T(1024)}, u32[]{:S(2)}) copy-start(f32[768]{0:T(1024)} %param.24) | copy-start | bytes 9220
  31.5 33.6 %copy-start.19 = (s32[32]{0:T(128)S(1)}, s32[32]{0:T(128)}, u32[]{:S(2)}) copy-start(s32[32]{0:T(128)} %param.17) | copy-start | bytes 388
  31.6 33.8 %copy-start.10 = (f32[2,192]{1,0:T(2,128)S(1)}, f32[2,192]{1,0:T(2,128)}, u32[]{:S(2)}) copy-start(f32[2,192]{1,0:T(2,128)} %param.20) | copy-start | bytes 4612
  31.7 58.0 %copy-start.11 = (f32[768]{0:T(1024)S(1)}, f32[768]{0:T(1024)}, u32[]{:S(2)}) copy-start(f32[768]{0:T(1024)} %param.27) | copy-start | bytes 9220
  31.7 58.0 %copy-start.12 = (f32[768]{0:T(1024)S(1)}, f32[768]{0:T(1024)}, u32[]{:S(2)}) copy-start(f32[768]{0:T(1024)} %param.28) | copy-start | bytes 9220
  31.7 58.0 %copy-start.13 = (f32[768]{0:T(1024)S(1)}, f32[768]{0:T(1024)}, u32[]{:S(2)}) copy-start(f32[768]{0:T(1024)} %param.29) | copy-start | bytes 9220
  31.7 58.0 %copy-start.14 = (f32[768]{0:T(1024)S(1)}, f32[768]{0:T(1024)}, u32[]{:S(2)}) copy-start(f32[768]{0:T(1024)} %param.30) | copy-start | bytes 9220
  31.7 58.0 %copy-start.15 = (f32[768]{0:T(1024)S(1)}, f32[768]{0:T(1024)}, u32[]{:S(2)}) copy-start(f32[768]{0:T(1024)} %param.22) | copy-start | bytes 9220
  31.7 58.0 %copy-start.16 = (f32[768]{0:T(1024)S(1)}, f32[768]{0:T(1024)}, u32[]{:S(2)}) copy-start(f32[768]{0:T(1024)} %param.26) | copy-start | bytes 9220
  31.7 59.5 %copy-start.5 = (bf16[768,3,192]{0,2,1:T(8,128)(2,1)S(1)}, bf16[768,3,192]{0,2,1:T(8,128)(2,1)}, u32[]{:S(2)}) copy-start(bf16[768,3,192]{0,2,1:T(8,128)(2,1)} %param.19) | copy-start | bytes 2654212
  60.3 44.0 %copy-start.2 = (bf16[4,3,96,768]{3,2,1,0:T(8,128)(2,1)}, bf16[4,3,96,768]{3,2,1,0:T(8,128)(2,1)S(1)}, u32[]{:S(2)}) copy-start(bf16[4,3,96,768]{3,2,1,0:T(8,128)(2,1)S(1)} %all_to_all.5.mine) | copy-start | bytes 5308420
  60.3 44.0 %collective-permute-start.3 = (bf16[4,3,96,768]{3,2,1,0:T(8,128)(2,1)S(1)}, bf16[4,3,96,768]{3,2,1,0:T(8,128)(2,1)}, u32[]{:S(2)}, u32[]{:S(2)}) collective-permute-start(bf16[4,3,96,768]{3,2,1,0:T(8,128)(2,1)S(1)} %all_to_all.5.mine), channel_id=1, source_target_pairs={{0,4},{4,0},{8,12},{12,8},{16,20},{20,16},{24,28},{28,24},{1,5},{5... | collective-permute-start | bytes 5308424 | tf_op jit(solution)/shard_map/ppermute | solution.py:523
  60.3 44.0 %copy-start.9 = (s32[4]{0:T(128)}, s32[4]{0:T(128)S(1)}, u32[]{:S(2)}) copy-start(s32[4]{0:T(128)S(1)} %iota_xor_fusion.slots) | copy-start | bytes 52
  149.8 116.9 %reduce-scatter.3.cloned.1.call-start = ((), (), s32[]{:S(2)}) async-start(), calls=%async_computation.4 | async-start | bytes 1327104 | tf_op jit(solution)/shard_map/reduce_scatter | solution.py:440
  217.3 3.5 %copy-start.18 = (f32[1,768]{1,0:T(1,128)S(1)}, f32[1,768]{1,0:T(1,128)}, u32[]{:S(2)}) copy-start(f32[1,768]{1,0:T(1,128)} %get-tuple-element.58) | copy-start | bytes 9220
  220.8 30.1 %copy-start.8 = (f32[4,768]{1,0:T(4,128)S(1)}, f32[4,768]{1,0:T(4,128)}, u32[]{:S(2)}) copy-start(f32[4,768]{1,0:T(4,128)} %get-tuple-element.55) | copy-start | bytes 36868
  220.8 30.1 %copy-start.17 = (f32[1,768]{1,0:T(1,128)S(1)}, f32[1,768]{1,0:T(1,128)}, u32[]{:S(2)}) copy-start(f32[1,768]{1,0:T(1,128)} %get-tuple-element.57) | copy-start | bytes 9220
  263.7 6.8 %copy-start.1 = (bf16[2000,192]{0,1:T(8,128)(2,1)S(1)}, bf16[2000,192]{0,1:T(8,128)(2,1)}, u32[]{:S(2)}) copy-start(bf16[2000,192]{0,1:T(8,128)(2,1)} %param.18) | copy-start | bytes 2304004
Sparse Core Ops, SparseCore 0:
  12.3 93.1 all-gather.3
Sparse Core Ops, SparseCore 1:
  149.9 39.4 reduce-scatter.4
  217.4 33.4 reduce-scatter.2

commit v3 on v2

v3 whole, which is shorter than its diff:
```python
import functools

import jax
import jax.numpy as jnp
from jax import lax
from jax.experimental import pallas as pl
from jax.experimental.pallas import tpu as pltpu
from jax.sharding import PartitionSpec as P

HEAD = 64
HEADS = 3
LEN = 64
EPS = 1e-05
BR = 512
VMEM_BYTES = 58 * 1024 * 1024
HIGHEST_PREC = lax.Precision.HIGHEST
F32 = jnp.float32
BF16 = jnp.bfloat16


def dot_nn(a, b):
    return lax.dot_general(a, b, (((1,), (0,)), ((), ())), preferred_element_type=F32)


def dot_nt(a, b):
    return lax.dot_general(a, b, (((1,), (1,)), ((), ())), preferred_element_type=F32)


def dot_tn(a, b):
    return lax.dot_general(a, b, (((0,), (0,)), ((), ())), preferred_element_type=F32)


def cost(out_shape, args, flops):
    size = sum(v.size * v.dtype.itemsize for v in (*args, *out_shape))
    return pl.CostEstimate(flops=int(flops), bytes_accessed=int(size), transcendentals=0)


def params():
    return pltpu.CompilerParams(
        dimension_semantics=("arbitrary",), vmem_limit_bytes=VMEM_BYTES
    )


def rows_spec(width, rows=BR):
    return pl.BlockSpec((rows, width), lambda i, *_: (i, 0))


def whole_spec(shape):
    return pl.BlockSpec(shape, lambda i, *_: (0,) * len(shape), pipeline_mode=pl.Buffered(1))


def slot_spec(shape, k):
    return pl.BlockSpec(
        (1,) + shape, lambda i, s: (s[k],) + (0,) * len(shape), pipeline_mode=pl.Buffered(1)
    )


def normed(x):
    mean = jnp.mean(x, axis=-1, keepdims=True)
    centred = x - mean
    spread = jnp.mean(centred * centred, axis=-1, keepdims=True)
    inv = lax.rsqrt(spread + EPS)
    return centred * inv, inv


def norm_back(d_out, gain, xhat, inv):
    gy = d_out * gain
    m1 = jnp.mean(gy, axis=-1, keepdims=True)
    m2 = jnp.mean(gy * xhat, axis=-1, keepdims=True)
    return inv * (gy - m1 - xhat * m2)


def fold8(x):
    return jnp.sum(x.reshape(x.shape[0] // 8, 8, x.shape[1]), axis=0)


def entry_of(tok_ref, time_ref):
    tok = tok_ref[...].astype(F32)
    n = tok.shape[0] // LEN
    return (tok.reshape(n, LEN, tok.shape[1]) + time_ref[0][:, None, :]).reshape(tok.shape)


def half_masks():
    lane = lax.broadcasted_iota(jnp.int32, (LEN, 2 * HEAD), 1)
    low = (lane < HEAD).astype(F32)
    return low.astype(BF16), (1.0 - low).astype(BF16), lane < HEAD


def block_diag(x, mlo, mhi):
    return jnp.concatenate([x * mlo, x * mhi], axis=0)


def load_own(att, wqkv, wo, s):
    hc = HEADS * HEAD
    for t in range(3):
        wqkv[(2 * t + s) * hc : (2 * t + s + 1) * hc, :] = att[t * hc : (t + 1) * hc, :]
    wo[s * hc : (s + 1) * hc, :] = att[3 * hc :, :]


def load_pieces(core, mine, other, k, wqkv, wo, s):
    hc = HEADS * HEAD
    n = hc // 2
    for src, at in ((mine, core * n), (other, (1 - core) * n)):
        for t in range(3):
            wqkv[pl.ds(pl.multiple_of((2 * t + s) * hc + at, 16), n), :] = src[t, k]
        wo[pl.ds(pl.multiple_of(s * hc + at, 16), n), :] = src[3, k]


def tile_list(rows, width):
    return [(s, j) for s in range(rows // LEN) for j in range(width // 128)]


def tile(ref, st, part=0, width=0):
    s, j = st
    return ref[s * LEN : (s + 1) * LEN, part * width + j * 128 : part * width + (j + 1) * 128]


def put_tile(ref, st, value, part=0, width=0):
    s, j = st
    ref[s * LEN : (s + 1) * LEN, part * width + j * 128 : part * width + (j + 1) * 128] = (
        value.astype(BF16)
    )


def attend(n_one, wqkv, wo, bias, qkv_ref, p_ref, mix_ref):
    width = wo.shape[0]
    qkv_ref[...] = (dot_nt(n_one, wqkv[...]) + bias).astype(BF16)
    mlo, mhi, low = half_masks()
    tiles = tile_list(n_one.shape[0], width)
    scores = [
        dot_nt(tile(qkv_ref, t, 1, width), block_diag(tile(qkv_ref, t, 0, width), mlo, mhi))
        for t in tiles
    ]
    probs = []
    for t, sc in zip(tiles, scores):
        top = jnp.max(sc, axis=0, keepdims=True)
        e = jnp.exp((sc - top) * (HEAD**-0.5))
        p = (e * (1.0 / jnp.sum(e, axis=0, keepdims=True))).astype(BF16)
        probs.append(p)
        put_tile(p_ref, t, p)
    both = [dot_tn(p, tile(qkv_ref, t, 2, width)) for t, p in zip(tiles, probs)]
    for t, r in zip(tiles, both):
        put_tile(mix_ref, t, jnp.where(low, r[:LEN], r[LEN:]))
    return dot_nn(mix_ref[...], wo[...])


def attend_first(
    core, tok, time, vecs, own, mine, other, bias,
    n_one_ref, qkv_ref, p_ref, mix_ref, part_ref, wqkv, wo,
):
    @pl.when(pl.program_id(0) == 0)
    def _():
        load_own(own, wqkv, wo, 0)
        load_pieces(core[0], mine, other, 0, wqkv, wo, 1)

    xhat, _ = normed(entry_of(tok, time))
    n_one = (xhat * vecs[0:1, :] + vecs[1:2, :]).astype(BF16)
    n_one_ref[...] = n_one
    part = attend(n_one, wqkv, wo, bias[0:1, :], qkv_ref, p_ref, mix_ref)
    part_ref[...] = part.astype(part_ref.dtype)


def attend_last(
    core, tok, time, n_one, part, vecs, mine, other, bias,
    qkv_ref, p_ref, middle_ref, n_two_ref, wqkv, wo, mix_ref,
):
    @pl.when(pl.program_id(0) == 0)
    def _():
        load_pieces(core[0], mine, other, 0, wqkv, wo, 0)
        load_pieces(core[0], mine, other, 1, wqkv, wo, 1)

    more = attend(n_one[...], wqkv, wo, bias[1:2, :], qkv_ref, p_ref, mix_ref)
    middle = entry_of(tok, time) + part[...].astype(F32) + more + vecs[4:5, :]
    middle_ref[...] = middle
    xhat, _ = normed(middle)
    n_two_ref[...] = (xhat * vecs[2:3, :] + vecs[3:4, :]).astype(BF16)


ERF_P = 0.3275911
ERF_A = (0.254829592, -0.284496736, 1.421413741, -1.453152027, 1.061405429)


def gelu_both(x):
    bell = jnp.exp(x * x * (-0.5))
    t = 1.0 / (1.0 + jnp.abs(x) * (ERF_P * 0.5**0.5))
    poly = t * (
        0.5 * ERF_A[0]
        + t * (0.5 * ERF_A[1] + t * (0.5 * ERF_A[2] + t * (0.5 * ERF_A[3] + t * (0.5 * ERF_A[4]))))
    )
    tail = poly * bell
    cdf = jnp.where(x >= 0, 1.0 - tail, tail)
    return x * cdf, cdf + x * bell * 0.3989422804014327


def mlp_slot(n_two, c, wi, wb, b):
    pre = dot_nt(n_two, wi) + b
    d_act = dot_nt(c, wb)
    act, slope = gelu_both(pre)
    act = act.astype(BF16)
    d_pre = (d_act * slope).astype(BF16)
    return act, d_pre


def mlp_own(n_two, c, wi, wb, vecs, out_ref, dn2_ref, grad_ref, gbin_ref, acc, sums):
    hid = wi.shape[0]

    @pl.when(pl.program_id(0) == 0)
    def _():
        acc[...] = jnp.zeros_like(acc)
        sums[...] = jnp.zeros_like(sums)

    act, d_pre = mlp_slot(n_two[...], c[...], wi[...], wb[...], vecs[6:7, :])
    sums[...] += fold8(d_pre.astype(F32))
    out_ref[...] = dot_nn(act, wb[...]).astype(BF16)
    dn2_ref[...] = dot_nn(d_pre, wi[...]).astype(BF16)
    acc[:, :hid] += dot_tn(n_two[...], d_pre)
    acc[:, hid:] += dot_tn(c[...], act)

    @pl.when(pl.program_id(0) == pl.num_programs(0) - 1)
    def _():
        grad_ref[...] = acc[...].astype(BF16)
        gbin_ref[...] = jnp.sum(sums[...], axis=0, keepdims=True)


def mlp_rest(
    slots, n_two, c, middle, out_in, dn2_in, vecs, w1, w2, w3, b,
    out_ref, dmid_ref, sums_ref, sums,
):
    hid = b.shape[-1]
    start_sums(sums)
    out = out_in[...].astype(F32)
    dn2 = dn2_in[...].astype(F32)
    for k, w in enumerate((w1, w2, w3)):
        act, d_pre = mlp_slot(
            n_two[...], c[...], w[0, :hid, :], w[0, hid:, :], b[k : k + 1, :]
        )
        out = out + dot_nn(act, w[0, hid:, :])
        dn2 = dn2 + dot_nn(d_pre, w[0, :hid, :])
    mid = middle[...]
    cot = c[...].astype(F32)
    out_ref[...] = (mid + out + vecs[5:6, :]).astype(BF16)
    xhat, inv = normed(mid)
    d_mid = cot + norm_back(dn2, vecs[2:3, :], xhat, inv)
    dmid_ref[...] = d_mid
    add_sums(sums, (dn2 * xhat, dn2, d_mid, cot))
    end_sums(sums, sums_ref)


def start_sums(sums):
    @pl.when(pl.program_id(0) == 0)
    def _():
        sums[...] = jnp.zeros_like(sums)


def add_sums(sums, terms):
    for k, term in enumerate(terms):
        sums[8 * k : 8 * k + 8, :] += fold8(term)


def end_sums(sums, sums_ref):
    @pl.when(pl.program_id(0) == pl.num_programs(0) - 1)
    def _():
        for k in range(sums_ref.shape[0]):
            sums_ref[k : k + 1, :] = jnp.sum(sums[8 * k : 8 * k + 8, :], axis=0, keepdims=True)


def attend_back(dml, qkv, p, wqkv, wo, dqkv, dmix):
    width = wo.shape[0]
    scale = HEAD**-0.5
    dmix[...] = dot_nt(dml, wo[...]).astype(BF16)
    mlo, mhi, low = half_masks()
    tiles = tile_list(dml.shape[0], width)
    d_outs = [block_diag(tile(dmix, t), mlo, mhi) for t in tiles]
    d_ps = [dot_nt(tile(qkv, t, 2, width), d) for t, d in zip(tiles, d_outs)]
    for t, d in zip(tiles, d_outs):
        put_tile(dqkv, t, dot_nn(tile(p, t), d), 2, width)
    d_ss = []
    for t, d_p in zip(tiles, d_ps):
        pf = tile(p, t).astype(F32)
        g = pf * d_p
        d_ss.append((g - pf * jnp.sum(g, axis=0, keepdims=True)).astype(BF16))
    for t, d_s in zip(tiles, d_ss):
        put_tile(
            dqkv, t, dot_nn(d_s, block_diag(tile(qkv, t, 0, width), mlo, mhi)) * scale, 1, width
        )
    both = [dot_tn(d_s, tile(qkv, t, 1, width)) for t, d_s in zip(tiles, d_ss)]
    for t, r in zip(tiles, both):
        put_tile(dqkv, t, jnp.where(low, r[:LEN], r[LEN:]) * scale)
    return dot_nn(dqkv[...], wqkv[...])


def back_first(
    core, dmid, n_one, mix, qkv, p, own, mine, other, dn1_ref, grad_ref, sums_ref,
    wqkv, wo, dqkv, dmix, acc, sums,
):
    @pl.when(pl.program_id(0) == 0)
    def _():
        load_own(own, wqkv, wo, 0)
        load_pieces(core[0], mine, other, 0, wqkv, wo, 1)
        acc[...] = jnp.zeros_like(acc)

    start_sums(sums)
    dml = dmid[...].astype(BF16)
    dn1_ref[...] = attend_back(dml, qkv, p, wqkv, wo, dqkv, dmix).astype(dn1_ref.dtype)
    width = wo.shape[0]
    for t in range(3):
        acc[:, t * 256 : (t + 1) * 256] += dot_tn(
            n_one[...], dqkv[:, t * width : t * width + 256]
        )
    acc[:, 768:] += dot_tn(dml, mix[:, :256])
    add_sums(sums, (dqkv[...].astype(F32),))
    end_sums(sums, sums_ref)

    @pl.when(pl.program_id(0) == pl.num_programs(0) - 1)
    def _():
        hc = HEADS * HEAD
        for t in range(4):
            grad_ref[:, t * hc : (t + 1) * hc] = acc[:, t * 256 : t * 256 + hc].astype(BF16)


def back_last(
    core, tok, time, dmid, dn1, vecs, qkv, p, mine, other, more,
    gtok_ref, terms_ref, wqkv, wo, dqkv, dmix, sums,
):
    @pl.when(pl.program_id(0) == 0)
    def _():
        load_pieces(core[0], mine, other, 0, wqkv, wo, 0)
        load_pieces(core[0], mine, other, 1, wqkv, wo, 1)

    start_sums(sums)
    d_mid = dmid[...]
    d_n = dn1[...].astype(F32) + attend_back(
        d_mid.astype(BF16), qkv, p, wqkv, wo, dqkv, dmix
    )
    xhat, inv = normed(entry_of(tok, time))
    d_entry = d_mid + norm_back(d_n, vecs[0:1, :], xhat, inv)
    gtok_ref[...] = d_entry.astype(BF16)
    n = d_entry.shape[0] // LEN
    at = pl.multiple_of(pl.program_id(0) * n, 8)
    terms_ref[pl.ds(at, n), :] = jnp.sum(d_entry.reshape(n, LEN, -1), axis=1)
    add_sums(sums, (d_n * xhat, d_n))

    @pl.when(pl.program_id(0) == pl.num_programs(0) - 1)
    def _():
        total = n * pl.num_programs(0)
        terms_ref[pl.ds(pl.multiple_of(total, 8), 8), :] = more[...]
        for k in range(2):
            terms_ref[pl.ds(total + 4 + k, 1), :] = jnp.sum(
                sums[8 * k : 8 * k + 8, :], axis=0, keepdims=True
            )


def call(kernel, grid, in_specs, out_specs, out_shape, scratch, slots, args, flops):
    if slots is None:
        return pl.pallas_call(
            kernel, grid=grid, in_specs=in_specs, out_specs=out_specs, out_shape=out_shape,
            scratch_shapes=scratch, compiler_params=params(),
            cost_estimate=cost(out_shape, args, flops),
        )(*args)
    return pl.pallas_call(
        kernel,
        grid_spec=pltpu.PrefetchScalarGridSpec(
            num_scalar_prefetch=1, grid=grid, in_specs=in_specs, out_specs=out_specs,
            scratch_shapes=scratch,
        ),
        out_shape=out_shape,
        compiler_params=params(),
        cost_estimate=cost(out_shape, args, flops),
    )(slots, *args)


def body(
    tokens, timesteps, time_table, w_qkv, b_qv, w_out, b_out, w_in, b_in, w_back, b_back,
    gain_one, shift_one, gain_two, shift_two, cotangent,
):
    sentences = timesteps.shape[0]
    rows, dim = tokens.shape
    hc = w_out.shape[0]
    hid = w_back.shape[0]
    table_cols = time_table.shape[1]
    n_tensor = dim // hc
    me = lax.axis_index("tensor")
    part = lax.axis_index("dp")
    dp = lax.axis_size("dp")
    order = [me ^ k for k in range(n_tensor)]
    fast = dp == 8 and n_tensor == 4
    sds = jax.ShapeDtypeStruct
    nb = rows // BR
    unit = 1e9

    att_own = jnp.concatenate(
        [jnp.transpose(w_qkv, (1, 2, 0)).reshape(3 * hc, dim), w_out], axis=0
    )
    n_att = att_own.shape[0] // dp
    att_piece = lax.dynamic_slice_in_dim(att_own, part * n_att, n_att, 0)

    steps_iota = lax.broadcasted_iota(jnp.int32, (sentences, time_table.shape[0]), 1)
    picked = timesteps[:, None] == steps_iota
    own_rows = jnp.dot(picked.astype(BF16), time_table, preferred_element_type=F32)
    bias_count = 2 + hid // hc
    own_bias = jnp.concatenate([b_qv, b_in.reshape(-1, hc)])
    if fast:
        core = (part % 2).astype(jnp.int32).reshape(1)
        planes = jnp.pad(three(own_bias), ((0, sentences - 3 * bias_count), (0, 0)))
        note = jnp.concatenate(
            [own_rows.astype(BF16), jnp.zeros((sentences, 256 - hc), BF16), planes,
             jnp.zeros((sentences, dim - 256 - hc), BF16)], axis=1
        )
        message = jnp.concatenate([att_piece, note])
        got = [lax.ppermute(message, "tensor", flipped(4, k)) for k in (1, 2, 3)]
        mine_a = spread_plane([got[0][:n_att]])
        mine_b = spread_plane([got[1][:n_att], got[2][:n_att]])
        other_a = lax.ppermute(mine_a, "dp", flipped(8, 1))
        time_slots = jnp.stack([own_rows] + [m[n_att:, :hc].astype(F32) for m in got])
        bias_slots = jnp.stack(
            [own_bias] + [of_three(m[n_att:, 256 : 256 + hc], bias_count) for m in got]
        )
    else:
        core = jnp.zeros((1,), jnp.int32)
        (mine_a, mine_b), (other_a, other_b) = spread_any(att_piece, order, dp)
        time_slots = picked_rows(lax.all_gather(own_rows, "tensor", axis=0), order)
        bias_slots = picked_rows(lax.all_gather(own_bias, "tensor", axis=0), order)

    wi_own = w_in.T
    mlp_shard = jnp.concatenate([wi_own, w_back], axis=0)
    n_mlp = mlp_shard.shape[0] // dp
    mlp_all = lax.all_gather(
        lax.dynamic_slice_in_dim(mlp_shard, part * n_mlp, n_mlp, 0),
        ("tensor", "dp"), axis=0, tiled=True,
    ).reshape(n_tensor, mlp_shard.shape[0], dim)

    time_rows = jnp.transpose(picked_rows(time_slots, order), (1, 0, 2))
    time_rows = time_rows.reshape(nb, BR // LEN, dim)
    bq, bv = bias_slots[:, 0].reshape(2, -1), bias_slots[:, 1].reshape(2, -1)
    bias_rows = jnp.concatenate([bq, jnp.zeros_like(bq), bv], axis=1)
    bi_rest = bias_slots[1:, 2:].reshape(3, hid)
    zero = jnp.zeros_like(b_out)
    vecs = jnp.stack([gain_one, shift_one, gain_two, shift_two, b_out, b_back, b_in, zero])

    grid = (nb,)
    width = 2 * hc
    time_spec = pl.BlockSpec((1, BR // LEN, dim), lambda i, *_: (i, 0, 0))
    vec = whole_spec((8, dim))
    own_spec = whole_spec((4 * hc, dim))
    piece_spec = lambda k: whole_spec((4, k, hc // 2, dim))
    bias_spec = whole_spec((2, 3 * width))
    weights = [pltpu.VMEM((3 * width, dim), BF16), pltpu.VMEM((width, dim), BF16)]
    back = [pltpu.VMEM((BR, 3 * width), BF16), pltpu.VMEM((BR, width), BF16)]

    n_one, qkv_a, p_a, mix_a, attn_part = call(
        attend_first, grid,
        [rows_spec(dim), time_spec, vec, own_spec, piece_spec(1), piece_spec(1), bias_spec],
        [rows_spec(dim), rows_spec(3 * width), rows_spec(width), rows_spec(width),
         rows_spec(dim)],
        [sds((rows, dim), BF16), sds((rows, 3 * width), BF16), sds((rows, width), BF16),
         sds((rows, width), BF16), sds((rows, dim), BF16)],
        weights, core,
        (tokens, time_rows, vecs, att_own, mine_a, other_a, bias_rows), 14 * unit,
    )
    if fast:
        mine_b, n_one = lax.optimization_barrier((mine_b, n_one))
        other_b = lax.ppermute(mine_b, "dp", flipped(8, 1))
    qkv_b, p_b, middle, n_two = call(
        attend_last, grid,
        [rows_spec(dim), time_spec, rows_spec(dim), rows_spec(dim), vec, piece_spec(2),
         piece_spec(2), bias_spec],
        [rows_spec(3 * width), rows_spec(width), rows_spec(dim), rows_spec(dim)],
        [sds((rows, 3 * width), BF16), sds((rows, width), BF16), sds((rows, dim), F32),
         sds((rows, dim), BF16)],
        weights + [pltpu.VMEM((BR, width), BF16)], core,
        (tokens, time_rows, n_one, attn_part, vecs, mine_b, other_b, bias_rows), 15 * unit,
    )
    out_acc, dn2_acc, mlp_grads, gbin = call(
        mlp_own, grid,
        [rows_spec(dim), rows_spec(dim), whole_spec((hid, dim)), whole_spec((hid, dim)), vec],
        [rows_spec(dim), rows_spec(dim), whole_spec((dim, 2 * hid)), whole_spec((1, hid))],
        [sds((rows, dim), BF16), sds((rows, dim), BF16), sds((dim, 2 * hid), BF16),
         sds((1, hid), F32)],
        [pltpu.VMEM((dim, 2 * hid), F32), pltpu.VMEM((8, hid), F32)], None,
        (n_two, cotangent, wi_own, w_back, vecs), 21 * unit,
    )

    def scattered(grad):
        return lax.psum_scatter(grad, "dp", scatter_dimension=0, tiled=True)

    mlp_grads, mlp_all = lax.optimization_barrier((mlp_grads, mlp_all))
    mlp_grads = scattered(mlp_grads)
    mlp_spec = lambda k: slot_spec((2 * hid, dim), k)
    output, d_mid, sums_two = call(
        mlp_rest, grid,
        [rows_spec(dim), rows_spec(dim), rows_spec(dim), rows_spec(dim), rows_spec(dim), vec,
         mlp_spec(1), mlp_spec(2), mlp_spec(3), whole_spec((3, hid))],
        [rows_spec(dim), rows_spec(dim), whole_spec((4, dim))],
        [sds((rows, dim), BF16), sds((rows, dim), F32), sds((4, dim), F32)],
        [pltpu.VMEM((32, dim), F32)], me ^ jnp.arange(n_tensor, dtype=jnp.int32),
        (n_two, cotangent, middle, out_acc, dn2_acc, vecs, mlp_all, mlp_all, mlp_all, bi_rest),
        44 * unit,
    )
    dn1_acc, att_grads, sums_qkv = call(
        back_first, grid,
        [rows_spec(dim), rows_spec(dim), rows_spec(width), rows_spec(3 * width),
         rows_spec(width), own_spec, piece_spec(1), piece_spec(1)],
        [rows_spec(dim), whole_spec((dim, 4 * hc)), whole_spec((1, 3 * width))],
        [sds((rows, dim), BF16), sds((dim, 4 * hc), BF16), sds((1, 3 * width), F32)],
        weights + back
        + [pltpu.VMEM((dim, 1024), F32), pltpu.VMEM((8, 3 * width), F32)],
        core,
        (d_mid, n_one, mix_a, qkv_a, p_a, att_own, mine_a, other_a), 18 * unit,
    )
    if fast:
        parts = lax.all_to_all(
            att_grads.reshape(dp, dim // dp, 4 * hc), "dp", 0, 0, tiled=True
        )
    else:
        att_grads = scattered(att_grads).astype(F32)
    bias_row = jnp.concatenate(
        [sums_qkv[:, :256], timesteps.astype(F32).reshape(1, -1),
         jnp.zeros((1, dim - 512 - sentences), F32), sums_qkv[:, 2 * width : 2 * width + 256]],
        axis=1,
    )
    more = jnp.concatenate([sums_two, jnp.zeros((2, dim), F32), gbin, bias_row])
    grad_win = mlp_grads[:, :hid].astype(F32)
    grad_wback = mlp_grads[:, hid:].astype(F32).T
    dn1_acc, grad_win, grad_wback = lax.optimization_barrier((dn1_acc, grad_win, grad_wback))
    grad_tokens, terms = call(
        back_last, grid,
        [rows_spec(dim), time_spec, rows_spec(dim), rows_spec(dim), vec,
         rows_spec(3 * width), rows_spec(width), piece_spec(2), piece_spec(2), vec],
        [rows_spec(dim), whole_spec((sentences + 8, dim))],
        [sds((rows, dim), BF16), sds((sentences + 8, dim), F32)],
        weights + back + [pltpu.VMEM((16, dim), F32)], core,
        (tokens, time_rows, d_mid, dn1_acc, vecs, qkv_b, p_b, mine_b, other_b, more), 20 * unit,
    )
    if fast:
        terms, parts = lax.optimization_barrier((terms, parts))
        att_grads = jnp.sum(parts.astype(F32), axis=0)
    terms = lax.all_gather(terms, "dp", axis=0)
    all_cols = lax.dynamic_slice_in_dim(
        terms[:, :sentences], me * table_cols, table_cols, 2
    ).reshape(-1, table_cols)
    small = jnp.sum(terms[:, sentences:], axis=0)
    all_steps = terms[:, -1, 256 : 256 + sentences].astype(jnp.int32).reshape(-1)
    all_picked = all_steps[:, None] == lax.broadcasted_iota(
        jnp.int32, (all_steps.shape[0], time_table.shape[0]), 1
    )
    grad_table = lax.dot_general(
        all_picked.astype(F32), all_cols, (((0,), (0,)), ((), ())),
        precision=HIGHEST_PREC, preferred_element_type=F32,
    )
    grad_wqkv = att_grads[:, : 3 * hc].reshape(-1, 3, hc)
    grad_wout = att_grads[:, 3 * hc :].T
    grad_bqv = jnp.stack([small[7, :hc], small[7, dim - 256 : dim - 256 + hc]])
    return (
        output, grad_tokens, grad_table, grad_wqkv, grad_bqv, grad_wout, small[2], grad_win,
        small[6], grad_wback, small[3], small[4], small[5], small[0], small[1],
    )


def picked_rows(array, order):
    return jnp.concatenate([lax.dynamic_slice_in_dim(array, k, 1, 0) for k in order])


def three(value):
    parts = []
    for _ in range(3):
        low = lax.reduce_precision(value, 8, 7)
        parts.append(low.astype(BF16))
        value = value - low
    return jnp.concatenate(parts)


def of_three(rows, n):
    rows = rows.astype(F32)
    return (rows[2 * n : 3 * n] + rows[n : 2 * n]) + rows[:n]


def flipped(n, bits):
    return [(i, i ^ bits) for i in range(n)]


def spread_plane(slots):
    slots = jnp.stack(slots)
    whole = jnp.broadcast_to(slots[None], (4,) + slots.shape)
    return lax.all_to_all(
        whole, "dp", 0, 0, tiled=True, axis_index_groups=[[0, 2, 4, 6], [1, 3, 5, 7]]
    )


def spread_any(piece, order, dp):
    shards = lax.all_gather(piece, ("tensor", "dp"), axis=0, tiled=True)
    n_tensor = len(order)
    rows = piece.shape[0] * dp
    shards = picked_rows(shards.reshape(n_tensor, rows, -1), order[1:])
    shards = shards.reshape(n_tensor - 1, 4, 2, rows // 8, -1)
    halves = [jnp.transpose(shards[:, :, c], (1, 0, 2, 3)) for c in (0, 1)]
    return tuple((h[:, :1], h[:, 1:]) for h in halves)


def solution(mesh):
    return jax.shard_map(
        body,
        mesh=mesh,
        in_specs=(
            P("dp", None), P("dp"), P(None, "tensor"), P(None, None, "tensor"), P(None, "tensor"),
            P("tensor", None), P(), P(None, "tensor"), P("tensor"), P("tensor", None), P(), P(),
            P(), P(), P(), P("dp", None),
        ),
        out_specs=(
            P("dp", None), P("dp", None), P(None, "tensor"), P("dp", None, "tensor"),
            P(None, "tensor"), P("tensor", "dp"), P(), P("dp", "tensor"), P("tensor"),
            P("tensor", "dp"), P(), P(), P(), P(), P(),
        ),
        check_vma=False,
    )
```

time: 278 us -> 230 us (0.83)
  blocking collectives: 60 us -> 12 us
  Pallas kernels: 153 us -> 141 us
  starting transfers between devices: 5.99 us -> 17.7 us
  waiting for transfers between devices: 13.8 us -> 24.1 us
  between operations: 21.8 us -> 14.6 us
  local copies, waits for them, and re-layouts: 13.8 us -> 10.4 us
    pallas_call x3 -> x1, Pallas kernels: 52.2 us -> 23.1 us  [call(): pl.pallas_call(kernel, grid=grid, in_specs=in_specs, out_specs=out_specs,...]
    all_to_all x1 -> x0, blocking collectives: 28.5 us -> none  [spread(): lax.all_to_all(whole, 'dp', 0, 0, tiled=True, axis_index_groups=[[0, 2, 4...]
    all_gather x1 -> x0, blocking collectives: 21.1 us -> none  [body(): lax.all_gather(jnp.concatenate([own_rows, b_qv, b_in.reshape(-1, hc), jnp...]
    pallas_call x3 -> x5, Pallas kernels: 101 us -> 118 us  [call(): pl.pallas_call(kernel, grid_spec=pltpu.PrefetchScalarGridSpec(num_scalar_...]
    all_to_all x0 -> x3, starting transfers between devices: none -> 11.8 us  [the longest x2 8.19 us: spread_plane(): lax.all_to_all(whole, 'dp', 0, 0, tiled=True, axis_index_groups=[[0, 2, 4...]
    all_to_all x0 -> x3, waiting for transfers between devices: none -> 9.79 us  [the longest x2 9.79 us: spread_plane(): lax.all_to_all(whole, 'dp', 0, 0, tiled=True, axis_index_groups=[[0, 2, 4...]
    ppermute x4 -> x5, waiting for transfers between devices: 13.7 us -> 11.6 us  [the longest x3 10 us: body(): got = [lax.ppermute(message, 'tensor', flipped(4, k)) for k in (1, 2, 3)]]
    ppermute x4 -> x5, starting transfers between devices: 5.68 us -> 5.69 us  [the longest x3 5.68 us: body(): got = [lax.ppermute(message, 'tensor', flipped(4, k)) for k in (1, 2, 3)]]
  transfers between devices with their start and end apart: 7 -> 10, of which waited for: 2 -> 6; matrix products, arithmetic and copies ran while one was open for 6% -> 5% of each run, Pallas kernels for 55% -> 61%
where the time goes in v3:
time: 230 us; the launch traced here: 229 us
  Pallas kernels  141 us (61%)
  waiting for transfers between devices  24.1 us (10%)
  starting transfers between devices  17.7 us (8%)
  between operations  14.6 us (6%)
  blocking collectives  12 us (5%)
  local copies, waits for them, and re-layouts  10.4 us (5%)
  other arithmetic  6.86 us (3%)
  matrix products  2.62 us (1%)
    pallas_call x5, Pallas kernels, call(): pl.pallas_call(kernel, grid_spec=pltpu.PrefetchScalarGridSpec(num_scalar_...  118 us
    pallas_call x1, Pallas kernels, call(): pl.pallas_call(kernel, grid=grid, in_specs=in_specs, out_specs=out_specs,...  23.1 us
    all_gather x1, blocking collectives, body(): terms = lax.all_gather(terms, 'dp', axis=0)  12 us
    ppermute x3, waiting for transfers between devices, body(): got = [lax.ppermute(message, 'tensor', flipped(4, k)) for k in (1, 2, 3)]  10 us
    all_to_all x2, waiting for transfers between devices, spread_plane(): lax.all_to_all(whole, 'dp', 0, 0, tiled=True, axis_index_groups=[[0, 2, 4...  9.79 us
    all_to_all x2, starting transfers between devices, spread_plane(): lax.all_to_all(whole, 'dp', 0, 0, tiled=True, axis_index_groups=[[0, 2, 4...  8.19 us
    ppermute x3, starting transfers between devices, body(): got = [lax.ppermute(message, 'tensor', flipped(4, k)) for k in (1, 2, 3)]  5.68 us
  transfers between devices with their start and end apart: 10, of which 6 were waited for; matrix products, arithmetic and copies ran while one was open for 5% of the time, Pallas kernels for 61%

profile of v3, /device:TPU:0, one launch (start us, length us, event | category | flops | bytes accessed | tf_op | source)
XLA Modules:
  0.0 229.0 jit_solution(17775615720338004410)
XLA Ops:
  7.2 0.0 copy-start
  7.2 0.0 all-gather.3.cloned.1.call-start
  7.3 1.6 copy.37
  8.9 0.0 copy-start.3
  8.9 0.0 copy-start.4
  8.9 0.0 copy-start.17
  9.0 0.9 fusion.2
  9.9 0.0 copy-start.13
  9.9 0.0 copy-start.14
  9.9 0.0 all-gather.3.cloned.1.call-update
  9.9 0.1 reshape.73
  10.0 0.6 copy-done.3
  10.6 0.1 copy-done.4
  10.7 0.1 fusion.4
  10.8 0.4 fusion.24
  11.2 0.1 maximum_maximum_fusion
  11.3 3.1 %collective-permute-start = (bf16[128,768]{1,0:T(8,128)(2,1)S(1)}, bf16[128,768]{1,0:T(8,128)(2,1)S(1)}, u32[]{:S(2)}, u32[]{:S(2)}) collective-permute-start(bf16[128,768]{1,0:T(8,128)(2,1)S(1)} %maximum_maximum_fusion), channel_id=1, source_target_pairs={{0,1},{1,0},{2,3},{3,2},{4,5},{5,4},{6,7},{7,6},{8,9},{9,8},{10,11... | collective-permute-start | bytes 589832 | tf_op jit(solution)/shard_map/ppermute | solution.py:410
  14.4 2.6 %collective-permute-start.1 = (bf16[128,768]{1,0:T(8,128)(2,1)S(1)}, bf16[128,768]{1,0:T(8,128)(2,1)S(1)}, u32[]{:S(2)}, u32[]{:S(2)}) collective-permute-start(bf16[128,768]{1,0:T(8,128)(2,1)S(1)} %maximum_maximum_fusion), channel_id=1, source_target_pairs={{0,2},{1,3},{2,0},{3,1},{4,6},{5,7},{6,4},{7,5},{8,10},{9,11},{10,... | collective-permute-start | bytes 589832 | tf_op jit(solution)/shard_map/ppermute | solution.py:410
  17.2 0.6 stack.95.vecs
  17.8 1.1 pad_maximum_fusion.own
  18.9 3.8 %collective-permute-done = bf16[128,768]{1,0:T(8,128)(2,1)S(1)} collective-permute-done((bf16[128,768]{1,0:T(8,128)(2,1)S(1)}, bf16[128,768]{1,0:T(8,128)(2,1)S(1)}, u32[]{:S(2)}, u32[]{:S(2)}) %collective-permute-start) | collective-permute-done | bytes 196640 | tf_op jit(solution)/shard_map/ppermute | solution.py:410
  22.7 0.9 broadcast_in_dim.30
  23.6 4.7 %all-to-all-start.1 = ((bf16[4,1,96,768]{3,2,1,0:T(8,128)(2,1)}), bf16[4,1,96,768]{3,2,1,0:T(8,128)(2,1)S(1)}, u32[]{:S(2)}, u32[]{:S(2)}) async-start(bf16[4,1,96,768]{3,2,1,0:T(8,128)(2,1)} %broadcast_in_dim.30), calls=%async_computation.1 | async-start | bytes 1179648 | tf_op jit(solution)/shard_map/all_to_all | solution.py:584
  28.3 6.3 %collective-permute-done.1 = bf16[128,768]{1,0:T(8,128)(2,1)S(1)} collective-permute-done((bf16[128,768]{1,0:T(8,128)(2,1)S(1)}, bf16[128,768]{1,0:T(8,128)(2,1)S(1)}, u32[]{:S(2)}, u32[]{:S(2)}) %collective-permute-start.1) | collective-permute-done | bytes 196640 | tf_op jit(solution)/shard_map/ppermute | solution.py:410
  34.7 1.1 all-to-all-done.1.mine
  35.8 0.1 reshape_squeeze.6
  35.9 0.1 reshape_squeeze.7
  36.0 0.1 copy.36
  36.1 0.8 reshape.74.time
  36.9 1.1 broadcast_in_dim.29
  38.0 3.5 %all-to-all-start = ((bf16[4,2,96,768]{3,2,1,0:T(8,128)(2,1)}), bf16[4,2,96,768]{3,2,1,0:T(8,128)(2,1)S(1)}, u32[]{:S(2)}, u32[]{:S(2)}) async-start(bf16[4,2,96,768]{3,2,1,0:T(8,128)(2,1)} %broadcast_in_dim.29), calls=%async_computation | async-start | bytes 2359296 | tf_op jit(solution)/shard_map/all_to_all | solution.py:584
  41.5 0.2 reduce-scatter.2.cloned.1.call-start
  41.7 0.6 pad_maximum_fusion.5.bias
  42.3 14.9 %shard_map.271 = (bf16[2048,768]{1,0:T(8,128)(2,1)}, bf16[2048,1152]{1,0:T(8,128)(2,1)}, bf16[2048,384]{1,0:T(8,128)(2,1)}, bf16[2048,384]{1,0:T(8,128)(2,1)}, bf16[2048,768]{1,0:T(8,128)(2,1)}) custom-call(s32[1]{0:T(128)} %bitcast.core, bf16[2048,768]{1,0:T(8,128)(2,1)} %tok.5, f32[4,8,768]{2,1,0:T(8,128)} %reshape.74.time, f32[8,768]{1,0:T(8,128)} %stack.95.vecs, ...), custom_call_target="tpu_custom_call" | custom-call | flops 14000000000 | bytes 19792896 | tf_op jit(solution)/shard_map/pallas_call | solution.py:360
  57.2 8.7 %all-to-all-done.mine = bf16[4,2,96,768]{3,2,1,0:T(8,128)(2,1)S(1)} async-done(((bf16[4,2,96,768]{3,2,1,0:T(8,128)(2,1)}), bf16[4,2,96,768]{3,2,1,0:T(8,128)(2,1)S(1)}, u32[]{:S(2)}, u32[]{:S(2)}) %all-to-all-start) | async-done | bytes 1179680 | tf_op jit(solution)/shard_map/all_to_all | solution.py:584
  65.9 0.1 pad.8.clone
  66.0 0.6 iota_xor_fusion.slots
  66.6 0.7 reshape.76.b
  67.3 1.6 collective-permute-done.4.other
  68.9 15.9 %shard_map.272 = (bf16[2048,1152]{1,0:T(8,128)(2,1)}, bf16[2048,384]{1,0:T(8,128)(2,1)}, f32[2048,768]{1,0:T(8,128)}, bf16[2048,768]{1,0:T(8,128)(2,1)}) custom-call(s32[1]{0:T(128)} %bitcast.core, bf16[2048,768]{1,0:T(8,128)(2,1)} %tok.5, f32[4,8,768]{2,1,0:T(8,128)} %reshape.74.time, bf16[2048,768]{1,0:T(8,128)(2,1)} %get-tuple-element.46.n_one, ...), custom_call_target="tpu_custom_call" | custom-call | flops 15000000512 | bytes 27657216 | tf_op jit(solution)/shard_map/pallas_call | solution.py:360
  84.8 23.1 %shard_map.273 = (bf16[2048,768]{1,0:T(8,128)(2,1)}, bf16[2048,768]{1,0:T(8,128)(2,1)}, bf16[768,1536]{1,0:T(8,128)(2,1)}, f32[1,768]{1,0:T(1,128)}) custom-call(bf16[2048,768]{1,0:T(8,128)(2,1)} %get-tuple-element.49.n_two, bf16[2048,768]{1,0:T(8,128)(2,1)} %c.3, bf16[768,768]{1,0:T(8,128)(2,1)} %bitcast.49, bf16[768,768]{1,0:T(8,128)(2,1)} %wb.1, ...), custom_call_target="tpu_custom_call" | custom-call | flops 20999999488 | bytes 17329152 | tf_op jit(solution)/shard_map/pallas_call | solution.py:355
  107.9 2.6 %all-gather.3.cloned.1.call-done = bf16[6144,768]{1,0:T(8,128)(2,1)} async-done(((bf16[192,768]{1,0:T(8,128)(2,1)}), bf16[6144,768]{1,0:T(8,128)(2,1)}) %all-gather.3.cloned.1.call-update) | async-done | bytes 9437200 | tf_op jit(solution)/shard_map/all_gather | solution.py:427
  110.5 0.0 reduce-scatter.2.cloned.1.call-update
  110.5 46.0 %shard_map.274 = (bf16[2048,768]{1,0:T(8,128)(2,1)}, f32[2048,768]{1,0:T(8,128)}, f32[4,768]{1,0:T(4,128)}) custom-call(s32[4]{0:T(128)} %iota_xor_fusion.slots, bf16[2048,768]{1,0:T(8,128)(2,1)} %get-tuple-element.49.n_two, bf16[2048,768]{1,0:T(8,128)(2,1)} %c.3, f32[2048,768]{1,0:T(8,128)} %get-tuple-element.50.middle, ...), custom_call_target="tpu_custom_call" | custom-call | flops 44000002048 | bytes 56669184 | tf_op jit(solution)/shard_map/pallas_call | solution.py:360
  156.5 20.8 %shard_map.275 = (bf16[2048,768]{1,0:T(8,128)(2,1)}, bf16[768,768]{1,0:T(8,128)(2,1)}, f32[1,1152]{1,0:T(1,128)}) custom-call(s32[1]{0:T(128)} %bitcast.core, f32[2048,768]{1,0:T(8,128)} %get-tuple-element.56.dmid, bf16[2048,768]{1,0:T(8,128)(2,1)} %get-tuple-element.46.n_one, bf16[2048,384]{1,0:T(8,128)(2,1)} %get-tuple-element.57.mix, ...), custom_call_target="tpu_custom_call" | custom-call | flops 17999998976 | bytes 23990784 | tf_op jit(solution)/shard_map/pallas_call | solution.py:360
  177.3 0.0 copy-start.8
  177.3 0.0 copy-start.15
  177.3 3.6 %all-to-all-start.2 = ((bf16[8,96,768]{2,1,0:T(8,128)(2,1)}), bf16[8,96,768]{2,1,0:T(8,128)(2,1)S(1)}, u32[]{:S(2)}, u32[]{:S(2)}) async-start(bf16[8,96,768]{2,1,0:T(8,128)(2,1)} %bitcast.55), calls=%async_computation.3 | async-start | bytes 2359296 | tf_op jit(solution)/shard_map/all_to_all | solution.py:511
  180.9 0.7 fusion.23
  181.6 0.7 maximum_maximum_fusion.1.more
  182.3 1.8 convert_bitcast_fusion
  184.1 20.2 %shard_map.276 = (bf16[2048,768]{1,0:T(8,128)(2,1)}, f32[40,768]{1,0:T(8,128)}) custom-call(s32[1]{0:T(128)} %bitcast.core, bf16[2048,768]{1,0:T(8,128)(2,1)} %tok.5, f32[4,8,768]{2,1,0:T(8,128)} %reshape.74.time, f32[2048,768]{1,0:T(8,128)} %get-tuple-element.56.dmid, bf16[2048,768]{1,0:T(8,128)(2,1)} %get-tuple-element.62.dn1, f32[8,768]{1,0:T(8,128)} %stack.95.vecs, ...), custom_call_target="tpu_custom_call" | custom-call | flops 20000000000 | bytes 24649728 | tf_op jit(solution)/shard_map/pallas_call | solution.py:360
  204.3 12.0 %all-gather = f32[320,768]{1,0:T(8,128)S(1)} all-gather(f32[40,768]{1,0:T(8,128)} %get-tuple-element.71), channel_id=2, replica_groups=mesh['dp'=8,'tensor'=4] {'dp'}, dimensions={0}, use_global_device_ids=true | all-gather | bytes 1105920 | tf_op jit(solution)/shard_map/all_gather | solution.py:537
  216.3 0.1 slice.178
  216.4 0.7 slice_reduce_fusion.1
  217.1 0.2 convert_reduce_fusion
  217.3 0.1 slice_bitcast_fusion.2
  217.4 0.1 convert_element_type.58
  217.4 0.2 copy.38
  217.6 0.9 copy.39
  218.5 0.7 copy.40
  219.2 0.6 pad_maximum_fusion.10
  219.8 0.1 constant_dynamic-slice_fusion
  219.9 2.2 fusion
  (68 shorter events, 0.4 us)
Async XLA Ops:
  7.2 3.6 %copy-start = (bf16[2000,192]{0,1:T(8,128)(2,1)S(1)}, bf16[2000,192]{0,1:T(8,128)(2,1)}, u32[]{:S(2)}) copy-start(bf16[2000,192]{0,1:T(8,128)(2,1)} %param.18) | copy-start | bytes 2304004
  7.2 103.3 %all-gather.3.cloned.1.call-start = ((), (), s32[]{:S(2)}) async-start(), calls=%async_computation.4 | async-start | bytes 9732096 | tf_op jit(solution)/shard_map/all_gather | solution.py:427
  7.2 2.7 %copy-start.7 = (f32[768]{0:T(1024)S(1)}, f32[768]{0:T(1024)}, u32[]{:S(2)}) copy-start(f32[768]{0:T(1024)} %param.24) | copy-start | bytes 9220
  7.3 2.7 %copy-start.16 = (f32[2,192]{1,0:T(2,128)S(1)}, f32[2,192]{1,0:T(2,128)}, u32[]{:S(2)}) copy-start(f32[2,192]{1,0:T(2,128)} %param.20) | copy-start | bytes 4612
  8.9 1.9 copy-start.2
  8.9 1.7 copy-start.3
  8.9 1.8 copy-start.4
  8.9 1.9 copy-start.17
  9.8 7.1 %copy-start.9 = (f32[768]{0:T(1024)S(1)}, f32[768]{0:T(1024)}, u32[]{:S(2)}) copy-start(f32[768]{0:T(1024)} %param.27) | copy-start | bytes 9220
  9.8 7.2 %copy-start.10 = (f32[768]{0:T(1024)S(1)}, f32[768]{0:T(1024)}, u32[]{:S(2)}) copy-start(f32[768]{0:T(1024)} %param.28) | copy-start | bytes 9220
  9.8 7.2 %copy-start.11 = (f32[768]{0:T(1024)S(1)}, f32[768]{0:T(1024)}, u32[]{:S(2)}) copy-start(f32[768]{0:T(1024)} %param.29) | copy-start | bytes 9220
  9.8 7.2 %copy-start.12 = (f32[768]{0:T(1024)S(1)}, f32[768]{0:T(1024)}, u32[]{:S(2)}) copy-start(f32[768]{0:T(1024)} %param.30) | copy-start | bytes 9220
  9.9 7.2 %copy-start.13 = (f32[768]{0:T(1024)S(1)}, f32[768]{0:T(1024)}, u32[]{:S(2)}) copy-start(f32[768]{0:T(1024)} %param.22) | copy-start | bytes 9220
  9.9 7.2 %copy-start.14 = (f32[768]{0:T(1024)S(1)}, f32[768]{0:T(1024)}, u32[]{:S(2)}) copy-start(f32[768]{0:T(1024)} %param.26) | copy-start | bytes 9220
  11.3 11.4 %collective-permute-start = (bf16[128,768]{1,0:T(8,128)(2,1)S(1)}, bf16[128,768]{1,0:T(8,128)(2,1)S(1)}, u32[]{:S(2)}, u32[]{:S(2)}) collective-permute-start(bf16[128,768]{1,0:T(8,128)(2,1)S(1)} %maximum_maximum_fusion), channel_id=1, source_target_pairs={{0,1},{1,0},{2,3},{3,2},{4,5},{5,4},{6,7},{7,6},{8,9},{9,8},{10,11... | collective-permute-start | bytes 589832 | tf_op jit(solution)/shard_map/ppermute | solution.py:410
  14.4 20.1 %collective-permute-start.1 = (bf16[128,768]{1,0:T(8,128)(2,1)S(1)}, bf16[128,768]{1,0:T(8,128)(2,1)S(1)}, u32[]{:S(2)}, u32[]{:S(2)}) collective-permute-start(bf16[128,768]{1,0:T(8,128)(2,1)S(1)} %maximum_maximum_fusion), channel_id=1, source_target_pairs={{0,2},{1,3},{2,0},{3,1},{4,6},{5,7},{6,4},{7,5},{8,10},{9,11},{10,... | collective-permute-start | bytes 589832 | tf_op jit(solution)/shard_map/ppermute | solution.py:410
  17.0 17.6 %collective-permute-start.2 = (bf16[128,768]{1,0:T(8,128)(2,1)S(1)}, bf16[128,768]{1,0:T(8,128)(2,1)S(1)}, u32[]{:S(2)}, u32[]{:S(2)}) collective-permute-start(bf16[128,768]{1,0:T(8,128)(2,1)S(1)} %maximum_maximum_fusion), channel_id=1, source_target_pairs={{0,3},{1,2},{2,1},{3,0},{4,7},{5,6},{6,5},{7,4},{8,11},{9,10},{10,... | collective-permute-start | bytes 589832 | tf_op jit(solution)/shard_map/ppermute | solution.py:410
  23.6 12.2 %all-to-all-start.1 = ((bf16[4,1,96,768]{3,2,1,0:T(8,128)(2,1)}), bf16[4,1,96,768]{3,2,1,0:T(8,128)(2,1)S(1)}, u32[]{:S(2)}, u32[]{:S(2)}) async-start(bf16[4,1,96,768]{3,2,1,0:T(8,128)(2,1)} %broadcast_in_dim.30), calls=%async_computation.1 | async-start | bytes 1179648 | tf_op jit(solution)/shard_map/all_to_all | solution.py:584
  35.8 2.2 copy-start.6
  35.8 6.6 %collective-permute-start.3 = (bf16[4,1,96,768]{3,2,1,0:T(8,128)(2,1)S(1)}, bf16[4,1,96,768]{3,2,1,0:T(8,128)(2,1)}, u32[]{:S(2)}, u32[]{:S(2)}) collective-permute-start(bf16[4,1,96,768]{3,2,1,0:T(8,128)(2,1)S(1)} %all-to-all-done.1.mine), channel_id=1, source_target_pairs={{0,4},{4,0},{8,12},{12,8},{16,20},{20,16},{24,28},{28,24},{1,5},{5... | collective-permute-start | bytes 1769480 | tf_op jit(solution)/shard_map/ppermute | solution.py:413
  38.0 27.9 %all-to-all-start = ((bf16[4,2,96,768]{3,2,1,0:T(8,128)(2,1)}), bf16[4,2,96,768]{3,2,1,0:T(8,128)(2,1)S(1)}, u32[]{:S(2)}, u32[]{:S(2)}) async-start(bf16[4,2,96,768]{3,2,1,0:T(8,128)(2,1)} %broadcast_in_dim.29), calls=%async_computation | async-start | bytes 2359296 | tf_op jit(solution)/shard_map/all_to_all | solution.py:584
  41.5 140.8 %reduce-scatter.2.cloned.1.call-start = ((), (), s32[]{:S(2)}) async-start(), calls=%async_computation.5 | async-start | bytes 2654208 | tf_op jit(solution)/shard_map/reduce_scatter | solution.py:484
  65.9 3.0 %copy-start.5 = (bf16[4,2,96,768]{3,2,1,0:T(8,128)(2,1)}, bf16[4,2,96,768]{3,2,1,0:T(8,128)(2,1)S(1)}, u32[]{:S(2)}) copy-start(bf16[4,2,96,768]{3,2,1,0:T(8,128)(2,1)S(1)} %all-to-all-done.mine) | copy-start | bytes 3538948
  65.9 3.0 %collective-permute-start.4 = (bf16[4,2,96,768]{3,2,1,0:T(8,128)(2,1)S(1)}, bf16[4,2,96,768]{3,2,1,0:T(8,128)(2,1)}, u32[]{:S(2)}, u32[]{:S(2)}) collective-permute-start(bf16[4,2,96,768]{3,2,1,0:T(8,128)(2,1)S(1)} %all-to-all-done.mine), channel_id=1, source_target_pairs={{0,4},{4,0},{8,12},{12,8},{16,20},{20,16},{24,28},{28,24},{1,5},{5... | collective-permute-start | bytes 3538952 | tf_op jit(solution)/shard_map/ppermute | solution.py:462
  177.3 4.3 %copy-start.8 = (f32[4,768]{1,0:T(4,128)S(1)}, f32[4,768]{1,0:T(4,128)}, u32[]{:S(2)}) copy-start(f32[4,768]{1,0:T(4,128)} %get-tuple-element.65) | copy-start | bytes 36868
  177.3 4.3 %copy-start.15 = (f32[1,768]{1,0:T(1,128)S(1)}, f32[1,768]{1,0:T(1,128)}, u32[]{:S(2)}) copy-start(f32[1,768]{1,0:T(1,128)} %get-tuple-element.66) | copy-start | bytes 9220
  177.3 27.0 %all-to-all-start.2 = ((bf16[8,96,768]{2,1,0:T(8,128)(2,1)}), bf16[8,96,768]{2,1,0:T(8,128)(2,1)S(1)}, u32[]{:S(2)}, u32[]{:S(2)}) async-start(bf16[8,96,768]{2,1,0:T(8,128)(2,1)} %bitcast.55), calls=%async_computation.3 | async-start | bytes 2359296 | tf_op jit(solution)/shard_map/all_to_all | solution.py:511
  217.1 5.1 %copy-start.1 = (bf16[2000,192]{0,1:T(8,128)(2,1)S(1)}, bf16[2000,192]{0,1:T(8,128)(2,1)}, u32[]{:S(2)}) copy-start(bf16[2000,192]{0,1:T(8,128)(2,1)} %param.18) | copy-start | bytes 2304004
Sparse Core Ops, SparseCore 0:
  11.5 98.9 all-gather.2
  113.8 41.0 reduce-scatter.1

commit v4 on v3

--- a/solution.py
+++ b/solution.py
@@ -193,7 +193,7 @@
 
 
 def mlp_slot(n_two, c, wi, wb, b):
-    pre = dot_nt(n_two, wi) + b
+    pre = dot_nn(n_two, wi) + b
     d_act = dot_nt(c, wb)
     act, slope = gelu_both(pre)
     act = act.astype(BF16)
@@ -202,7 +202,7 @@
 
 
 def mlp_own(n_two, c, wi, wb, vecs, out_ref, dn2_ref, grad_ref, gbin_ref, acc, sums):
-    hid = wi.shape[0]
+    hid = wb.shape[0]
 
     @pl.when(pl.program_id(0) == 0)
     def _():
@@ -212,7 +212,7 @@
     act, d_pre = mlp_slot(n_two[...], c[...], wi[...], wb[...], vecs[6:7, :])
     sums[...] += fold8(d_pre.astype(F32))
     out_ref[...] = dot_nn(act, wb[...]).astype(BF16)
-    dn2_ref[...] = dot_nn(d_pre, wi[...]).astype(BF16)
+    dn2_ref[...] = dot_nt(d_pre, wi[...]).astype(BF16)
     acc[:, :hid] += dot_tn(n_two[...], d_pre)
     acc[:, hid:] += dot_tn(c[...], act)
 
@@ -222,28 +222,8 @@
         gbin_ref[...] = jnp.sum(sums[...], axis=0, keepdims=True)
 
 
-def mlp_rest(
-    slots, n_two, c, middle, out_in, dn2_in, vecs, w1, w2, w3, b,
-    out_ref, dmid_ref, sums_ref, sums,
-):
-    hid = b.shape[-1]
-    start_sums(sums)
-    out = out_in[...].astype(F32)
-    dn2 = dn2_in[...].astype(F32)
-    for k, w in enumerate((w1, w2, w3)):
-        act, d_pre = mlp_slot(
-            n_two[...], c[...], w[0, :hid, :], w[0, hid:, :], b[k : k + 1, :]
-        )
-        out = out + dot_nn(act, w[0, hid:, :])
-        dn2 = dn2 + dot_nn(d_pre, w[0, :hid, :])
-    mid = middle[...]
-    cot = c[...].astype(F32)
-    out_ref[...] = (mid + out + vecs[5:6, :]).astype(BF16)
-    xhat, inv = normed(mid)
-    d_mid = cot + norm_back(dn2, vecs[2:3, :], xhat, inv)
-    dmid_ref[...] = d_mid
-    add_sums(sums, (dn2 * xhat, dn2, d_mid, cot))
-    end_sums(sums, sums_ref)
+def total(rows):
+    return jnp.sum(rows, axis=0, keepdims=True)
 
 
 def start_sums(sums):
@@ -289,18 +269,39 @@
     return dot_nn(dqkv[...], wqkv[...])
 
 
-def back_first(
-    core, dmid, n_one, mix, qkv, p, own, mine, other, dn1_ref, grad_ref, sums_ref,
-    wqkv, wo, dqkv, dmix, acc, sums,
+def rest_and_back(
+    slots, n_two, c, middle, out_in, dn2_in, vecs, w1, w2, w3, b,
+    n_one, mix, qkv, p, own, mine, other, gbin, steps,
+    out_ref, dmid_ref, dn1_ref, grad_ref, more_ref,
+    sums, wqkv, wo, dqkv, dmix, acc, bias_sums,
 ):
     @pl.when(pl.program_id(0) == 0)
     def _():
         load_own(own, wqkv, wo, 0)
-        load_pieces(core[0], mine, other, 0, wqkv, wo, 1)
+        load_pieces(slots[4], mine, other, 0, wqkv, wo, 1)
         acc[...] = jnp.zeros_like(acc)
 
     start_sums(sums)
-    dml = dmid[...].astype(BF16)
+    start_sums(bias_sums)
+
+    dim = n_two.shape[1]
+    out = out_in[...].astype(F32)
+    dn2 = dn2_in[...].astype(F32)
+    for k, w in enumerate((w1, w2, w3)):
+        act, d_pre = mlp_slot(
+            n_two[...], c[...], w[0, :dim, :], w[0, dim:, :], b[k : k + 1, :]
+        )
+        out = out + dot_nn(act, w[0, dim:, :])
+        dn2 = dn2 + dot_nt(d_pre, w[0, :dim, :])
+    mid = middle[...]
+    cot = c[...].astype(F32)
+    out_ref[...] = (mid + out + vecs[5:6, :]).astype(BF16)
+    xhat, inv = normed(mid)
+    d_mid = cot + norm_back(dn2, vecs[2:3, :], xhat, inv)
+    dmid_ref[...] = d_mid
+    add_sums(sums, (dn2 * xhat, dn2, d_mid, cot))
+
+    dml = d_mid.astype(BF16)
     dn1_ref[...] = attend_back(dml, qkv, p, wqkv, wo, dqkv, dmix).astype(dn1_ref.dtype)
     width = wo.shape[0]
     for t in range(3):
@@ -308,24 +309,34 @@
             n_one[...], dqkv[:, t * width : t * width + 256]
         )
     acc[:, 768:] += dot_tn(dml, mix[:, :256])
-    add_sums(sums, (dqkv[...].astype(F32),))
-    end_sums(sums, sums_ref)
+    add_sums(bias_sums, (dqkv[...].astype(F32),))
 
     @pl.when(pl.program_id(0) == pl.num_programs(0) - 1)
     def _():
+        for r in range(4):
+            more_ref[r : r + 1, :] = total(sums[8 * r : 8 * r + 8, :])
+        more_ref[4:6, :] = jnp.zeros_like(more_ref[4:6, :])
+        more_ref[6:7, :] = gbin[...]
+        more_ref[7:8, :] = steps[...]
+        bias = total(bias_sums[...])
+        more_ref[7:8, :256] = bias[:, :256]
+        more_ref[7:8, 512:] = bias[:, 2 * width : 2 * width + 256]
         hc = HEADS * HEAD
         for t in range(4):
             grad_ref[:, t * hc : (t + 1) * hc] = acc[:, t * 256 : t * 256 + hc].astype(BF16)
 
 
 def back_last(
-    core, tok, time, dmid, dn1, vecs, qkv, p, mine, other, more,
-    gtok_ref, terms_ref, wqkv, wo, dqkv, dmix, sums,
+    places, tok, time, dmid, dn1, vecs, qkv, p, mine, other, more, mlp_sums,
+    gtok_ref, terms_ref, gwin_ref, gwback_ref, wqkv, wo, dqkv, dmix, sums, per,
 ):
     @pl.when(pl.program_id(0) == 0)
     def _():
-        load_pieces(core[0], mine, other, 0, wqkv, wo, 0)
-        load_pieces(core[0], mine, other, 1, wqkv, wo, 1)
+        load_pieces(places[4], mine, other, 0, wqkv, wo, 0)
+        load_pieces(places[4], mine, other, 1, wqkv, wo, 1)
+        hid = gwin_ref.shape[1]
+        gwin_ref[...] = mlp_sums[:, :hid].astype(F32)
+        gwback_ref[...] = mlp_sums[:, hid:].astype(F32)
 
     start_sums(sums)
     d_mid = dmid[...]
@@ -337,17 +348,23 @@
     gtok_ref[...] = d_entry.astype(BF16)
     n = d_entry.shape[0] // LEN
     at = pl.multiple_of(pl.program_id(0) * n, 8)
-    terms_ref[pl.ds(at, n), :] = jnp.sum(d_entry.reshape(n, LEN, -1), axis=1)
+    per[pl.ds(at, n), :] = jnp.sum(d_entry.reshape(n, LEN, -1), axis=1)
     add_sums(sums, (d_n * xhat, d_n))
 
     @pl.when(pl.program_id(0) == pl.num_programs(0) - 1)
     def _():
-        total = n * pl.num_programs(0)
-        terms_ref[pl.ds(pl.multiple_of(total, 8), 8), :] = more[...]
-        for k in range(2):
-            terms_ref[pl.ds(total + 4 + k, 1), :] = jnp.sum(
-                sums[8 * k : 8 * k + 8, :], axis=0, keepdims=True
-            )
+        cols = per.shape[1] // 4
+        own = per[:, :cols]
+        for j in range(1, 4):
+            own = jnp.where(places[0] == j, per[:, j * cols : (j + 1) * cols], own)
+        for j in range(4):
+            terms_ref[0, :8, j * cols : (j + 1) * cols] = own[8 * j : 8 * j + 8, :]
+        terms_ref[0, 8:12, :] = more[0:4, :]
+        terms_ref[0, 12:13, :] = total(sums[0:8, :])
+        terms_ref[0, 13:14, :] = total(sums[8:16, :])
+        terms_ref[0, 14:16, :] = more[6:8, :]
+        for k in range(1, terms_ref.shape[0]):
+            terms_ref[k] = terms_ref[0]
 
 
 def call(kernel, grid, in_specs, out_specs, out_shape, scratch, slots, args, flops):
@@ -421,15 +438,27 @@
         time_slots = picked_rows(lax.all_gather(own_rows, "tensor", axis=0), order)
         bias_slots = picked_rows(lax.all_gather(own_bias, "tensor", axis=0), order)
 
-    wi_own = w_in.T
-    mlp_shard = jnp.concatenate([wi_own, w_back], axis=0)
-    n_mlp = mlp_shard.shape[0] // dp
-    mlp_all = lax.all_gather(
-        lax.dynamic_slice_in_dim(mlp_shard, part * n_mlp, n_mlp, 0),
-        ("tensor", "dp"), axis=0, tiled=True,
-    ).reshape(n_tensor, mlp_shard.shape[0], dim)
-
-    time_rows = jnp.transpose(picked_rows(time_slots, order), (1, 0, 2))
+    n_mlp = (dim + hid) // dp
+    if fast:
+        first = dim // n_mlp
+        up = lax.dynamic_slice_in_dim(w_in, jnp.minimum(part, first - 1) * n_mlp, n_mlp, 0)
+        down = lax.dynamic_slice_in_dim(w_back, jnp.maximum(part - first, 0) * n_mlp, n_mlp, 0)
+        mlp_piece = jnp.where(part < first, up, down)
+    else:
+        mlp_piece = lax.dynamic_slice_in_dim(
+            jnp.concatenate([w_in, w_back]), part * n_mlp, n_mlp, 0
+        )
+    mlp_all = lax.all_gather(mlp_piece, ("tensor", "dp"), axis=0, tiled=True)
+    mlp_all = mlp_all.reshape(n_tensor, dim + hid, dim)
+
+    time_rows = jnp.concatenate([time_slots[k] for k in range(n_tensor)], axis=1)
+    for bit in range(n_tensor.bit_length() - 1):
+        step = hc << bit
+        swapped = jnp.concatenate(
+            [time_rows[:, (j ^ 1) * step : ((j ^ 1) + 1) * step] for j in range(dim // step)],
+            axis=1,
+        )
+        time_rows = jnp.where((me >> bit) % 2 == 1, swapped, time_rows)
     time_rows = time_rows.reshape(nb, BR // LEN, dim)
     bq, bv = bias_slots[:, 0].reshape(2, -1), bias_slots[:, 1].reshape(2, -1)
     bias_rows = jnp.concatenate([bq, jnp.zeros_like(bq), bv], axis=1)
@@ -472,12 +501,12 @@
     )
     out_acc, dn2_acc, mlp_grads, gbin = call(
         mlp_own, grid,
-        [rows_spec(dim), rows_spec(dim), whole_spec((hid, dim)), whole_spec((hid, dim)), vec],
+        [rows_spec(dim), rows_spec(dim), whole_spec((dim, hid)), whole_spec((hid, dim)), vec],
         [rows_spec(dim), rows_spec(dim), whole_spec((dim, 2 * hid)), whole_spec((1, hid))],
         [sds((rows, dim), BF16), sds((rows, dim), BF16), sds((dim, 2 * hid), BF16),
          sds((1, hid), F32)],
         [pltpu.VMEM((dim, 2 * hid), F32), pltpu.VMEM((8, hid), F32)], None,
-        (n_two, cotangent, wi_own, w_back, vecs), 21 * unit,
+        (n_two, cotangent, w_in, w_back, vecs), 21 * unit,
     )
 
     def scattered(grad):
@@ -485,61 +514,60 @@
 
     mlp_grads, mlp_all = lax.optimization_barrier((mlp_grads, mlp_all))
     mlp_grads = scattered(mlp_grads)
-    mlp_spec = lambda k: slot_spec((2 * hid, dim), k)
-    output, d_mid, sums_two = call(
-        mlp_rest, grid,
+    mlp_spec = lambda k: slot_spec((dim + hid, dim), k)
+    places = jnp.concatenate([me ^ jnp.arange(n_tensor, dtype=jnp.int32), core])
+    spread_steps = jnp.pad(timesteps.astype(F32), (256, dim - 256 - sentences)).reshape(1, dim)
+    output, d_mid, dn1_acc, att_grads, more = call(
+        rest_and_back, grid,
         [rows_spec(dim), rows_spec(dim), rows_spec(dim), rows_spec(dim), rows_spec(dim), vec,
-         mlp_spec(1), mlp_spec(2), mlp_spec(3), whole_spec((3, hid))],
-        [rows_spec(dim), rows_spec(dim), whole_spec((4, dim))],
-        [sds((rows, dim), BF16), sds((rows, dim), F32), sds((4, dim), F32)],
-        [pltpu.VMEM((32, dim), F32)], me ^ jnp.arange(n_tensor, dtype=jnp.int32),
-        (n_two, cotangent, middle, out_acc, dn2_acc, vecs, mlp_all, mlp_all, mlp_all, bi_rest),
-        44 * unit,
-    )
-    dn1_acc, att_grads, sums_qkv = call(
-        back_first, grid,
-        [rows_spec(dim), rows_spec(dim), rows_spec(width), rows_spec(3 * width),
-         rows_spec(width), own_spec, piece_spec(1), piece_spec(1)],
-        [rows_spec(dim), whole_spec((dim, 4 * hc)), whole_spec((1, 3 * width))],
-        [sds((rows, dim), BF16), sds((dim, 4 * hc), BF16), sds((1, 3 * width), F32)],
-        weights + back
+         mlp_spec(1), mlp_spec(2), mlp_spec(3), whole_spec((3, hid)),
+         rows_spec(dim), rows_spec(width), rows_spec(3 * width), rows_spec(width), own_spec,
+         piece_spec(1), piece_spec(1), whole_spec((1, dim)), whole_spec((1, dim))],
+        [rows_spec(dim), rows_spec(dim), rows_spec(dim), whole_spec((dim, 4 * hc)), vec],
+        [sds((rows, dim), BF16), sds((rows, dim), F32), sds((rows, dim), BF16),
+         sds((dim, 4 * hc), BF16), sds((8, dim), F32)],
+        [pltpu.VMEM((32, dim), F32)] + weights + back
         + [pltpu.VMEM((dim, 1024), F32), pltpu.VMEM((8, 3 * width), F32)],
-        core,
-        (d_mid, n_one, mix_a, qkv_a, p_a, att_own, mine_a, other_a), 18 * unit,
-    )
+        places,
+        (n_two, cotangent, middle, out_acc, dn2_acc, vecs, mlp_all, mlp_all, mlp_all, bi_rest,
+         n_one, mix_a, qkv_a, p_a, att_own, mine_a, other_a, gbin, spread_steps),
+        62 * unit,
+    )
+    copies = dp if fast else 1
     if fast:
         parts = lax.all_to_all(
             att_grads.reshape(dp, dim // dp, 4 * hc), "dp", 0, 0, tiled=True
         )
     else:
         att_grads = scattered(att_grads).astype(F32)
-    bias_row = jnp.concatenate(
-        [sums_qkv[:, :256], timesteps.astype(F32).reshape(1, -1),
-         jnp.zeros((1, dim - 512 - sentences), F32), sums_qkv[:, 2 * width : 2 * width + 256]],
-        axis=1,
-    )
-    more = jnp.concatenate([sums_two, jnp.zeros((2, dim), F32), gbin, bias_row])
-    grad_win = mlp_grads[:, :hid].astype(F32)
-    grad_wback = mlp_grads[:, hid:].astype(F32).T
-    dn1_acc, grad_win, grad_wback = lax.optimization_barrier((dn1_acc, grad_win, grad_wback))
-    grad_tokens, terms = call(
+    grad_tokens, terms, grad_win, grad_wback = call(
         back_last, grid,
         [rows_spec(dim), time_spec, rows_spec(dim), rows_spec(dim), vec,
-         rows_spec(3 * width), rows_spec(width), piece_spec(2), piece_spec(2), vec],
-        [rows_spec(dim), whole_spec((sentences + 8, dim))],
-        [sds((rows, dim), BF16), sds((sentences + 8, dim), F32)],
-        weights + back + [pltpu.VMEM((16, dim), F32)], core,
-        (tokens, time_rows, d_mid, dn1_acc, vecs, qkv_b, p_b, mine_b, other_b, more), 20 * unit,
-    )
+         rows_spec(3 * width), rows_spec(width), piece_spec(2), piece_spec(2), vec,
+         whole_spec(mlp_grads.shape)],
+        [rows_spec(dim), whole_spec((copies, 16, dim)),
+         whole_spec((dim // dp, hid)), whole_spec((dim // dp, hid))],
+        [sds((rows, dim), BF16), sds((copies, 16, dim), F32),
+         sds((dim // dp, hid), F32), sds((dim // dp, hid), F32)],
+        weights + back + [pltpu.VMEM((16, dim), F32), pltpu.VMEM((sentences, dim), F32)],
+        places,
+        (tokens, time_rows, d_mid, dn1_acc, vecs, qkv_b, p_b, mine_b, other_b, more, mlp_grads),
+        20 * unit,
+    )
+
     if fast:
         terms, parts = lax.optimization_barrier((terms, parts))
+        terms = lax.all_to_all(terms, "dp", 0, 0, tiled=True)
+    else:
+        terms = lax.all_gather(terms, "dp", axis=0, tiled=True)
+    if fast:
         att_grads = jnp.sum(parts.astype(F32), axis=0)
-    terms = lax.all_gather(terms, "dp", axis=0)
-    all_cols = lax.dynamic_slice_in_dim(
-        terms[:, :sentences], me * table_cols, table_cols, 2
-    ).reshape(-1, table_cols)
-    small = jnp.sum(terms[:, sentences:], axis=0)
-    all_steps = terms[:, -1, 256 : 256 + sentences].astype(jnp.int32).reshape(-1)
+    grad_wqkv = att_grads[:, : 3 * hc].reshape(-1, 3, hc)
+    grad_wout = att_grads[:, 3 * hc :].T
+    all_cols = terms[:, :8].reshape(-1, table_cols)
+    small = jnp.sum(terms[:, 8:], axis=0)
+    all_steps = terms[:, -1, 256 : 256 + sentences].astype(jnp.int32)
+    all_steps = jnp.transpose(all_steps.reshape(dp, 4, 8), (0, 2, 1)).reshape(-1)
     all_picked = all_steps[:, None] == lax.broadcasted_iota(
         jnp.int32, (all_steps.shape[0], time_table.shape[0]), 1
     )
@@ -547,12 +575,10 @@
         all_picked.astype(F32), all_cols, (((0,), (0,)), ((), ())),
         precision=HIGHEST_PREC, preferred_element_type=F32,
     )
-    grad_wqkv = att_grads[:, : 3 * hc].reshape(-1, 3, hc)
-    grad_wout = att_grads[:, 3 * hc :].T
     grad_bqv = jnp.stack([small[7, :hc], small[7, dim - 256 : dim - 256 + hc]])
     return (
         output, grad_tokens, grad_table, grad_wqkv, grad_bqv, grad_wout, small[2], grad_win,
-        small[6], grad_wback, small[3], small[4], small[5], small[0], small[1],
+        small[6], grad_wback.T, small[3], small[4], small[5], small[0], small[1],
     )
 
 

time: 230 us -> 222 us (0.965)
  blocking collectives: 12 us -> 0 us
  waiting for transfers between devices: 24.1 us -> 29.2 us
  starting transfers between devices: 17.7 us -> 20.9 us
  Pallas kernels: 141 us -> 138 us
    all_gather x1 -> x0, blocking collectives: 12 us -> none  [body(): terms = lax.all_gather(terms, 'dp', axis=0)]
    all_to_all x0 -> x1, waiting for transfers between devices: none -> 6.28 us  [body(): terms = lax.all_to_all(terms, 'dp', 0, 0, tiled=True)]
    all_to_all x0 -> x1, starting transfers between devices: none -> 4.1 us  [body(): terms = lax.all_to_all(terms, 'dp', 0, 0, tiled=True)]
    select_n x0 -> x3, other arithmetic: none -> 2.87 us  [the longest x1 2 us: body(): mlp_piece = jnp.where(part < first, up, down)]
    pallas_call x5 -> x4, Pallas kernels: 118 us -> 115 us  [call(): pl.pallas_call(kernel, grid_spec=pltpu.PrefetchScalarGridSpec(num_scalar_...]
  transfers between devices with their start and end apart: 10 -> 11, of which waited for: 6 -> 7; matrix products, arithmetic and copies ran while one was open for 5% -> 6% of each run, Pallas kernels for 61% -> 62%
where the time goes in v4:
time: 222 us
  Pallas kernels  138 us (62%)
  waiting for transfers between devices  29.2 us (13%)
  starting transfers between devices  20.9 us (9%)
  between operations  14.6 us (7%)
  local copies, waits for them, and re-layouts  8.84 us (4%)
  other arithmetic  7.85 us (4%)
  matrix products  2.61 us (1%)
    pallas_call x4, Pallas kernels, call(): pl.pallas_call(kernel, grid_spec=pltpu.PrefetchScalarGridSpec(num_scalar_...  115 us
    pallas_call x1, Pallas kernels, call(): pl.pallas_call(kernel, grid=grid, in_specs=in_specs, out_specs=out_specs,...  22.8 us
    ppermute x3, waiting for transfers between devices, body(): got = [lax.ppermute(message, 'tensor', flipped(4, k)) for k in (1, 2, 3)]  10.8 us
    all_to_all x2, waiting for transfers between devices, spread_plane(): lax.all_to_all(whole, 'dp', 0, 0, tiled=True, axis_index_groups=[[0, 2, 4...  7.49 us
    all_to_all x2, starting transfers between devices, spread_plane(): lax.all_to_all(whole, 'dp', 0, 0, tiled=True, axis_index_groups=[[0, 2, 4...  7.42 us
    all_to_all x1, waiting for transfers between devices, body(): terms = lax.all_to_all(terms, 'dp', 0, 0, tiled=True)  6.28 us
    ppermute x3, starting transfers between devices, body(): got = [lax.ppermute(message, 'tensor', flipped(4, k)) for k in (1, 2, 3)]  5.68 us
  transfers between devices with their start and end apart: 11, of which 7 were waited for; matrix products, arithmetic and copies ran while one was open for 6% of the time, Pallas kernels for 62%

profile of v4, /device:TPU:0, one launch (start us, length us, event | category | flops | bytes accessed | tf_op | source)
XLA Modules:
  0.0 221.9 jit_solution(14126432178620858752)
XLA Ops:
  7.2 0.0 copy-start
  7.2 0.0 copy-start.6
  7.2 0.0 copy-start.3
  7.2 0.0 copy-start.2
  7.3 0.0 all-gather.2.cloned.1.call-start
  7.4 2.0 dynamic-slice_select_fusion
  9.4 0.0 all-gather.2.cloned.1.call-update
  9.4 0.8 reshape.79
  10.2 0.7 fusion.15
  10.9 1.0 fusion.3
  11.9 0.4 fusion.22
  12.3 0.1 maximum_maximum_fusion
  12.4 3.1 %collective-permute-start = (bf16[128,768]{1,0:T(8,128)(2,1)S(1)}, bf16[128,768]{1,0:T(8,128)(2,1)S(1)}, u32[]{:S(2)}, u32[]{:S(2)}) collective-permute-start(bf16[128,768]{1,0:T(8,128)(2,1)S(1)} %maximum_maximum_fusion), channel_id=1, source_target_pairs={{0,1},{1,0},{2,3},{3,2},{4,5},{5,4},{6,7},{7,6},{8,9},{9,8},{10,11... | collective-permute-start | bytes 589832 | tf_op jit(solution)/shard_map/ppermute | solution.py:427
  15.5 2.6 %collective-permute-start.2 = (bf16[128,768]{1,0:T(8,128)(2,1)S(1)}, bf16[128,768]{1,0:T(8,128)(2,1)S(1)}, u32[]{:S(2)}, u32[]{:S(2)}) collective-permute-start(bf16[128,768]{1,0:T(8,128)(2,1)S(1)} %maximum_maximum_fusion), channel_id=1, source_target_pairs={{0,2},{1,3},{2,0},{3,1},{4,6},{5,7},{6,4},{7,5},{8,10},{9,11},{10,... | collective-permute-start | bytes 589832 | tf_op jit(solution)/shard_map/ppermute | solution.py:427
  18.1 0.0 collective-permute-start.1
  18.3 0.6 stack.63.vecs
  18.9 1.1 pad_maximum_fusion.own
  20.0 3.8 %collective-permute-done = bf16[128,768]{1,0:T(8,128)(2,1)S(1)} collective-permute-done((bf16[128,768]{1,0:T(8,128)(2,1)S(1)}, bf16[128,768]{1,0:T(8,128)(2,1)S(1)}, u32[]{:S(2)}, u32[]{:S(2)}) %collective-permute-start) | collective-permute-done | bytes 196640 | tf_op jit(solution)/shard_map/ppermute | solution.py:427
  23.8 0.9 broadcast_in_dim.24
  24.7 3.9 %all-to-all-start.1 = ((bf16[4,1,96,768]{3,2,1,0:T(8,128)(2,1)}), bf16[4,1,96,768]{3,2,1,0:T(8,128)(2,1)S(1)}, u32[]{:S(2)}, u32[]{:S(2)}) async-start(bf16[4,1,96,768]{3,2,1,0:T(8,128)(2,1)} %broadcast_in_dim.24), calls=%async_computation.1 | async-start | bytes 1179648 | tf_op jit(solution)/shard_map/all_to_all | solution.py:610
  28.6 7.0 %collective-permute-done.2 = bf16[128,768]{1,0:T(8,128)(2,1)S(1)} collective-permute-done((bf16[128,768]{1,0:T(8,128)(2,1)S(1)}, bf16[128,768]{1,0:T(8,128)(2,1)S(1)}, u32[]{:S(2)}, u32[]{:S(2)}) %collective-permute-start.2) | collective-permute-done | bytes 196640 | tf_op jit(solution)/shard_map/ppermute | solution.py:427
  35.6 0.0 collective-permute-done.1
  35.7 0.1 maximum_select_fusion
  35.9 0.4 all-to-all-done.1.mine
  36.3 0.0 collective-permute-start.3
  36.3 0.1 reshape_squeeze.6
  36.4 0.1 reshape_squeeze.7
  36.5 1.1 broadcast_in_dim.23
  37.7 3.5 %all-to-all-start = ((bf16[4,2,96,768]{3,2,1,0:T(8,128)(2,1)}), bf16[4,2,96,768]{3,2,1,0:T(8,128)(2,1)S(1)}, u32[]{:S(2)}, u32[]{:S(2)}) async-start(bf16[4,2,96,768]{3,2,1,0:T(8,128)(2,1)} %broadcast_in_dim.23), calls=%async_computation | async-start | bytes 2359296 | tf_op jit(solution)/shard_map/all_to_all | solution.py:610
  41.2 0.0 reduce-scatter.2.cloned.1.call-start
  41.2 0.8 maximum_select_fusion.1.time
  42.0 0.6 pad_maximum_fusion.4.bias
  42.6 0.0 collective-permute-done.3.other
  42.6 0.8 copy-done.14
  43.4 14.8 %shard_map.271 = (bf16[2048,768]{1,0:T(8,128)(2,1)}, bf16[2048,1152]{1,0:T(8,128)(2,1)}, bf16[2048,384]{1,0:T(8,128)(2,1)}, bf16[2048,384]{1,0:T(8,128)(2,1)}, bf16[2048,768]{1,0:T(8,128)(2,1)}) custom-call(s32[1]{0:T(128)} %bitcast.core, bf16[2048,768]{1,0:T(8,128)(2,1)} %tok.5, f32[4,8,768]{2,1,0:T(8,128)} %maximum_select_fusion.1.time, ...), custom_call_target="tpu_custom_call" | custom-call | flops 14000000000 | bytes 19792896 | tf_op jit(solution)/shard_map/pallas_call | solution.py:377
  58.3 7.1 %all-to-all-done.mine = bf16[4,2,96,768]{3,2,1,0:T(8,128)(2,1)S(1)} async-done(((bf16[4,2,96,768]{3,2,1,0:T(8,128)(2,1)}), bf16[4,2,96,768]{3,2,1,0:T(8,128)(2,1)S(1)}, u32[]{:S(2)}, u32[]{:S(2)}) %all-to-all-start) | async-done | bytes 1179680 | tf_op jit(solution)/shard_map/all_to_all | solution.py:610
  65.4 0.0 collective-permute-start.4
  65.4 0.6 reshape.82.steps
  66.0 0.6 pad_add_fusion.slots.places
  66.6 0.7 reshape.81.b
  67.3 1.0 collective-permute-done.4.other
  68.3 16.1 %shard_map.272 = (bf16[2048,1152]{1,0:T(8,128)(2,1)}, bf16[2048,384]{1,0:T(8,128)(2,1)}, f32[2048,768]{1,0:T(8,128)}, bf16[2048,768]{1,0:T(8,128)(2,1)}) custom-call(s32[1]{0:T(128)} %bitcast.core, bf16[2048,768]{1,0:T(8,128)(2,1)} %tok.5, f32[4,8,768]{2,1,0:T(8,128)} %maximum_select_fusion.1.time, bf16[2048,768]{1,0:T(8,128)(2,1)} %get-tuple-element.44.n_one, ...), custom_call_target="tpu_custom_call" | custom-call | flops 15000000512 | bytes 27657216 | tf_op jit(solution)/shard_map/pallas_call | solution.py:377
  84.4 22.8 %shard_map.273 = (bf16[2048,768]{1,0:T(8,128)(2,1)}, bf16[2048,768]{1,0:T(8,128)(2,1)}, bf16[768,1536]{1,0:T(8,128)(2,1)}, f32[1,768]{1,0:T(1,128)}) custom-call(bf16[2048,768]{1,0:T(8,128)(2,1)} %get-tuple-element.47.n_two, bf16[2048,768]{1,0:T(8,128)(2,1)} %c.3, bf16[768,768]{1,0:T(8,128)(2,1)} %wi.1, bf16[768,768]{1,0:T(8,128)(2,1)} %wb.1, ...), custom_call_target="tpu_custom_call" | custom-call | flops 20999999488 | bytes 17329152 | tf_op jit(solution)/shard_map/pallas_call | solution.py:372
  107.2 3.5 %all-gather.2.cloned.1.call-done = bf16[6144,768]{1,0:T(8,128)(2,1)} async-done(((bf16[192,768]{1,0:T(8,128)(2,1)}), bf16[6144,768]{1,0:T(8,128)(2,1)}) %all-gather.2.cloned.1.call-update) | async-done | bytes 9437200 | tf_op jit(solution)/shard_map/all_gather | solution.py:451
  110.7 0.0 reduce-scatter.2.cloned.1.call-update
  110.7 62.7 %shard_map.274 = (bf16[2048,768]{1,0:T(8,128)(2,1)}, f32[2048,768]{1,0:T(8,128)}, bf16[2048,768]{1,0:T(8,128)(2,1)}, bf16[768,768]{1,0:T(8,128)(2,1)}, f32[8,768]{1,0:T(8,128)}) custom-call(s32[5]{0:T(128)} %pad_add_fusion.slots.places, bf16[2048,768]{1,0:T(8,128)(2,1)} %get-tuple-element.47.n_two, bf16[2048,768]{1,0:T(8,128)(2,1)} %c.3, ...), custom_call_target="tpu_custom_call" | custom-call | flops 62000001024 | bytes 74382336 | tf_op jit(solution)/shard_map/pallas_call | solution.py:377
  173.4 3.6 %all-to-all-start.2 = ((bf16[8,96,768]{2,1,0:T(8,128)(2,1)}), bf16[8,96,768]{2,1,0:T(8,128)(2,1)S(1)}, u32[]{:S(2)}, u32[]{:S(2)}) async-start(bf16[8,96,768]{2,1,0:T(8,128)(2,1)} %bitcast.38), calls=%async_computation.3 | async-start | bytes 2359296 | tf_op jit(solution)/shard_map/all_to_all | solution.py:538
  177.0 0.0 reduce-scatter.2.cloned.1.call-done.mlp_sums
  177.0 21.5 %shard_map.275 = (bf16[2048,768]{1,0:T(8,128)(2,1)}, f32[8,16,768]{2,1,0:T(8,128)}, f32[96,768]{1,0:T(8,128)}, f32[96,768]{1,0:T(8,128)}) custom-call(s32[5]{0:T(128)} %pad_add_fusion.slots.places, bf16[2048,768]{1,0:T(8,128)(2,1)} %tok.5, f32[4,8,768]{2,1,0:T(8,128)} %maximum_select_fusion.1.time, f32[2048,768]{1,0:T(8,128)} %get-tuple-element.58.dmid, ...), custom_call_target="tpu_custom_call" | custom-call | flops 20000000000 | bytes 25804800 | tf_op jit(solution)/shard_map/pallas_call | solution.py:377
  198.6 4.1 %all-to-all-start.3 = ((f32[8,16,768]{2,1,0:T(8,128)}), f32[8,16,768]{2,1,0:T(8,128)S(1)}, u32[]{:S(2)}, u32[]{:S(2)}) async-start(f32[8,16,768]{2,1,0:T(8,128)} %get-tuple-element.67), calls=%async_computation.4 | async-start | bytes 786432 | tf_op jit(solution)/shard_map/all_to_all | solution.py:560
  202.7 0.2 convert_reduce_fusion
  202.9 0.1 slice_bitcast_fusion.2
  203.0 0.0 copy-start.1
  203.0 0.7 copy.36
  203.7 0.1 copy.34
  203.9 0.9 copy.35
  204.7 6.3 %all-to-all-done.3 = f32[8,16,768]{2,1,0:T(8,128)S(1)} async-done(((f32[8,16,768]{2,1,0:T(8,128)}), f32[8,16,768]{2,1,0:T(8,128)S(1)}, u32[]{:S(2)}, u32[]{:S(2)}) %all-to-all-start.3) | async-done | bytes 393248 | tf_op jit(solution)/shard_map/all_to_all | solution.py:560
  211.1 0.7 slice_reduce_fusion.1
  211.7 0.1 convert_element_type.61
  211.8 0.1 copy.33
  211.9 0.1 eq.32
  212.1 0.1 reshape.84
  212.2 0.6 pad_maximum_fusion.9
  212.8 2.2 %fusion = f32[2000,192]{0,1:T(8,128)} fusion(f32[256,192]{1,0:T(8,128)S(1)} %reshape.84, s32[256]{0:T(256)S(1)} %eq.32), kind=kOutput, calls=%fused_computation.2 | convolution fusion | flops 1180160000 | bytes 1733632 | tf_op jit(solution)/shard_map/dot_general | solution.py:574
  (57 shorter events, 0.4 us)
Async XLA Ops:
  7.2 4.7 %copy-start = (bf16[2000,192]{0,1:T(8,128)(2,1)S(1)}, bf16[2000,192]{0,1:T(8,128)(2,1)}, u32[]{:S(2)}) copy-start(bf16[2000,192]{0,1:T(8,128)(2,1)} %param.18) | copy-start | bytes 2304004
  7.2 10.9 %copy-start.6 = (f32[768]{0:T(1024)S(1)}, f32[768]{0:T(1024)}, u32[]{:S(2)}) copy-start(f32[768]{0:T(1024)} %param.24) | copy-start | bytes 9220
  7.2 11.7 %copy-start.3 = (bf16[192,768]{1,0:T(8,128)(2,1)S(1)}, bf16[192,768]{1,0:T(8,128)(2,1)}, u32[]{:S(2)}) copy-start(bf16[192,768]{1,0:T(8,128)(2,1)} %param.21) | copy-start | bytes 884740
  7.2 11.7 %copy-start.2 = (bf16[768,3,192]{0,2,1:T(8,128)(2,1)S(1)}, bf16[768,3,192]{0,2,1:T(8,128)(2,1)}, u32[]{:S(2)}) copy-start(bf16[768,3,192]{0,2,1:T(8,128)(2,1)} %param.19) | copy-start | bytes 2654212
  7.2 4.6 %copy-start.13 = (s32[32]{0:T(128)S(1)}, s32[32]{0:T(128)}, u32[]{:S(2)}) copy-start(s32[32]{0:T(128)} %param.17) | copy-start | bytes 388
  7.2 10.8 %copy-start.7 = (f32[768]{0:T(1024)S(1)}, f32[768]{0:T(1024)}, u32[]{:S(2)}) copy-start(f32[768]{0:T(1024)} %param.22) | copy-start | bytes 9220
  7.3 10.9 %copy-start.8 = (f32[768]{0:T(1024)S(1)}, f32[768]{0:T(1024)}, u32[]{:S(2)}) copy-start(f32[768]{0:T(1024)} %param.26) | copy-start | bytes 9220
  7.3 10.9 %copy-start.9 = (f32[768]{0:T(1024)S(1)}, f32[768]{0:T(1024)}, u32[]{:S(2)}) copy-start(f32[768]{0:T(1024)} %param.27) | copy-start | bytes 9220
  7.3 10.9 %copy-start.10 = (f32[768]{0:T(1024)S(1)}, f32[768]{0:T(1024)}, u32[]{:S(2)}) copy-start(f32[768]{0:T(1024)} %param.28) | copy-start | bytes 9220
  7.3 10.9 %copy-start.11 = (f32[768]{0:T(1024)S(1)}, f32[768]{0:T(1024)}, u32[]{:S(2)}) copy-start(f32[768]{0:T(1024)} %param.29) | copy-start | bytes 9220
  7.3 10.9 %copy-start.12 = (f32[768]{0:T(1024)S(1)}, f32[768]{0:T(1024)}, u32[]{:S(2)}) copy-start(f32[768]{0:T(1024)} %param.30) | copy-start | bytes 9220
  7.3 103.4 %all-gather.2.cloned.1.call-start = ((), (), s32[]{:S(2)}) async-start(), calls=%async_computation.5 | async-start | bytes 9732096 | tf_op jit(solution)/shard_map/all_gather | solution.py:451
  12.4 11.4 %collective-permute-start = (bf16[128,768]{1,0:T(8,128)(2,1)S(1)}, bf16[128,768]{1,0:T(8,128)(2,1)S(1)}, u32[]{:S(2)}, u32[]{:S(2)}) collective-permute-start(bf16[128,768]{1,0:T(8,128)(2,1)S(1)} %maximum_maximum_fusion), channel_id=1, source_target_pairs={{0,1},{1,0},{2,3},{3,2},{4,5},{5,4},{6,7},{7,6},{8,9},{9,8},{10,11... | collective-permute-start | bytes 589832 | tf_op jit(solution)/shard_map/ppermute | solution.py:427
  15.5 20.2 %collective-permute-start.2 = (bf16[128,768]{1,0:T(8,128)(2,1)S(1)}, bf16[128,768]{1,0:T(8,128)(2,1)S(1)}, u32[]{:S(2)}, u32[]{:S(2)}) collective-permute-start(bf16[128,768]{1,0:T(8,128)(2,1)S(1)} %maximum_maximum_fusion), channel_id=1, source_target_pairs={{0,2},{1,3},{2,0},{3,1},{4,6},{5,7},{6,4},{7,5},{8,10},{9,11},{10,... | collective-permute-start | bytes 589832 | tf_op jit(solution)/shard_map/ppermute | solution.py:427
  18.1 17.6 %collective-permute-start.1 = (bf16[128,768]{1,0:T(8,128)(2,1)S(1)}, bf16[128,768]{1,0:T(8,128)(2,1)S(1)}, u32[]{:S(2)}, u32[]{:S(2)}) collective-permute-start(bf16[128,768]{1,0:T(8,128)(2,1)S(1)} %maximum_maximum_fusion), channel_id=1, source_target_pairs={{0,3},{1,2},{2,1},{3,0},{4,7},{5,6},{6,5},{7,4},{8,11},{9,10},{10,... | collective-permute-start | bytes 589832 | tf_op jit(solution)/shard_map/ppermute | solution.py:427
  24.7 11.6 %all-to-all-start.1 = ((bf16[4,1,96,768]{3,2,1,0:T(8,128)(2,1)}), bf16[4,1,96,768]{3,2,1,0:T(8,128)(2,1)S(1)}, u32[]{:S(2)}, u32[]{:S(2)}) async-start(bf16[4,1,96,768]{3,2,1,0:T(8,128)(2,1)} %broadcast_in_dim.24), calls=%async_computation.1 | async-start | bytes 1179648 | tf_op jit(solution)/shard_map/all_to_all | solution.py:610
  36.3 1.4 copy-start.5
  36.3 6.3 %collective-permute-start.3 = (bf16[4,1,96,768]{3,2,1,0:T(8,128)(2,1)S(1)}, bf16[4,1,96,768]{3,2,1,0:T(8,128)(2,1)S(1)}, u32[]{:S(2)}, u32[]{:S(2)}) collective-permute-start(bf16[4,1,96,768]{3,2,1,0:T(8,128)(2,1)S(1)} %all-to-all-done.1.mine), channel_id=1, source_target_pairs={{0,4},{4,0},{8,12},{12,8},{16,20},{20,16},{24,28},{28,24},{1,5},{5... | collective-permute-start | bytes 1769480 | tf_op jit(solution)/shard_map/ppermute | solution.py:430
  37.7 27.7 %all-to-all-start = ((bf16[4,2,96,768]{3,2,1,0:T(8,128)(2,1)}), bf16[4,2,96,768]{3,2,1,0:T(8,128)(2,1)S(1)}, u32[]{:S(2)}, u32[]{:S(2)}) async-start(bf16[4,2,96,768]{3,2,1,0:T(8,128)(2,1)} %broadcast_in_dim.23), calls=%async_computation | async-start | bytes 2359296 | tf_op jit(solution)/shard_map/all_to_all | solution.py:610
  41.2 135.8 %reduce-scatter.2.cloned.1.call-start = ((), (), s32[]{:S(2)}) async-start(), calls=%async_computation.6 | async-start | bytes 2654208 | tf_op jit(solution)/shard_map/reduce_scatter | solution.py:513
  42.6 0.8 copy-start.14
  65.4 3.0 %copy-start.4 = (bf16[4,2,96,768]{3,2,1,0:T(8,128)(2,1)}, bf16[4,2,96,768]{3,2,1,0:T(8,128)(2,1)S(1)}, u32[]{:S(2)}) copy-start(bf16[4,2,96,768]{3,2,1,0:T(8,128)(2,1)S(1)} %all-to-all-done.mine) | copy-start | bytes 3538948
  65.4 3.0 %collective-permute-start.4 = (bf16[4,2,96,768]{3,2,1,0:T(8,128)(2,1)S(1)}, bf16[4,2,96,768]{3,2,1,0:T(8,128)(2,1)}, u32[]{:S(2)}, u32[]{:S(2)}) collective-permute-start(bf16[4,2,96,768]{3,2,1,0:T(8,128)(2,1)S(1)} %all-to-all-done.mine), channel_id=1, source_target_pairs={{0,4},{4,0},{8,12},{12,8},{16,20},{20,16},{24,28},{28,24},{1,5},{5... | collective-permute-start | bytes 3538952 | tf_op jit(solution)/shard_map/ppermute | solution.py:491
  173.4 25.1 %all-to-all-start.2 = ((bf16[8,96,768]{2,1,0:T(8,128)(2,1)}), bf16[8,96,768]{2,1,0:T(8,128)(2,1)S(1)}, u32[]{:S(2)}, u32[]{:S(2)}) async-start(bf16[8,96,768]{2,1,0:T(8,128)(2,1)} %bitcast.38), calls=%async_computation.3 | async-start | bytes 2359296 | tf_op jit(solution)/shard_map/all_to_all | solution.py:538
  198.6 12.4 %all-to-all-start.3 = ((f32[8,16,768]{2,1,0:T(8,128)}), f32[8,16,768]{2,1,0:T(8,128)S(1)}, u32[]{:S(2)}, u32[]{:S(2)}) async-start(f32[8,16,768]{2,1,0:T(8,128)} %get-tuple-element.67), calls=%async_computation.4 | async-start | bytes 786432 | tf_op jit(solution)/shard_map/all_to_all | solution.py:560
  203.0 12.1 %copy-start.1 = (bf16[2000,192]{0,1:T(8,128)(2,1)S(1)}, bf16[2000,192]{0,1:T(8,128)(2,1)}, u32[]{:S(2)}) copy-start(bf16[2000,192]{0,1:T(8,128)(2,1)} %param.18) | copy-start | bytes 2304004
Sparse Core Ops, SparseCore 0:
  11.6 99.0 all-gather.1
  114.1 41.1 reduce-scatter.1

commit v5 on v4

--- a/solution.py
+++ b/solution.py
@@ -298,10 +298,10 @@
     out_ref[...] = (mid + out + vecs[5:6, :]).astype(BF16)
     xhat, inv = normed(mid)
     d_mid = cot + norm_back(dn2, vecs[2:3, :], xhat, inv)
-    dmid_ref[...] = d_mid
     add_sums(sums, (dn2 * xhat, dn2, d_mid, cot))
 
     dml = d_mid.astype(BF16)
+    dmid_ref[...] = dml
     dn1_ref[...] = attend_back(dml, qkv, p, wqkv, wo, dqkv, dmix).astype(dn1_ref.dtype)
     width = wo.shape[0]
     for t in range(3):
@@ -339,12 +339,9 @@
         gwback_ref[...] = mlp_sums[:, hid:].astype(F32)
 
     start_sums(sums)
-    d_mid = dmid[...]
-    d_n = dn1[...].astype(F32) + attend_back(
-        d_mid.astype(BF16), qkv, p, wqkv, wo, dqkv, dmix
-    )
+    d_n = dn1[...].astype(F32) + attend_back(dmid[...], qkv, p, wqkv, wo, dqkv, dmix)
     xhat, inv = normed(entry_of(tok, time))
-    d_entry = d_mid + norm_back(d_n, vecs[0:1, :], xhat, inv)
+    d_entry = dmid[...].astype(F32) + norm_back(d_n, vecs[0:1, :], xhat, inv)
     gtok_ref[...] = d_entry.astype(BF16)
     n = d_entry.shape[0] // LEN
     at = pl.multiple_of(pl.program_id(0) * n, 8)
@@ -524,8 +521,7 @@
          rows_spec(dim), rows_spec(width), rows_spec(3 * width), rows_spec(width), own_spec,
          piece_spec(1), piece_spec(1), whole_spec((1, dim)), whole_spec((1, dim))],
         [rows_spec(dim), rows_spec(dim), rows_spec(dim), whole_spec((dim, 4 * hc)), vec],
-        [sds((rows, dim), BF16), sds((rows, dim), F32), sds((rows, dim), BF16),
-         sds((dim, 4 * hc), BF16), sds((8, dim), F32)],
+        [sds((rows, dim), BF16)] * 3 + [sds((dim, 4 * hc), BF16), sds((8, dim), F32)],
         [pltpu.VMEM((32, dim), F32)] + weights + back
         + [pltpu.VMEM((dim, 1024), F32), pltpu.VMEM((8, 3 * width), F32)],
         places,

time: 222 us -> 222 us (level)
  no operation moved by 1% of the time
where the time goes in v5:
time: 222 us; the launch traced here: 221 us
  Pallas kernels  137 us (62%)
  waiting for transfers between devices  29.2 us (13%)
  starting transfers between devices  20.9 us (9%)
  between operations  14.6 us (7%)
  local copies, waits for them, and re-layouts  8.84 us (4%)
  other arithmetic  7.9 us (4%)
  matrix products  2.62 us (1%)
    pallas_call x4, Pallas kernels, call(): pl.pallas_call(kernel, grid_spec=pltpu.PrefetchScalarGridSpec(num_scalar_...  114 us
    pallas_call x1, Pallas kernels, call(): pl.pallas_call(kernel, grid=grid, in_specs=in_specs, out_specs=out_specs,...  22.8 us
    ppermute x3, waiting for transfers between devices, body(): got = [lax.ppermute(message, 'tensor', flipped(4, k)) for k in (1, 2, 3)]  10.8 us
    all_to_all x2, waiting for transfers between devices, spread_plane(): lax.all_to_all(whole, 'dp', 0, 0, tiled=True, axis_index_groups=[[0, 2, 4...  7.47 us
    all_to_all x2, starting transfers between devices, spread_plane(): lax.all_to_all(whole, 'dp', 0, 0, tiled=True, axis_index_groups=[[0, 2, 4...  7.42 us
    all_to_all x1, waiting for transfers between devices, body(): terms = lax.all_to_all(terms, 'dp', 0, 0, tiled=True)  6.28 us
    ppermute x3, starting transfers between devices, body(): got = [lax.ppermute(message, 'tensor', flipped(4, k)) for k in (1, 2, 3)]  5.68 us
  transfers between devices with their start and end apart: 11, of which 7 were waited for; matrix products, arithmetic and copies ran while one was open for 6% of the time, Pallas kernels for 62%

profile of v5, /device:TPU:0, one launch (start us, length us, event | category | flops | bytes accessed | tf_op | source)
XLA Modules:
  0.0 221.3 jit_solution(18138751217782379596)
XLA Ops:
  7.2 0.0 copy-start
  7.2 0.0 copy-start.6
  7.2 0.0 copy-start.3
  7.2 0.0 copy-start.2
  7.3 0.0 all-gather.2.cloned.1.call-start
  7.4 2.0 dynamic-slice_select_fusion
  9.4 0.0 all-gather.2.cloned.1.call-update
  9.4 0.8 reshape.79
  10.2 0.7 fusion.15
  10.9 1.0 fusion.3
  11.9 0.4 fusion.22
  12.3 0.1 maximum_maximum_fusion
  12.4 3.1 %collective-permute-start = (bf16[128,768]{1,0:T(8,128)(2,1)S(1)}, bf16[128,768]{1,0:T(8,128)(2,1)S(1)}, u32[]{:S(2)}, u32[]{:S(2)}) collective-permute-start(bf16[128,768]{1,0:T(8,128)(2,1)S(1)} %maximum_maximum_fusion), channel_id=1, source_target_pairs={{0,1},{1,0},{2,3},{3,2},{4,5},{5,4},{6,7},{7,6},{8,9},{9,8},{10,11... | collective-permute-start | bytes 589832 | tf_op jit(solution)/shard_map/ppermute | solution.py:424
  15.5 2.6 %collective-permute-start.2 = (bf16[128,768]{1,0:T(8,128)(2,1)S(1)}, bf16[128,768]{1,0:T(8,128)(2,1)S(1)}, u32[]{:S(2)}, u32[]{:S(2)}) collective-permute-start(bf16[128,768]{1,0:T(8,128)(2,1)S(1)} %maximum_maximum_fusion), channel_id=1, source_target_pairs={{0,2},{1,3},{2,0},{3,1},{4,6},{5,7},{6,4},{7,5},{8,10},{9,11},{10,... | collective-permute-start | bytes 589832 | tf_op jit(solution)/shard_map/ppermute | solution.py:424
  18.1 0.0 collective-permute-start.1
  18.3 0.6 stack.63.vecs
  18.9 1.1 pad_maximum_fusion.own
  20.1 3.7 %collective-permute-done = bf16[128,768]{1,0:T(8,128)(2,1)S(1)} collective-permute-done((bf16[128,768]{1,0:T(8,128)(2,1)S(1)}, bf16[128,768]{1,0:T(8,128)(2,1)S(1)}, u32[]{:S(2)}, u32[]{:S(2)}) %collective-permute-start) | collective-permute-done | bytes 196640 | tf_op jit(solution)/shard_map/ppermute | solution.py:424
  23.8 0.9 broadcast_in_dim.24
  24.7 3.9 %all-to-all-start.1 = ((bf16[4,1,96,768]{3,2,1,0:T(8,128)(2,1)}), bf16[4,1,96,768]{3,2,1,0:T(8,128)(2,1)S(1)}, u32[]{:S(2)}, u32[]{:S(2)}) async-start(bf16[4,1,96,768]{3,2,1,0:T(8,128)(2,1)} %broadcast_in_dim.24), calls=%async_computation.1 | async-start | bytes 1179648 | tf_op jit(solution)/shard_map/all_to_all | solution.py:606
  28.6 7.0 %collective-permute-done.2 = bf16[128,768]{1,0:T(8,128)(2,1)S(1)} collective-permute-done((bf16[128,768]{1,0:T(8,128)(2,1)S(1)}, bf16[128,768]{1,0:T(8,128)(2,1)S(1)}, u32[]{:S(2)}, u32[]{:S(2)}) %collective-permute-start.2) | collective-permute-done | bytes 196640 | tf_op jit(solution)/shard_map/ppermute | solution.py:424
  35.6 0.0 collective-permute-done.1
  35.7 0.1 maximum_select_fusion
  35.9 0.4 all-to-all-done.1.mine
  36.3 0.0 collective-permute-start.3
  36.3 0.1 reshape_squeeze.6
  36.4 0.1 reshape_squeeze.7
  36.5 1.1 broadcast_in_dim.23
  37.6 3.5 %all-to-all-start = ((bf16[4,2,96,768]{3,2,1,0:T(8,128)(2,1)}), bf16[4,2,96,768]{3,2,1,0:T(8,128)(2,1)S(1)}, u32[]{:S(2)}, u32[]{:S(2)}) async-start(bf16[4,2,96,768]{3,2,1,0:T(8,128)(2,1)} %broadcast_in_dim.23), calls=%async_computation | async-start | bytes 2359296 | tf_op jit(solution)/shard_map/all_to_all | solution.py:606
  41.2 0.0 reduce-scatter.2.cloned.1.call-start
  41.2 0.8 maximum_select_fusion.1.time
  42.0 0.6 pad_maximum_fusion.4.bias
  42.6 0.0 collective-permute-done.3.other
  42.6 0.8 copy-done.14
  43.4 14.8 %shard_map.271 = (bf16[2048,768]{1,0:T(8,128)(2,1)}, bf16[2048,1152]{1,0:T(8,128)(2,1)}, bf16[2048,384]{1,0:T(8,128)(2,1)}, bf16[2048,384]{1,0:T(8,128)(2,1)}, bf16[2048,768]{1,0:T(8,128)(2,1)}) custom-call(s32[1]{0:T(128)} %bitcast.core, bf16[2048,768]{1,0:T(8,128)(2,1)} %tok.5, f32[4,8,768]{2,1,0:T(8,128)} %maximum_select_fusion.1.time, ...), custom_call_target="tpu_custom_call" | custom-call | flops 14000000000 | bytes 19792896 | tf_op jit(solution)/shard_map/pallas_call | solution.py:374
  58.3 7.1 %all-to-all-done.mine = bf16[4,2,96,768]{3,2,1,0:T(8,128)(2,1)S(1)} async-done(((bf16[4,2,96,768]{3,2,1,0:T(8,128)(2,1)}), bf16[4,2,96,768]{3,2,1,0:T(8,128)(2,1)S(1)}, u32[]{:S(2)}, u32[]{:S(2)}) %all-to-all-start) | async-done | bytes 1179680 | tf_op jit(solution)/shard_map/all_to_all | solution.py:606
  65.3 0.0 collective-permute-start.4
  65.4 0.6 reshape.82.steps
  66.0 0.6 pad_add_fusion.slots.places
  66.6 0.7 reshape.81.b
  67.3 1.0 collective-permute-done.4.other
  68.3 16.0 %shard_map.272 = (bf16[2048,1152]{1,0:T(8,128)(2,1)}, bf16[2048,384]{1,0:T(8,128)(2,1)}, f32[2048,768]{1,0:T(8,128)}, bf16[2048,768]{1,0:T(8,128)(2,1)}) custom-call(s32[1]{0:T(128)} %bitcast.core, bf16[2048,768]{1,0:T(8,128)(2,1)} %tok.5, f32[4,8,768]{2,1,0:T(8,128)} %maximum_select_fusion.1.time, bf16[2048,768]{1,0:T(8,128)(2,1)} %get-tuple-element.44.n_one, ...), custom_call_target="tpu_custom_call" | custom-call | flops 15000000512 | bytes 27657216 | tf_op jit(solution)/shard_map/pallas_call | solution.py:374
  84.3 22.8 %shard_map.273 = (bf16[2048,768]{1,0:T(8,128)(2,1)}, bf16[2048,768]{1,0:T(8,128)(2,1)}, bf16[768,1536]{1,0:T(8,128)(2,1)}, f32[1,768]{1,0:T(1,128)}) custom-call(bf16[2048,768]{1,0:T(8,128)(2,1)} %get-tuple-element.47.n_two, bf16[2048,768]{1,0:T(8,128)(2,1)} %c.3, bf16[768,768]{1,0:T(8,128)(2,1)} %wi.1, bf16[768,768]{1,0:T(8,128)(2,1)} %wb.1, ...), custom_call_target="tpu_custom_call" | custom-call | flops 20999999488 | bytes 17329152 | tf_op jit(solution)/shard_map/pallas_call | solution.py:369
  107.2 3.6 %all-gather.2.cloned.1.call-done = bf16[6144,768]{1,0:T(8,128)(2,1)} async-done(((bf16[192,768]{1,0:T(8,128)(2,1)}), bf16[6144,768]{1,0:T(8,128)(2,1)}) %all-gather.2.cloned.1.call-update) | async-done | bytes 9437200 | tf_op jit(solution)/shard_map/all_gather | solution.py:448
  110.7 0.0 reduce-scatter.2.cloned.1.call-update
  110.8 62.1 %shard_map.274 = (bf16[2048,768]{1,0:T(8,128)(2,1)}, bf16[2048,768]{1,0:T(8,128)(2,1)}, bf16[2048,768]{1,0:T(8,128)(2,1)}, bf16[768,768]{1,0:T(8,128)(2,1)}, f32[8,768]{1,0:T(8,128)}) custom-call(s32[5]{0:T(128)} %pad_add_fusion.slots.places, bf16[2048,768]{1,0:T(8,128)(2,1)} %get-tuple-element.47.n_two, bf16[2048,768]{1,0:T(8,128)(2,1)} %c.3, ...), custom_call_target="tpu_custom_call" | custom-call | flops 62000001024 | bytes 71236608 | tf_op jit(solution)/shard_map/pallas_call | solution.py:374
  172.8 3.6 %all-to-all-start.2 = ((bf16[8,96,768]{2,1,0:T(8,128)(2,1)}), bf16[8,96,768]{2,1,0:T(8,128)(2,1)S(1)}, u32[]{:S(2)}, u32[]{:S(2)}) async-start(bf16[8,96,768]{2,1,0:T(8,128)(2,1)} %bitcast.38), calls=%async_computation.3 | async-start | bytes 2359296 | tf_op jit(solution)/shard_map/all_to_all | solution.py:534
  176.4 0.0 reduce-scatter.2.cloned.1.call-done.mlp_sums
  176.4 21.6 %shard_map.275 = (bf16[2048,768]{1,0:T(8,128)(2,1)}, f32[8,16,768]{2,1,0:T(8,128)}, f32[96,768]{1,0:T(8,128)}, f32[96,768]{1,0:T(8,128)}) custom-call(s32[5]{0:T(128)} %pad_add_fusion.slots.places, bf16[2048,768]{1,0:T(8,128)(2,1)} %tok.5, f32[4,8,768]{2,1,0:T(8,128)} %maximum_select_fusion.1.time, bf16[2048,768]{1,0:T(8,128)(2,1)} %get-tuple-element.58.dmid, ...), custom_call_target="tpu_custom_call" | custom-call | flops 20000000000 | bytes 22659072 | tf_op jit(solution)/shard_map/pallas_call | solution.py:374
  198.0 4.1 %all-to-all-start.3 = ((f32[8,16,768]{2,1,0:T(8,128)}), f32[8,16,768]{2,1,0:T(8,128)S(1)}, u32[]{:S(2)}, u32[]{:S(2)}) async-start(f32[8,16,768]{2,1,0:T(8,128)} %get-tuple-element.67), calls=%async_computation.4 | async-start | bytes 786432 | tf_op jit(solution)/shard_map/all_to_all | solution.py:556
  202.1 0.2 convert_reduce_fusion
  202.3 0.1 slice_bitcast_fusion.2
  202.4 0.0 copy-start.1
  202.4 0.7 copy.36
  203.2 0.1 copy.34
  203.3 0.9 copy.35
  204.2 6.3 %all-to-all-done.3 = f32[8,16,768]{2,1,0:T(8,128)S(1)} async-done(((f32[8,16,768]{2,1,0:T(8,128)}), f32[8,16,768]{2,1,0:T(8,128)S(1)}, u32[]{:S(2)}, u32[]{:S(2)}) %all-to-all-start.3) | async-done | bytes 393248 | tf_op jit(solution)/shard_map/all_to_all | solution.py:556
  210.5 0.7 slice_reduce_fusion.1
  211.2 0.1 convert_element_type.61
  211.3 0.1 copy.33
  211.4 0.1 eq.32
  211.5 0.1 reshape.84
  211.6 0.6 pad_maximum_fusion.9
  212.2 2.3 %fusion = f32[2000,192]{0,1:T(8,128)} fusion(f32[256,192]{1,0:T(8,128)S(1)} %reshape.84, s32[256]{0:T(256)S(1)} %eq.32), kind=kOutput, calls=%fused_computation.2 | convolution fusion | flops 1180160000 | bytes 1733632 | tf_op jit(solution)/shard_map/dot_general | solution.py:570
  (57 shorter events, 0.4 us)
Async XLA Ops:
  7.2 4.7 %copy-start = (bf16[2000,192]{0,1:T(8,128)(2,1)S(1)}, bf16[2000,192]{0,1:T(8,128)(2,1)}, u32[]{:S(2)}) copy-start(bf16[2000,192]{0,1:T(8,128)(2,1)} %param.18) | copy-start | bytes 2304004
  7.2 10.9 %copy-start.6 = (f32[768]{0:T(1024)S(1)}, f32[768]{0:T(1024)}, u32[]{:S(2)}) copy-start(f32[768]{0:T(1024)} %param.24) | copy-start | bytes 9220
  7.2 11.7 %copy-start.3 = (bf16[192,768]{1,0:T(8,128)(2,1)S(1)}, bf16[192,768]{1,0:T(8,128)(2,1)}, u32[]{:S(2)}) copy-start(bf16[192,768]{1,0:T(8,128)(2,1)} %param.21) | copy-start | bytes 884740
  7.2 11.7 %copy-start.2 = (bf16[768,3,192]{0,2,1:T(8,128)(2,1)S(1)}, bf16[768,3,192]{0,2,1:T(8,128)(2,1)}, u32[]{:S(2)}) copy-start(bf16[768,3,192]{0,2,1:T(8,128)(2,1)} %param.19) | copy-start | bytes 2654212
  7.2 4.6 %copy-start.13 = (s32[32]{0:T(128)S(1)}, s32[32]{0:T(128)}, u32[]{:S(2)}) copy-start(s32[32]{0:T(128)} %param.17) | copy-start | bytes 388
  7.2 10.8 %copy-start.7 = (f32[768]{0:T(1024)S(1)}, f32[768]{0:T(1024)}, u32[]{:S(2)}) copy-start(f32[768]{0:T(1024)} %param.22) | copy-start | bytes 9220
  7.3 10.9 %copy-start.8 = (f32[768]{0:T(1024)S(1)}, f32[768]{0:T(1024)}, u32[]{:S(2)}) copy-start(f32[768]{0:T(1024)} %param.26) | copy-start | bytes 9220
  7.3 10.9 %copy-start.9 = (f32[768]{0:T(1024)S(1)}, f32[768]{0:T(1024)}, u32[]{:S(2)}) copy-start(f32[768]{0:T(1024)} %param.27) | copy-start | bytes 9220
  7.3 10.9 %copy-start.10 = (f32[768]{0:T(1024)S(1)}, f32[768]{0:T(1024)}, u32[]{:S(2)}) copy-start(f32[768]{0:T(1024)} %param.28) | copy-start | bytes 9220
  7.3 10.9 %copy-start.11 = (f32[768]{0:T(1024)S(1)}, f32[768]{0:T(1024)}, u32[]{:S(2)}) copy-start(f32[768]{0:T(1024)} %param.29) | copy-start | bytes 9220
  7.3 10.9 %copy-start.12 = (f32[768]{0:T(1024)S(1)}, f32[768]{0:T(1024)}, u32[]{:S(2)}) copy-start(f32[768]{0:T(1024)} %param.30) | copy-start | bytes 9220
  7.3 103.4 %all-gather.2.cloned.1.call-start = ((), (), s32[]{:S(2)}) async-start(), calls=%async_computation.5 | async-start | bytes 9732096 | tf_op jit(solution)/shard_map/all_gather | solution.py:448
  12.4 11.4 %collective-permute-start = (bf16[128,768]{1,0:T(8,128)(2,1)S(1)}, bf16[128,768]{1,0:T(8,128)(2,1)S(1)}, u32[]{:S(2)}, u32[]{:S(2)}) collective-permute-start(bf16[128,768]{1,0:T(8,128)(2,1)S(1)} %maximum_maximum_fusion), channel_id=1, source_target_pairs={{0,1},{1,0},{2,3},{3,2},{4,5},{5,4},{6,7},{7,6},{8,9},{9,8},{10,11... | collective-permute-start | bytes 589832 | tf_op jit(solution)/shard_map/ppermute | solution.py:424
  15.5 20.2 %collective-permute-start.2 = (bf16[128,768]{1,0:T(8,128)(2,1)S(1)}, bf16[128,768]{1,0:T(8,128)(2,1)S(1)}, u32[]{:S(2)}, u32[]{:S(2)}) collective-permute-start(bf16[128,768]{1,0:T(8,128)(2,1)S(1)} %maximum_maximum_fusion), channel_id=1, source_target_pairs={{0,2},{1,3},{2,0},{3,1},{4,6},{5,7},{6,4},{7,5},{8,10},{9,11},{10,... | collective-permute-start | bytes 589832 | tf_op jit(solution)/shard_map/ppermute | solution.py:424
  18.1 17.6 %collective-permute-start.1 = (bf16[128,768]{1,0:T(8,128)(2,1)S(1)}, bf16[128,768]{1,0:T(8,128)(2,1)S(1)}, u32[]{:S(2)}, u32[]{:S(2)}) collective-permute-start(bf16[128,768]{1,0:T(8,128)(2,1)S(1)} %maximum_maximum_fusion), channel_id=1, source_target_pairs={{0,3},{1,2},{2,1},{3,0},{4,7},{5,6},{6,5},{7,4},{8,11},{9,10},{10,... | collective-permute-start | bytes 589832 | tf_op jit(solution)/shard_map/ppermute | solution.py:424
  24.7 11.6 %all-to-all-start.1 = ((bf16[4,1,96,768]{3,2,1,0:T(8,128)(2,1)}), bf16[4,1,96,768]{3,2,1,0:T(8,128)(2,1)S(1)}, u32[]{:S(2)}, u32[]{:S(2)}) async-start(bf16[4,1,96,768]{3,2,1,0:T(8,128)(2,1)} %broadcast_in_dim.24), calls=%async_computation.1 | async-start | bytes 1179648 | tf_op jit(solution)/shard_map/all_to_all | solution.py:606
  36.3 1.4 copy-start.5
  36.3 6.3 %collective-permute-start.3 = (bf16[4,1,96,768]{3,2,1,0:T(8,128)(2,1)S(1)}, bf16[4,1,96,768]{3,2,1,0:T(8,128)(2,1)S(1)}, u32[]{:S(2)}, u32[]{:S(2)}) collective-permute-start(bf16[4,1,96,768]{3,2,1,0:T(8,128)(2,1)S(1)} %all-to-all-done.1.mine), channel_id=1, source_target_pairs={{0,4},{4,0},{8,12},{12,8},{16,20},{20,16},{24,28},{28,24},{1,5},{5... | collective-permute-start | bytes 1769480 | tf_op jit(solution)/shard_map/ppermute | solution.py:427
  37.6 27.7 %all-to-all-start = ((bf16[4,2,96,768]{3,2,1,0:T(8,128)(2,1)}), bf16[4,2,96,768]{3,2,1,0:T(8,128)(2,1)S(1)}, u32[]{:S(2)}, u32[]{:S(2)}) async-start(bf16[4,2,96,768]{3,2,1,0:T(8,128)(2,1)} %broadcast_in_dim.23), calls=%async_computation | async-start | bytes 2359296 | tf_op jit(solution)/shard_map/all_to_all | solution.py:606
  41.2 135.3 %reduce-scatter.2.cloned.1.call-start = ((), (), s32[]{:S(2)}) async-start(), calls=%async_computation.6 | async-start | bytes 2654208 | tf_op jit(solution)/shard_map/reduce_scatter | solution.py:510
  42.6 0.8 copy-start.14
  65.3 3.0 %copy-start.4 = (bf16[4,2,96,768]{3,2,1,0:T(8,128)(2,1)}, bf16[4,2,96,768]{3,2,1,0:T(8,128)(2,1)S(1)}, u32[]{:S(2)}) copy-start(bf16[4,2,96,768]{3,2,1,0:T(8,128)(2,1)S(1)} %all-to-all-done.mine) | copy-start | bytes 3538948
  65.3 3.0 %collective-permute-start.4 = (bf16[4,2,96,768]{3,2,1,0:T(8,128)(2,1)S(1)}, bf16[4,2,96,768]{3,2,1,0:T(8,128)(2,1)}, u32[]{:S(2)}, u32[]{:S(2)}) collective-permute-start(bf16[4,2,96,768]{3,2,1,0:T(8,128)(2,1)S(1)} %all-to-all-done.mine), channel_id=1, source_target_pairs={{0,4},{4,0},{8,12},{12,8},{16,20},{20,16},{24,28},{28,24},{1,5},{5... | collective-permute-start | bytes 3538952 | tf_op jit(solution)/shard_map/ppermute | solution.py:488
  172.8 25.2 %all-to-all-start.2 = ((bf16[8,96,768]{2,1,0:T(8,128)(2,1)}), bf16[8,96,768]{2,1,0:T(8,128)(2,1)S(1)}, u32[]{:S(2)}, u32[]{:S(2)}) async-start(bf16[8,96,768]{2,1,0:T(8,128)(2,1)} %bitcast.38), calls=%async_computation.3 | async-start | bytes 2359296 | tf_op jit(solution)/shard_map/all_to_all | solution.py:534
  198.0 12.4 %all-to-all-start.3 = ((f32[8,16,768]{2,1,0:T(8,128)}), f32[8,16,768]{2,1,0:T(8,128)S(1)}, u32[]{:S(2)}, u32[]{:S(2)}) async-start(f32[8,16,768]{2,1,0:T(8,128)} %get-tuple-element.67), calls=%async_computation.4 | async-start | bytes 786432 | tf_op jit(solution)/shard_map/all_to_all | solution.py:556
  202.4 12.1 %copy-start.1 = (bf16[2000,192]{0,1:T(8,128)(2,1)S(1)}, bf16[2000,192]{0,1:T(8,128)(2,1)}, u32[]{:S(2)}) copy-start(bf16[2000,192]{0,1:T(8,128)(2,1)} %param.18) | copy-start | bytes 2304004
Sparse Core Ops, SparseCore 0:
  11.6 99.0 all-gather.1
  114.1 41.0 reduce-scatter.1

commit v6 on v5

--- a/solution.py
+++ b/solution.py
@@ -288,11 +288,11 @@
     out = out_in[...].astype(F32)
     dn2 = dn2_in[...].astype(F32)
     for k, w in enumerate((w1, w2, w3)):
-        act, d_pre = mlp_slot(
-            n_two[...], c[...], w[0, :dim, :], w[0, dim:, :], b[k : k + 1, :]
-        )
-        out = out + dot_nn(act, w[0, dim:, :])
-        dn2 = dn2 + dot_nt(d_pre, w[0, :dim, :])
+        wi = w[:4, 0].reshape(-1, dim)
+        wb = w[4:, 0].reshape(-1, dim)
+        act, d_pre = mlp_slot(n_two[...], c[...], wi, wb, b[k : k + 1, :])
+        out = out + dot_nn(act, wb)
+        dn2 = dn2 + dot_nt(d_pre, wi)
     mid = middle[...]
     cot = c[...].astype(F32)
     out_ref[...] = (mid + out + vecs[5:6, :]).astype(BF16)
@@ -445,8 +445,11 @@
         mlp_piece = lax.dynamic_slice_in_dim(
             jnp.concatenate([w_in, w_back]), part * n_mlp, n_mlp, 0
         )
-    mlp_all = lax.all_gather(mlp_piece, ("tensor", "dp"), axis=0, tiled=True)
-    mlp_all = mlp_all.reshape(n_tensor, dim + hid, dim)
+    mlp_all = lax.all_gather(mlp_piece, ("dp", "tensor"), axis=0, tiled=True)
+    mlp_all = mlp_all.reshape(dp, n_tensor, n_mlp, dim)
+    if not fast:
+        mlp_all = jnp.transpose(mlp_all, (0, 2, 1, 3)).reshape(8, -1, n_tensor, dim)
+        mlp_all = jnp.transpose(mlp_all, (0, 2, 1, 3))
 
     time_rows = jnp.concatenate([time_slots[k] for k in range(n_tensor)], axis=1)
     for bit in range(n_tensor.bit_length() - 1):
@@ -511,7 +514,10 @@
 
     mlp_grads, mlp_all = lax.optimization_barrier((mlp_grads, mlp_all))
     mlp_grads = scattered(mlp_grads)
-    mlp_spec = lambda k: slot_spec((dim + hid, dim), k)
+    mlp_spec = lambda k: pl.BlockSpec(
+        (8, 1, (dim + hid) // 8, dim), lambda i, s: (0, s[k], 0, 0),
+        pipeline_mode=pl.Buffered(1),
+    )
     places = jnp.concatenate([me ^ jnp.arange(n_tensor, dtype=jnp.int32), core])
     spread_steps = jnp.pad(timesteps.astype(F32), (256, dim - 256 - sentences)).reshape(1, dim)
     output, d_mid, dn1_acc, att_grads, more = call(

time: 222 us -> 221 us (level)
  no operation moved by 1% of the time
where the time goes in v6:
time: 221 us; the launch traced here: 220 us
  Pallas kernels  136 us (62%)
  waiting for transfers between devices  29.2 us (13%)
  starting transfers between devices  20.9 us (9%)
  between operations  14.6 us (7%)
  local copies, waits for them, and re-layouts  8.84 us (4%)
  other arithmetic  7.9 us (4%)
  matrix products  2.62 us (1%)
    pallas_call x4, Pallas kernels, call(): pl.pallas_call(kernel, grid_spec=pltpu.PrefetchScalarGridSpec(num_scalar_...  113 us
    pallas_call x1, Pallas kernels, call(): pl.pallas_call(kernel, grid=grid, in_specs=in_specs, out_specs=out_specs,...  22.8 us
    ppermute x3, waiting for transfers between devices, body(): got = [lax.ppermute(message, 'tensor', flipped(4, k)) for k in (1, 2, 3)]  10.8 us
    all_to_all x2, waiting for transfers between devices, spread_plane(): lax.all_to_all(whole, 'dp', 0, 0, tiled=True, axis_index_groups=[[0, 2, 4...  7.47 us
    all_to_all x2, starting transfers between devices, spread_plane(): lax.all_to_all(whole, 'dp', 0, 0, tiled=True, axis_index_groups=[[0, 2, 4...  7.42 us
    all_to_all x1, waiting for transfers between devices, body(): terms = lax.all_to_all(terms, 'dp', 0, 0, tiled=True)  6.28 us
    ppermute x3, starting transfers between devices, body(): got = [lax.ppermute(message, 'tensor', flipped(4, k)) for k in (1, 2, 3)]  5.68 us
  transfers between devices with their start and end apart: 11, of which 7 were waited for; matrix products, arithmetic and copies ran while one was open for 6% of the time, Pallas kernels for 62%

profile of v6, /device:TPU:0, one launch (start us, length us, event | category | flops | bytes accessed | tf_op | source)
XLA Modules:
  0.0 220.1 jit_solution(7745189395014163744)
XLA Ops:
  7.2 0.0 copy-start
  7.2 0.0 copy-start.6
  7.2 0.0 copy-start.3
  7.2 0.0 copy-start.2
  7.3 0.0 all-gather.2.cloned.1.call-start
  7.4 2.0 dynamic-slice_select_fusion
  9.4 0.0 all-gather.2.cloned.1.call-update
  9.4 0.8 reshape.79
  10.2 0.7 fusion.15
  10.9 1.0 fusion.3
  11.9 0.4 fusion.22
  12.3 0.1 maximum_maximum_fusion
  12.4 3.1 %collective-permute-start = (bf16[128,768]{1,0:T(8,128)(2,1)S(1)}, bf16[128,768]{1,0:T(8,128)(2,1)S(1)}, u32[]{:S(2)}, u32[]{:S(2)}) collective-permute-start(bf16[128,768]{1,0:T(8,128)(2,1)S(1)} %maximum_maximum_fusion), channel_id=1, source_target_pairs={{0,1},{1,0},{2,3},{3,2},{4,5},{5,4},{6,7},{7,6},{8,9},{9,8},{10,11... | collective-permute-start | bytes 589832 | tf_op jit(solution)/shard_map/ppermute | solution.py:424
  15.5 2.6 %collective-permute-start.2 = (bf16[128,768]{1,0:T(8,128)(2,1)S(1)}, bf16[128,768]{1,0:T(8,128)(2,1)S(1)}, u32[]{:S(2)}, u32[]{:S(2)}) collective-permute-start(bf16[128,768]{1,0:T(8,128)(2,1)S(1)} %maximum_maximum_fusion), channel_id=1, source_target_pairs={{0,2},{1,3},{2,0},{3,1},{4,6},{5,7},{6,4},{7,5},{8,10},{9,11},{10,... | collective-permute-start | bytes 589832 | tf_op jit(solution)/shard_map/ppermute | solution.py:424
  18.1 0.0 collective-permute-start.1
  18.3 0.6 stack.63.vecs
  18.9 1.1 pad_maximum_fusion.own
  20.1 3.7 %collective-permute-done = bf16[128,768]{1,0:T(8,128)(2,1)S(1)} collective-permute-done((bf16[128,768]{1,0:T(8,128)(2,1)S(1)}, bf16[128,768]{1,0:T(8,128)(2,1)S(1)}, u32[]{:S(2)}, u32[]{:S(2)}) %collective-permute-start) | collective-permute-done | bytes 196640 | tf_op jit(solution)/shard_map/ppermute | solution.py:424
  23.8 0.9 broadcast_in_dim.24
  24.7 3.9 %all-to-all-start.1 = ((bf16[4,1,96,768]{3,2,1,0:T(8,128)(2,1)}), bf16[4,1,96,768]{3,2,1,0:T(8,128)(2,1)S(1)}, u32[]{:S(2)}, u32[]{:S(2)}) async-start(bf16[4,1,96,768]{3,2,1,0:T(8,128)(2,1)} %broadcast_in_dim.24), calls=%async_computation.1 | async-start | bytes 1179648 | tf_op jit(solution)/shard_map/all_to_all | solution.py:612
  28.6 7.0 %collective-permute-done.2 = bf16[128,768]{1,0:T(8,128)(2,1)S(1)} collective-permute-done((bf16[128,768]{1,0:T(8,128)(2,1)S(1)}, bf16[128,768]{1,0:T(8,128)(2,1)S(1)}, u32[]{:S(2)}, u32[]{:S(2)}) %collective-permute-start.2) | collective-permute-done | bytes 196640 | tf_op jit(solution)/shard_map/ppermute | solution.py:424
  35.6 0.0 collective-permute-done.1
  35.7 0.1 maximum_select_fusion
  35.9 0.4 all-to-all-done.1.mine
  36.3 0.0 collective-permute-start.3
  36.3 0.1 reshape_squeeze.6
  36.4 0.1 reshape_squeeze.7
  36.5 1.1 broadcast_in_dim.23
  37.6 3.5 %all-to-all-start = ((bf16[4,2,96,768]{3,2,1,0:T(8,128)(2,1)}), bf16[4,2,96,768]{3,2,1,0:T(8,128)(2,1)S(1)}, u32[]{:S(2)}, u32[]{:S(2)}) async-start(bf16[4,2,96,768]{3,2,1,0:T(8,128)(2,1)} %broadcast_in_dim.23), calls=%async_computation | async-start | bytes 2359296 | tf_op jit(solution)/shard_map/all_to_all | solution.py:612
  41.2 0.0 reduce-scatter.2.cloned.1.call-start
  41.2 0.8 maximum_select_fusion.1.time
  42.0 0.6 pad_maximum_fusion.4.bias
  42.6 0.0 collective-permute-done.3.other
  42.6 0.8 copy-done.14
  43.4 14.8 %shard_map.271 = (bf16[2048,768]{1,0:T(8,128)(2,1)}, bf16[2048,1152]{1,0:T(8,128)(2,1)}, bf16[2048,384]{1,0:T(8,128)(2,1)}, bf16[2048,384]{1,0:T(8,128)(2,1)}, bf16[2048,768]{1,0:T(8,128)(2,1)}) custom-call(s32[1]{0:T(128)} %bitcast.core, bf16[2048,768]{1,0:T(8,128)(2,1)} %tok.5, f32[4,8,768]{2,1,0:T(8,128)} %maximum_select_fusion.1.time, ...), custom_call_target="tpu_custom_call" | custom-call | flops 14000000000 | bytes 19792896 | tf_op jit(solution)/shard_map/pallas_call | solution.py:374
  58.3 7.1 %all-to-all-done.mine = bf16[4,2,96,768]{3,2,1,0:T(8,128)(2,1)S(1)} async-done(((bf16[4,2,96,768]{3,2,1,0:T(8,128)(2,1)}), bf16[4,2,96,768]{3,2,1,0:T(8,128)(2,1)S(1)}, u32[]{:S(2)}, u32[]{:S(2)}) %all-to-all-start) | async-done | bytes 1179680 | tf_op jit(solution)/shard_map/all_to_all | solution.py:612
  65.4 0.6 reshape.82.steps
  66.0 0.6 pad_add_fusion.slots.places
  66.6 0.7 reshape.81.b
  67.3 1.0 collective-permute-done.4.other
  68.3 16.0 %shard_map.272 = (bf16[2048,1152]{1,0:T(8,128)(2,1)}, bf16[2048,384]{1,0:T(8,128)(2,1)}, f32[2048,768]{1,0:T(8,128)}, bf16[2048,768]{1,0:T(8,128)(2,1)}) custom-call(s32[1]{0:T(128)} %bitcast.core, bf16[2048,768]{1,0:T(8,128)(2,1)} %tok.5, f32[4,8,768]{2,1,0:T(8,128)} %maximum_select_fusion.1.time, bf16[2048,768]{1,0:T(8,128)(2,1)} %get-tuple-element.44.n_one, ...), custom_call_target="tpu_custom_call" | custom-call | flops 15000000512 | bytes 27657216 | tf_op jit(solution)/shard_map/pallas_call | solution.py:374
  84.3 22.8 %shard_map.273 = (bf16[2048,768]{1,0:T(8,128)(2,1)}, bf16[2048,768]{1,0:T(8,128)(2,1)}, bf16[768,1536]{1,0:T(8,128)(2,1)}, f32[1,768]{1,0:T(1,128)}) custom-call(bf16[2048,768]{1,0:T(8,128)(2,1)} %get-tuple-element.47.n_two, bf16[2048,768]{1,0:T(8,128)(2,1)} %c.3, bf16[768,768]{1,0:T(8,128)(2,1)} %wi.1, bf16[768,768]{1,0:T(8,128)(2,1)} %wb.1, ...), custom_call_target="tpu_custom_call" | custom-call | flops 20999999488 | bytes 17329152 | tf_op jit(solution)/shard_map/pallas_call | solution.py:369
  107.2 3.5 %all-gather.2.cloned.1.call-done = bf16[6144,768]{1,0:T(8,128)(2,1)} async-done(((bf16[192,768]{1,0:T(8,128)(2,1)}), bf16[6144,768]{1,0:T(8,128)(2,1)}) %all-gather.2.cloned.1.call-update) | async-done | bytes 9437200 | tf_op jit(solution)/shard_map/all_gather | solution.py:448
  110.7 0.0 reduce-scatter.2.cloned.1.call-update
  110.7 60.9 %shard_map.274 = (bf16[2048,768]{1,0:T(8,128)(2,1)}, bf16[2048,768]{1,0:T(8,128)(2,1)}, bf16[2048,768]{1,0:T(8,128)(2,1)}, bf16[768,768]{1,0:T(8,128)(2,1)}, f32[8,768]{1,0:T(8,128)}) custom-call(s32[5]{0:T(128)} %pad_add_fusion.slots.places, bf16[2048,768]{1,0:T(8,128)(2,1)} %get-tuple-element.47.n_two, bf16[2048,768]{1,0:T(8,128)(2,1)} %c.3, ...), custom_call_target="tpu_custom_call" | custom-call | flops 62000001024 | bytes 71236608 | tf_op jit(solution)/shard_map/pallas_call | solution.py:374
  171.7 3.6 %all-to-all-start.2 = ((bf16[8,96,768]{2,1,0:T(8,128)(2,1)}), bf16[8,96,768]{2,1,0:T(8,128)(2,1)S(1)}, u32[]{:S(2)}, u32[]{:S(2)}) async-start(bf16[8,96,768]{2,1,0:T(8,128)(2,1)} %bitcast.38), calls=%async_computation.3 | async-start | bytes 2359296 | tf_op jit(solution)/shard_map/all_to_all | solution.py:540
  175.2 0.0 reduce-scatter.2.cloned.1.call-done.mlp_sums
  175.3 21.6 %shard_map.275 = (bf16[2048,768]{1,0:T(8,128)(2,1)}, f32[8,16,768]{2,1,0:T(8,128)}, f32[96,768]{1,0:T(8,128)}, f32[96,768]{1,0:T(8,128)}) custom-call(s32[5]{0:T(128)} %pad_add_fusion.slots.places, bf16[2048,768]{1,0:T(8,128)(2,1)} %tok.5, f32[4,8,768]{2,1,0:T(8,128)} %maximum_select_fusion.1.time, bf16[2048,768]{1,0:T(8,128)(2,1)} %get-tuple-element.58.dmid, ...), custom_call_target="tpu_custom_call" | custom-call | flops 20000000000 | bytes 22659072 | tf_op jit(solution)/shard_map/pallas_call | solution.py:374
  196.8 0.0 all-to-all-done.2
  196.8 4.1 %all-to-all-start.3 = ((f32[8,16,768]{2,1,0:T(8,128)}), f32[8,16,768]{2,1,0:T(8,128)S(1)}, u32[]{:S(2)}, u32[]{:S(2)}) async-start(f32[8,16,768]{2,1,0:T(8,128)} %get-tuple-element.67), calls=%async_computation.4 | async-start | bytes 786432 | tf_op jit(solution)/shard_map/all_to_all | solution.py:562
  201.0 0.2 convert_reduce_fusion
  201.1 0.1 slice_bitcast_fusion.2
  201.2 0.0 copy-start.1
  201.2 0.7 copy.36
  202.0 0.1 copy.34
  202.1 0.9 copy.35
  203.0 6.3 %all-to-all-done.3 = f32[8,16,768]{2,1,0:T(8,128)S(1)} async-done(((f32[8,16,768]{2,1,0:T(8,128)}), f32[8,16,768]{2,1,0:T(8,128)S(1)}, u32[]{:S(2)}, u32[]{:S(2)}) %all-to-all-start.3) | async-done | bytes 393248 | tf_op jit(solution)/shard_map/all_to_all | solution.py:562
  209.3 0.7 slice_reduce_fusion.1
  210.0 0.1 convert_element_type.61
  210.1 0.1 copy.33
  210.2 0.1 eq.32
  210.3 0.1 reshape.84
  210.5 0.6 pad_maximum_fusion.9
  211.0 2.3 %fusion = f32[2000,192]{0,1:T(8,128)} fusion(f32[256,192]{1,0:T(8,128)S(1)} %reshape.84, s32[256]{0:T(256)S(1)} %eq.32), kind=kOutput, calls=%fused_computation.2 | convolution fusion | flops 1180160000 | bytes 1733632 | tf_op jit(solution)/shard_map/dot_general | solution.py:576
  (57 shorter events, 0.4 us)
Async XLA Ops:
  7.2 4.7 %copy-start = (bf16[2000,192]{0,1:T(8,128)(2,1)S(1)}, bf16[2000,192]{0,1:T(8,128)(2,1)}, u32[]{:S(2)}) copy-start(bf16[2000,192]{0,1:T(8,128)(2,1)} %param.18) | copy-start | bytes 2304004
  7.2 10.9 %copy-start.6 = (f32[768]{0:T(1024)S(1)}, f32[768]{0:T(1024)}, u32[]{:S(2)}) copy-start(f32[768]{0:T(1024)} %param.24) | copy-start | bytes 9220
  7.2 11.7 %copy-start.3 = (bf16[192,768]{1,0:T(8,128)(2,1)S(1)}, bf16[192,768]{1,0:T(8,128)(2,1)}, u32[]{:S(2)}) copy-start(bf16[192,768]{1,0:T(8,128)(2,1)} %param.21) | copy-start | bytes 884740
  7.2 11.7 %copy-start.2 = (bf16[768,3,192]{0,2,1:T(8,128)(2,1)S(1)}, bf16[768,3,192]{0,2,1:T(8,128)(2,1)}, u32[]{:S(2)}) copy-start(bf16[768,3,192]{0,2,1:T(8,128)(2,1)} %param.19) | copy-start | bytes 2654212
  7.2 4.6 %copy-start.13 = (s32[32]{0:T(128)S(1)}, s32[32]{0:T(128)}, u32[]{:S(2)}) copy-start(s32[32]{0:T(128)} %param.17) | copy-start | bytes 388
  7.2 10.8 %copy-start.7 = (f32[768]{0:T(1024)S(1)}, f32[768]{0:T(1024)}, u32[]{:S(2)}) copy-start(f32[768]{0:T(1024)} %param.22) | copy-start | bytes 9220
  7.3 10.9 %copy-start.8 = (f32[768]{0:T(1024)S(1)}, f32[768]{0:T(1024)}, u32[]{:S(2)}) copy-start(f32[768]{0:T(1024)} %param.26) | copy-start | bytes 9220
  7.3 10.9 %copy-start.9 = (f32[768]{0:T(1024)S(1)}, f32[768]{0:T(1024)}, u32[]{:S(2)}) copy-start(f32[768]{0:T(1024)} %param.27) | copy-start | bytes 9220
  7.3 10.9 %copy-start.10 = (f32[768]{0:T(1024)S(1)}, f32[768]{0:T(1024)}, u32[]{:S(2)}) copy-start(f32[768]{0:T(1024)} %param.28) | copy-start | bytes 9220
  7.3 10.9 %copy-start.11 = (f32[768]{0:T(1024)S(1)}, f32[768]{0:T(1024)}, u32[]{:S(2)}) copy-start(f32[768]{0:T(1024)} %param.29) | copy-start | bytes 9220
  7.3 10.9 %copy-start.12 = (f32[768]{0:T(1024)S(1)}, f32[768]{0:T(1024)}, u32[]{:S(2)}) copy-start(f32[768]{0:T(1024)} %param.30) | copy-start | bytes 9220
  7.3 103.4 %all-gather.2.cloned.1.call-start = ((), (), s32[]{:S(2)}) async-start(), calls=%async_computation.5 | async-start | bytes 9732096 | tf_op jit(solution)/shard_map/all_gather | solution.py:448
  12.4 11.4 %collective-permute-start = (bf16[128,768]{1,0:T(8,128)(2,1)S(1)}, bf16[128,768]{1,0:T(8,128)(2,1)S(1)}, u32[]{:S(2)}, u32[]{:S(2)}) collective-permute-start(bf16[128,768]{1,0:T(8,128)(2,1)S(1)} %maximum_maximum_fusion), channel_id=1, source_target_pairs={{0,1},{1,0},{2,3},{3,2},{4,5},{5,4},{6,7},{7,6},{8,9},{9,8},{10,11... | collective-permute-start | bytes 589832 | tf_op jit(solution)/shard_map/ppermute | solution.py:424
  15.5 20.2 %collective-permute-start.2 = (bf16[128,768]{1,0:T(8,128)(2,1)S(1)}, bf16[128,768]{1,0:T(8,128)(2,1)S(1)}, u32[]{:S(2)}, u32[]{:S(2)}) collective-permute-start(bf16[128,768]{1,0:T(8,128)(2,1)S(1)} %maximum_maximum_fusion), channel_id=1, source_target_pairs={{0,2},{1,3},{2,0},{3,1},{4,6},{5,7},{6,4},{7,5},{8,10},{9,11},{10,... | collective-permute-start | bytes 589832 | tf_op jit(solution)/shard_map/ppermute | solution.py:424
  18.1 17.6 %collective-permute-start.1 = (bf16[128,768]{1,0:T(8,128)(2,1)S(1)}, bf16[128,768]{1,0:T(8,128)(2,1)S(1)}, u32[]{:S(2)}, u32[]{:S(2)}) collective-permute-start(bf16[128,768]{1,0:T(8,128)(2,1)S(1)} %maximum_maximum_fusion), channel_id=1, source_target_pairs={{0,3},{1,2},{2,1},{3,0},{4,7},{5,6},{6,5},{7,4},{8,11},{9,10},{10,... | collective-permute-start | bytes 589832 | tf_op jit(solution)/shard_map/ppermute | solution.py:424
  24.7 11.6 %all-to-all-start.1 = ((bf16[4,1,96,768]{3,2,1,0:T(8,128)(2,1)}), bf16[4,1,96,768]{3,2,1,0:T(8,128)(2,1)S(1)}, u32[]{:S(2)}, u32[]{:S(2)}) async-start(bf16[4,1,96,768]{3,2,1,0:T(8,128)(2,1)} %broadcast_in_dim.24), calls=%async_computation.1 | async-start | bytes 1179648 | tf_op jit(solution)/shard_map/all_to_all | solution.py:612
  36.3 1.4 copy-start.5
  36.3 6.3 %collective-permute-start.3 = (bf16[4,1,96,768]{3,2,1,0:T(8,128)(2,1)S(1)}, bf16[4,1,96,768]{3,2,1,0:T(8,128)(2,1)S(1)}, u32[]{:S(2)}, u32[]{:S(2)}) collective-permute-start(bf16[4,1,96,768]{3,2,1,0:T(8,128)(2,1)S(1)} %all-to-all-done.1.mine), channel_id=1, source_target_pairs={{0,4},{4,0},{8,12},{12,8},{16,20},{20,16},{24,28},{28,24},{1,5},{5... | collective-permute-start | bytes 1769480 | tf_op jit(solution)/shard_map/ppermute | solution.py:427
  37.6 27.7 %all-to-all-start = ((bf16[4,2,96,768]{3,2,1,0:T(8,128)(2,1)}), bf16[4,2,96,768]{3,2,1,0:T(8,128)(2,1)S(1)}, u32[]{:S(2)}, u32[]{:S(2)}) async-start(bf16[4,2,96,768]{3,2,1,0:T(8,128)(2,1)} %broadcast_in_dim.23), calls=%async_computation | async-start | bytes 2359296 | tf_op jit(solution)/shard_map/all_to_all | solution.py:612
  41.2 134.1 %reduce-scatter.2.cloned.1.call-start = ((), (), s32[]{:S(2)}) async-start(), calls=%async_computation.6 | async-start | bytes 2654208 | tf_op jit(solution)/shard_map/reduce_scatter | solution.py:513
  42.6 0.8 copy-start.14
  65.3 3.0 %copy-start.4 = (bf16[4,2,96,768]{3,2,1,0:T(8,128)(2,1)}, bf16[4,2,96,768]{3,2,1,0:T(8,128)(2,1)S(1)}, u32[]{:S(2)}) copy-start(bf16[4,2,96,768]{3,2,1,0:T(8,128)(2,1)S(1)} %all-to-all-done.mine) | copy-start | bytes 3538948
  65.3 3.0 %collective-permute-start.4 = (bf16[4,2,96,768]{3,2,1,0:T(8,128)(2,1)S(1)}, bf16[4,2,96,768]{3,2,1,0:T(8,128)(2,1)}, u32[]{:S(2)}, u32[]{:S(2)}) collective-permute-start(bf16[4,2,96,768]{3,2,1,0:T(8,128)(2,1)S(1)} %all-to-all-done.mine), channel_id=1, source_target_pairs={{0,4},{4,0},{8,12},{12,8},{16,20},{20,16},{24,28},{28,24},{1,5},{5... | collective-permute-start | bytes 3538952 | tf_op jit(solution)/shard_map/ppermute | solution.py:491
  171.7 25.2 %all-to-all-start.2 = ((bf16[8,96,768]{2,1,0:T(8,128)(2,1)}), bf16[8,96,768]{2,1,0:T(8,128)(2,1)S(1)}, u32[]{:S(2)}, u32[]{:S(2)}) async-start(bf16[8,96,768]{2,1,0:T(8,128)(2,1)} %bitcast.38), calls=%async_computation.3 | async-start | bytes 2359296 | tf_op jit(solution)/shard_map/all_to_all | solution.py:540
  196.8 12.4 %all-to-all-start.3 = ((f32[8,16,768]{2,1,0:T(8,128)}), f32[8,16,768]{2,1,0:T(8,128)S(1)}, u32[]{:S(2)}, u32[]{:S(2)}) async-start(f32[8,16,768]{2,1,0:T(8,128)} %get-tuple-element.67), calls=%async_computation.4 | async-start | bytes 786432 | tf_op jit(solution)/shard_map/all_to_all | solution.py:562
  201.2 12.1 %copy-start.1 = (bf16[2000,192]{0,1:T(8,128)(2,1)S(1)}, bf16[2000,192]{0,1:T(8,128)(2,1)}, u32[]{:S(2)}) copy-start(bf16[2000,192]{0,1:T(8,128)(2,1)} %param.18) | copy-start | bytes 2304004
Sparse Core Ops, SparseCore 0:
  11.5 99.1 all-gather.1
  114.0 41.0 reduce-scatter.1
